TPU v7x, 512 devices: a whole 4x4x16 slice. The times are simulated.
512 devices in a mesh: feat: 32 (over z, core), node: 16 (over x, y).
Axes of the slice: x: 4, y: 4, z: 16, core: 2. Of those that a mesh axis runs over, the one named last changes fastest.
Arguments:
- features: bfloat16 [16384, 1024], P('node', 'feat'), may hold values from -6 to 6
- target_feats: bfloat16 [16384, 1024], P('node', 'feat'), may hold values from -6 to 6
- tile_values: bfloat16 [512, 128, 128], P('node'), may hold values from 0 to 0.088378906
- tile_index: int32 [512, 2], P('node'), may hold values from 0 to 127, as said below
- tile_count: int32 [16], P('node'), may hold values from 8 to 32, as said below
- self_weight1: bfloat16 [1024, 256], P('feat'), may hold values from -0.1875 to 0.1875
- neigh_weight1: bfloat16 [1024, 256], P('feat'), may hold values from -0.1875 to 0.1875
- self_weight2: bfloat16 [256, 256], replicated, may hold values from -0.375 to 0.375
- neigh_weight2: bfloat16 [256, 256], replicated, may hold values from -0.375 to 0.375
- neighbors: int32 [4096, 10], P('node'), may hold values from 0 to 1023
- seed_index: int32 [4096], P('node'), may hold values from 0 to 1023, as said below
- cotangent: bfloat16 [4096, 256], P('node'), may hold values from -6 to 6
Outputs:
- output: bfloat16 [4096, 256], P('node')
- grad_w1: float32 [2, 1024, 256], P(None, 'feat')
- grad_w2: float32 [2, 256, 256], P(None, 'feat')
Inputs may be any that keep to these rules, and one draw needn't show every extreme that they name: `tile_index`: column 0 names a block of 128 layer-one targets among all 16384; column 1 a block of 128 sources among the 1024 stored on the slot's own node index. A node index uses the first tile_count slots of its 32; some node index uses all of them. `seed_index`: the seeds of one node index are distinct targets of it.
All inputs are finite; a program needn't handle non-finite values.
Results may differ from a plain program's by a relative error of at most 0.0058.
Values may be sent and summed in bfloat16 or wider, within the bound.
No kernel may reach another device: no remote copies, remote signals or barrier semaphores. Data moves between devices by JAX's collectives and lax.ppermute only.
A program may use at most 64 MiB of HBM per device.

v0:
```python
import jax
import jax.numpy as jnp
from jax import lax
from jax.sharding import PartitionSpec as P

TILE_GRP = 8


def silu_slope(values):
    sigmoid = jax.nn.sigmoid(values)
    return sigmoid * (1.0 + values * (1.0 - sigmoid))


def per_device(
    features,
    target_feats,
    tile_values,
    tile_index,
    tile_count,
    self_weight1,
    neigh_weight1,
    self_weight2,
    neigh_weight2,
    neighbors,
    seed_index,
    cotangent,
):
    src_rows, columns = features.shape
    tgt_rows = target_feats.shape[0]
    block = tile_values.shape[1]
    hsize = self_weight2.shape[0]
    owners = lax.axis_size("node")
    all_rows = tgt_rows * owners
    src_blocks = features.reshape(src_rows // block, block, columns)
    group_size = TILE_GRP
    live_tiles = tile_count[0]
    rounds = (live_tiles + group_size - 1) // group_size

    def add_group(position, running):
        first_slot = position * group_size
        tile_block = lax.dynamic_slice_in_dim(tile_values, first_slot, group_size, 0)
        tile_pairs = lax.dynamic_slice_in_dim(tile_index, first_slot, group_size, 0)
        sources = src_blocks[tile_pairs[:, 1]]
        products = jnp.einsum(
            "gij,gjc->gic", tile_block, sources, preferred_element_type=jnp.float32
        )
        in_use = first_slot + jnp.arange(group_size, dtype=jnp.int32) < live_tiles
        products = products * in_use[:, None, None].astype(jnp.float32)
        return running.at[tile_pairs[:, 0]].add(products)

    start_sum = jnp.zeros((all_rows // block, block, columns), jnp.float32)
    aggregate = lax.fori_loop(0, rounds, add_group, start_sum).reshape(all_rows, columns)
    agg_own = lax.psum_scatter(aggregate, "node", scatter_dimension=0, tiled=True)
    agg_half = agg_own.astype(jnp.bfloat16)
    partial_pre = jnp.dot(target_feats, self_weight1, preferred_element_type=jnp.float32) + jnp.dot(
        agg_half, neigh_weight1, preferred_element_type=jnp.float32
    )
    feat_count = lax.axis_size("feat")
    feat_index = lax.axis_index("feat")
    pre_one = lax.psum(partial_pre, "feat")
    hidden = jax.nn.silu(pre_one).astype(jnp.bfloat16)
    seed_count, fanout = neighbors.shape
    own = hidden[seed_index]
    nbr_mean = (jnp.sum(hidden[neighbors], axis=1, dtype=jnp.float32) / fanout).astype(jnp.bfloat16)
    pre_two = jnp.dot(own, self_weight2, preferred_element_type=jnp.float32) + jnp.dot(
        nbr_mean, neigh_weight2, preferred_element_type=jnp.float32
    )
    output = jax.nn.silu(pre_two).astype(jnp.bfloat16)
    slope_two = (cotangent.astype(jnp.float32) * silu_slope(pre_two)).astype(jnp.bfloat16)
    part_rows = hsize // feat_count
    own_cols = lax.dynamic_slice_in_dim(own, feat_index * part_rows, part_rows, 1)
    mean_cols = lax.dynamic_slice_in_dim(nbr_mean, feat_index * part_rows, part_rows, 1)
    grad_self2 = jnp.dot(own_cols.T, slope_two, preferred_element_type=jnp.float32)
    grad_neigh2 = jnp.dot(mean_cols.T, slope_two, preferred_element_type=jnp.float32)
    back_mean = jnp.dot(slope_two, neigh_weight2.T, preferred_element_type=jnp.float32) / fanout
    back_self = jnp.dot(slope_two, self_weight2.T, preferred_element_type=jnp.float32)
    spread = jnp.broadcast_to(back_mean[:, None, :], (seed_count, fanout, hsize)).reshape(
        seed_count * fanout, hsize
    )
    back_hidden = (
        jnp.zeros((tgt_rows, hsize), jnp.float32)
        .at[neighbors.reshape(-1)]
        .add(spread)
        .at[seed_index]
        .add(back_self)
    )
    slope_one = (back_hidden * silu_slope(pre_one)).astype(jnp.bfloat16)
    grad_self1 = jnp.dot(target_feats.T, slope_one, preferred_element_type=jnp.float32)
    grad_neigh1 = jnp.dot(agg_half.T, slope_one, preferred_element_type=jnp.float32)
    summed_one, summed_two = lax.psum(
        (jnp.stack([grad_self1, grad_neigh1]), jnp.stack([grad_self2, grad_neigh2])), "node"
    )
    return (output, summed_one, summed_two)


def solution(mesh):
    placed = (
        P("node", "feat"),
        P("node", "feat"),
        P("node", None, None),
        P("node", None),
        P("node"),
        P("feat", None),
        P("feat", None),
        P(),
        P(),
        P("node", None),
        P("node"),
        P("node", None),
    )
    return jax.shard_map(
        per_device,
        mesh=mesh,
        in_specs=placed,
        out_specs=(P("node", None), P(None, "feat", None), P(None, "feat", None)),
        check_vma=False,
    )
```

profile of v0, /device:TPU:1, one launch (start us, length us, event | category | flops | bytes accessed | tf_op | source)
XLA Modules:
  0.0 493.4 jit_solution(10480702718453900415)
XLA Ops:
  7.2 0.0 copy-start
  7.2 0.0 copy-start.6
  7.2 0.0 reduce-scatter.2.cloned.1.call-start
  7.9 1.0 copy.18
  9.0 0.2 broadcast_in_dim.13
  9.2 0.0 copy-done.6
  9.2 6.9 %while.10 = (s32[]{:T(128)}, f32[128,128,32]{1,2,0:T(8,128)S(1)}, s32[]{:T(128)}, s32[32,2]{0,1:T(2,128)S(1)}, bf16[32,128,128]{2,1,0:T(8,128)(2,1)}, /*index=5*...) while((s32[]{:T(128)}, f32[128,128,32]{1,2,0:T(8,128)S(1)}, ...), condition=%wide.region_2.3_spmd, body=%wide.region_0.2_spmd.sunk | while | flops 8455246 | bytes 987723 | solution.py:52
  9.3 0.1 constant_dynamic-slice_fusion.2
  9.3 0.6 gather_fusion
  9.9 0.7 compare_convert_fusion.2
  10.6 1.2 convolution_multiply_fusion.3
  11.8 0.8 scatter_fusion
  12.7 0.1 constant_dynamic-slice_fusion.2
  12.8 0.6 gather_fusion
  13.4 0.7 compare_convert_fusion.2
  14.1 1.2 convolution_multiply_fusion.3
  15.3 0.8 scatter_fusion
  16.2 1.5 copy_bitcast_fusion
  17.6 0.0 reduce-scatter.2.cloned.1.call-update
  17.7 0.0 all-reduce.3.cloned.1.call-start
  17.7 0.6 copy-done.5
  18.4 0.1 copy.21
  18.5 0.1 copy.20
  18.6 0.1 reshape.76
  18.7 0.1 reshape.56
  18.9 0.0 copy-done.4
  18.9 0.0 copy-done.7
  18.9 0.0 copy-start.9
  18.9 0.3 fusion.13
  19.2 98.8 %reduce-scatter.2.cloned.1.call-done = f32[1024,32]{0,1:T(8,128)} async-done(((f32[16384,32]{0,1:T(8,128)}), f32[1024,32]{0,1:T(8,128)}) %reduce-scatter.2.cloned.1.call-update) | async-done | bytes 131088 | tf_op jit(solution)/shard_map/reduce_scatter | solution.py:53
  118.1 0.0 copy-done.8
  118.1 2.2 convolution_add_fusion
  120.3 0.0 all-reduce.3.cloned.1.call-update
  120.3 0.0 all-reduce.5.cloned.1.call-start
  120.4 0.0 copy-done.9
  120.5 211.6 %all-reduce.3.cloned.1.call-done = f32[1024,256]{1,0:T(8,128)} async-done(((f32[1024,256]{1,0:T(8,128)}), f32[1024,256]{1,0:T(8,128)}) %all-reduce.3.cloned.1.call-update) | async-done | bytes 1048592 | tf_op jit(solution)/shard_map/psum | solution.py:60
  332.1 1.5 multiply_convert_fusion.1
  333.6 7.6 %gather_fusion.2 = bf16[2560,256]{1,0:T(8,128)(2,1)S(1)} fusion(bf16[1024,256]{1,0:T(8,128)(2,1)S(1)} %multiply_convert_fusion.1, s32[3072]{0:T(1024)S(1)} %pad_clamp_fusion.1), kind=kCustom, calls=%fused_computation.2 | custom fusion | bytes 2631680 | tf_op jit(solution)/shard_map/gather | solution.py:64
  341.1 2.1 reshape.110
  343.2 3.0 reduce_sum.9
  346.2 0.0 copy-start.10
  346.3 1.2 gather_fusion.1
  347.4 0.0 copy-done.3
  347.4 0.2 fusion.14
  347.6 0.0 copy-done
  347.6 0.9 multiply_convert_fusion.2
  348.6 0.2 convolution_bitcast_fusion.2
  348.8 0.3 convolution_bitcast_fusion.3
  349.1 0.2 convolution_multiply_fusion.1
  349.3 0.2 fusion.15
  349.5 2.3 broadcast_in_dim.27
  351.8 4.5 reshape.94
  356.3 14.9 %scatter_custom_fusion.1 = f32[1024,256]{1,0:T(8,128)S(1)} fusion(s32[2560]{0:T(1024)S(1)} %fusion.10, f32[2560,256]{1,0:T(8,128)} %reshape.94, f32[]{:T(128)} %constant.24.clone.1), kind=kCustom, calls=%fused_computation.27 | custom fusion | flops 655360 | bytes 1049088 | tf_op jit(solution)/shard_map/scatter-add | solution.py:83
  371.3 0.0 copy-start.1
  371.3 2.4 scatter_fusion.1
  373.7 0.4 multiply_convert_fusion
  374.1 0.2 convolution_bitcast_fusion
  374.3 0.3 copy-done.2
  374.6 0.2 convolution_bitcast_fusion.1
  374.8 0.6 pad_maximum_fusion
  375.4 0.0 all-reduce.5.cloned.1.call-update
  375.4 60.5 %psum.23 = f32[2,8,256]{2,1,0:T(8,128)} all-reduce(f32[2,8,256]{2,1,0:T(8,128)S(1)} %pad_maximum_fusion.1), channel_id=1, replica_groups=mesh['feat'=32,'node'=16] {'node'}, use_global_device_ids=true, to_apply=%region_9.10 | all-reduce | flops 4096 | bytes 32768 | tf_op jit(solution)/shard_map/psum | solution.py:90
  435.9 49.4 %all-reduce.5.cloned.1.call-done = f32[2,32,256]{2,1,0:T(8,128)} async-done(((f32[2,32,256]{2,1,0:T(8,128)}), f32[2,32,256]{2,1,0:T(8,128)}) %all-reduce.5.cloned.1.call-update) | async-done | bytes 65552 | tf_op jit(solution)/shard_map/psum | solution.py:90
  485.4 1.5 copy.36
  (19 shorter events, 0.1 us)
Async XLA Ops:
  7.2 340.4 %copy-start = (bf16[256,256]{1,0:T(8,128)(2,1)S(1)}, bf16[256,256]{1,0:T(8,128)(2,1)}, u32[]{:S(2)}) copy-start(bf16[256,256]{1,0:T(8,128)(2,1)} %param.22) | copy-start | bytes 393220
  7.2 2.0 copy-start.6
  7.2 110.9 %reduce-scatter.2.cloned.1.call-start = ((), (), s32[]{:S(2)}) async-start(), calls=%async_computation.1 | async-start | bytes 2228224 | tf_op jit(solution)/shard_map/reduce_scatter | solution.py:53
  17.6 0.7 copy-start.5
  17.6 1.3 copy-start.4
  17.6 1.3 copy-start.7
  17.6 100.4 %copy-start.8 = (bf16[32,256]{1,0:T(8,128)(2,1)S(1)}, bf16[32,256]{1,0:T(8,128)(2,1)}, u32[]{:S(2)}) copy-start(bf16[32,256]{1,0:T(8,128)(2,1)} %param.20) | copy-start | bytes 49156
  17.7 314.4 %all-reduce.3.cloned.1.call-start = ((), (), s32[]{:S(2)}) async-start(), calls=%async_computation.2 | async-start | bytes 2097152 | tf_op jit(solution)/shard_map/psum | solution.py:60
  18.9 101.5 %copy-start.9 = (s32[256]{0:T(256)S(1)}, s32[256]{0:T(256)}, u32[]{:S(2)}) copy-start(s32[256]{0:T(256)} %param.24) | copy-start | bytes 3076
  120.3 365.1 %all-reduce.5.cloned.1.call-start = ((), (), s32[]{:S(2)}) async-start(), calls=%async_computation.3 | async-start | bytes 131072 | tf_op jit(solution)/shard_map/psum | solution.py:90
  343.2 4.2 copy-start.3
  346.2 1.4 copy-start.10
  371.3 2.4 copy-start.1
  373.7 0.9 copy-start.2
Sparse Core Ops, SparseCore 0:
  17.8 100.2 reduce-scatter.1
  120.5 211.5 all-reduce.2
  375.6 109.7 all-reduce.4
where the time goes:
time: 492 us; the launch traced here: 493 us
  waiting for transfers between devices  360 us (73%)
  blocking collectives  60.5 us (12%)
  other arithmetic  25.9 us (5%)
  local copies, waits for them, and re-layouts  24.7 us (5%)
  between operations  14.7 us (3%)
  matrix products  7.45 us (2%)
    psum x1, waiting for transfers between devices, per_device(): pre_one = lax.psum(partial_pre, 'feat')  212 us
    reduce_scatter x1, waiting for transfers between devices, per_device(): lax.psum_scatter(aggregate, 'node', scatter_dimension=0, tiled=True)  98.8 us
    psum x1, blocking collectives, per_device(): lax.psum((jnp.stack([grad_self1, grad_neigh1]), jnp.stack([grad_self2, gr...  60.5 us
    psum x1, waiting for transfers between devices, per_device(): lax.psum((jnp.stack([grad_self1, grad_neigh1]), jnp.stack([grad_self2, gr...  49.4 us
    scatter-add x2, other arithmetic, per_device(): back_hidden = jnp.zeros((tgt_rows, hsize), jnp.float32).at[neighbors.resh...  17.3 us
  transfers between devices with their start and end apart: 3, of which 3 were waited for; matrix products, arithmetic and copies ran while one was open for 0% of the time, Pallas kernels for 0%

commit v1 on v0

v1 whole, which is shorter than its diff:
```python
import jax
import jax.numpy as jnp
from jax import lax
from jax.experimental import pallas as pl
from jax.experimental.pallas import tpu as pltpu
from jax.sharding import Mesh
from jax.sharding import PartitionSpec as P

BF16 = jnp.bfloat16
F32 = jnp.float32
NODE = ("x", "y")
FEAT = ("zh", "zl", "c")
MIB = 1 << 20

VMEM = pl.BlockSpec(memory_space=pltpu.VMEM)
SMEM = pl.BlockSpec(memory_space=pltpu.SMEM)


def contract(left, right, left_dim, right_dim):
    return lax.dot_general(
        left, right, (((left_dim,), (right_dim,)), ((), ())), preferred_element_type=F32
    )


def aggregate_kernel(count_ref, index_ref, tiles_ref, feats_ref, out_ref, sources, total):
    slots, block, _ = tiles_ref.shape
    for position in range(sources.shape[0]):
        sources[position] = feats_ref[:, position * block : (position + 1) * block]
    total[...] = jnp.zeros_like(total)
    live_tiles = count_ref[0]
    for slot in range(slots):
        target = index_ref[0, slot]
        source = index_ref[1, slot]
        in_use = (slot < live_tiles).astype(F32)
        product = contract(sources[source], tiles_ref[slot], 1, 1)
        total[target] += product * in_use
    out_ref[...] = total[...].astype(BF16)


def partial_kernel(core_ref, parts_ref, targets_ref, self_ref, neigh_ref, agg_ref, keep_ref, send_ref, halves):
    columns = targets_ref.shape[0]
    block = parts_ref.shape[2]
    owned = parts_ref[0].astype(F32)
    for position in range(1, parts_ref.shape[0]):
        owned += parts_ref[position].astype(F32)
    owned = owned.astype(BF16)
    for position in range(owned.shape[0] // columns):
        agg_ref[:, position * block : (position + 1) * block] = owned[
            position * columns : (position + 1) * columns
        ]
    inputs = jnp.concatenate([targets_ref[...], agg_ref[...]], axis=0)
    weights = jnp.concatenate([self_ref[...], neigh_ref[...]], axis=0)
    partial_pre = contract(inputs, weights, 0, 0)
    half = halves.shape[1]
    halves[0] = partial_pre[:half]
    halves[1] = partial_pre[half:]
    core = core_ref[0]
    keep_ref[...] = halves[core]
    send_ref[...] = halves[1 - core].astype(BF16)


def step_kernel(
    feat_ref,
    pre_ref,
    neighbors_ref,
    seeds_ref,
    self_ref,
    neigh_ref,
    cotangent_ref,
    targets_ref,
    agg_ref,
    output_ref,
    grads_ref,
    picks,
    scratch,
):
    rows = pre_ref.shape[0]
    fanout, seeds = neighbors_ref.shape
    columns = targets_ref.shape[0]
    row_of = lax.broadcasted_iota(jnp.int32, (rows, seeds), 0)
    counts = jnp.zeros((rows, seeds), F32)
    for entry in range(fanout):
        counts += (row_of == neighbors_ref[entry : entry + 1, :]).astype(F32)
    picks[:, :seeds] = counts.astype(BF16)
    picks[:, seeds:] = (row_of == seeds_ref[...]).astype(F32).astype(BF16)

    pre_one = pre_ref[...].astype(F32)
    sigmoid = jax.nn.sigmoid(pre_one)
    hidden = (pre_one * sigmoid).astype(BF16)
    gathered = contract(picks[...], hidden, 0, 0)
    nbr_mean = (gathered[:seeds] / fanout).astype(BF16)
    own = gathered[seeds:].astype(BF16)
    pre_two = contract(own, self_ref[...], 1, 0) + contract(nbr_mean, neigh_ref[...], 1, 0)
    gate = jax.nn.sigmoid(pre_two)
    output_ref[...] = (pre_two * gate).astype(BF16)
    slope_two = (
        cotangent_ref[...].astype(F32) * (gate * (1.0 + pre_two * (1.0 - gate)))
    ).astype(BF16)

    scratch[0] = contract(own, slope_two, 0, 0)
    scratch[1] = contract(nbr_mean, slope_two, 0, 0)

    back = jnp.concatenate(
        [contract(slope_two, neigh_ref[...], 1, 1) / fanout, contract(slope_two, self_ref[...], 1, 1)],
        axis=0,
    )
    back_high = back.astype(BF16)
    back_low = (back - back_high.astype(F32)).astype(BF16)
    chosen = picks[...]
    back_hidden = contract(chosen, back_high, 1, 0) + contract(chosen, back_low, 1, 0)
    slope_one = (back_hidden * (sigmoid * (1.0 + pre_one * (1.0 - sigmoid)))).astype(BF16)
    inputs = jnp.concatenate([targets_ref[...], agg_ref[...]], axis=0)
    grad_one = contract(inputs, slope_one, 1, 0).astype(BF16)
    part_rows = (grads_ref.shape[1] - 2 * columns) // 2
    first = pl.multiple_of(feat_ref[0] * part_rows, part_rows)
    grad_two = jnp.concatenate(
        [scratch[0, pl.ds(first, part_rows), :], scratch[1, pl.ds(first, part_rows), :]], axis=0
    ).astype(BF16)
    every = jnp.concatenate([grad_one, grad_two], axis=0)
    for position in range(grads_ref.shape[0]):
        grads_ref[position] = every


def per_device(
    features,
    target_feats,
    tile_values,
    tile_index,
    tile_count,
    self_weight1,
    neigh_weight1,
    self_weight2,
    neigh_weight2,
    neighbors,
    seed_index,
    cotangent,
):
    src_rows, columns = features.shape
    tgt_rows = target_feats.shape[0]
    slots, block, _ = tile_values.shape
    hsize = self_weight2.shape[0]
    owners = lax.axis_size(NODE)
    feat_count = lax.axis_size(FEAT)
    part_rows = hsize // feat_count
    near, far = lax.axis_size("zl"), lax.axis_size("zh")
    all_blocks = tgt_rows * owners // block
    targets = target_feats.T
    core = lax.axis_index("c").reshape(1)
    feat = lax.axis_index(FEAT).reshape(1)

    with jax.named_scope("aggregate_tiles"):
        aggregate = pl.pallas_call(
            aggregate_kernel,
            out_shape=jax.ShapeDtypeStruct((all_blocks, columns, block), BF16),
            in_specs=[SMEM, SMEM, VMEM, VMEM],
            out_specs=VMEM,
            scratch_shapes=[
                pltpu.VMEM((src_rows // block, columns, block), BF16),
                pltpu.VMEM((all_blocks, columns, block), F32),
            ],
            compiler_params=pltpu.CompilerParams(vmem_limit_bytes=16 * MIB),
        )(tile_count, tile_index.T, tile_values, features.T)
    with jax.named_scope("aggregate_exchange"):
        parts = lax.all_to_all(
            aggregate.reshape(owners, tgt_rows // block * columns, block), NODE, 0, 0, tiled=True
        )
    half = tgt_rows // 2
    with jax.named_scope("partial_pre"):
        agg_half, keep, send = pl.pallas_call(
            partial_kernel,
            out_shape=[
                jax.ShapeDtypeStruct((columns, tgt_rows), BF16),
                jax.ShapeDtypeStruct((half, hsize), F32),
                jax.ShapeDtypeStruct((half, hsize), BF16),
            ],
            in_specs=[SMEM] + [VMEM] * 4,
            out_specs=[VMEM] * 3,
            scratch_shapes=[pltpu.VMEM((2, half, hsize), F32)],
            compiler_params=pltpu.CompilerParams(vmem_limit_bytes=16 * MIB),
        )(core, parts, targets, self_weight1, neigh_weight1)
    with jax.named_scope("pre_sum_cores"):
        pair = keep + lax.ppermute(send, "c", [(0, 1), (1, 0)]).astype(F32)
    with jax.named_scope("pre_sum_near"):
        rows = half // near
        blocks = lax.all_to_all(
            pair.astype(BF16).reshape(near, rows, hsize), "zl", 0, 0, tiled=True
        )
        quarter = jnp.sum(blocks.astype(F32), axis=0).astype(BF16)
    with jax.named_scope("pre_sum_far"):
        copies = lax.all_to_all(
            jnp.broadcast_to(quarter[None], (far, rows, hsize)), "zh", 0, 0, tiled=True
        )
        pre_rows = jnp.sum(copies.astype(F32), axis=0).astype(BF16)
    with jax.named_scope("pre_gather"):
        pre_one = lax.all_gather(pre_rows, ("c", "zl"), tiled=True)

    grad_rows = 2 * columns + 2 * part_rows
    with jax.named_scope("step"):
        output, grads = pl.pallas_call(
            step_kernel,
            out_shape=[
                jax.ShapeDtypeStruct(cotangent.shape, BF16),
                jax.ShapeDtypeStruct((owners, grad_rows, hsize), BF16),
            ],
            in_specs=[SMEM] + [VMEM] * 8,
            out_specs=[VMEM] * 2,
            scratch_shapes=[
                pltpu.VMEM((tgt_rows, 2 * neighbors.shape[0]), BF16),
                pltpu.VMEM((2, hsize, hsize), F32),
            ],
            compiler_params=pltpu.CompilerParams(vmem_limit_bytes=32 * MIB),
        )(
            feat,
            pre_one,
            neighbors.T,
            seed_index.reshape(1, -1),
            self_weight2,
            neigh_weight2,
            cotangent,
            targets,
            agg_half,
        )
    with jax.named_scope("grad_sum"):
        grads = lax.all_to_all(grads, NODE, 0, 0, tiled=True)
        grads = jnp.sum(grads.astype(F32), axis=0)
    grad_one = grads[: 2 * columns].reshape(2, columns, hsize)
    grad_two = grads[2 * columns :].reshape(2, part_rows, hsize)
    return (output, grad_one, grad_two)


def solution(mesh):
    fine = Mesh(mesh.devices.reshape(4, 4, 2, 4, 4), FEAT + NODE)
    placed = (
        P(NODE, FEAT),
        P(NODE, FEAT),
        P(NODE, None, None),
        P(NODE, None),
        P(NODE),
        P(FEAT, None),
        P(FEAT, None),
        P(),
        P(),
        P(NODE, None),
        P(NODE),
        P(NODE, None),
    )
    return jax.shard_map(
        per_device,
        mesh=fine,
        in_specs=placed,
        out_specs=(P(NODE, None), P(None, FEAT, None), P(None, FEAT, None)),
        check_vma=False,
    )
```

time: 492 us -> 129 us (0.26)
  waiting for transfers between devices: 360 us -> 28.5 us
  other arithmetic: 25.9 us -> 0.23 us
  starting transfers between devices: 0.12 us -> 25.6 us
  local copies, waits for them, and re-layouts: 24.7 us -> 4.73 us
  between operations: 14.7 us -> 1.38 us
  matrix products: 7.45 us -> 0 us
  Pallas kernels: 0 us -> 6.06 us
    psum x2 -> x0, waiting for transfers between devices: 261 us -> none  [the longest x1 212 us: per_device(): pre_one = lax.psum(partial_pre, 'feat')]
    reduce_scatter x1 -> x0, waiting for transfers between devices: 98.8 us -> none  [per_device(): lax.psum_scatter(aggregate, 'node', scatter_dimension=0, tiled=True)]
    psum x1 -> x0, blocking collectives: 60.5 us -> none  [per_device(): lax.psum((jnp.stack([grad_self1, grad_neigh1]), jnp.stack([grad_self2, gr...]
    all_gather x0 -> x1, blocking collectives: none -> 34.4 us  [per_device(): pre_one = lax.all_gather(pre_rows, ('c', 'zl'), tiled=True)]
    all_to_all x0 -> x2, blocking collectives: none -> 28 us  [the longest x1 15 us: per_device(): grads = lax.all_to_all(grads, NODE, 0, 0, tiled=True)]
    all_to_all x0 -> x2, waiting for transfers between devices: none -> 27.3 us  [the longest x1 14.2 us: per_device(): lax.all_to_all(aggregate.reshape(owners, tgt_rows // block * columns, blo...]
    all_to_all x0 -> x2, starting transfers between devices: none -> 19.8 us  [the longest x1 12.1 us: per_device(): lax.all_to_all(jnp.broadcast_to(quarter[None], (far, rows, hsize)), 'zh',...]
    scatter-add x4 -> x0, other arithmetic: 19 us -> none  [the longest x2 17.3 us: per_device(): back_hidden = jnp.zeros((tgt_rows, hsize), jnp.float32).at[neighbors.resh...]
where the time goes in v1:
time: 129 us
  blocking collectives  62.5 us (48%)
  waiting for transfers between devices  28.5 us (22%)
  starting transfers between devices  25.6 us (20%)
  Pallas kernels  6.06 us (5%)
  local copies, waits for them, and re-layouts  4.73 us (4%)
  between operations  1.38 us (1%)
    all_gather x1, blocking collectives, per_device(): pre_one = lax.all_gather(pre_rows, ('c', 'zl'), tiled=True)  34.4 us
    all_to_all x1, blocking collectives, per_device(): grads = lax.all_to_all(grads, NODE, 0, 0, tiled=True)  15 us
    all_to_all x1, waiting for transfers between devices, per_device(): lax.all_to_all(aggregate.reshape(owners, tgt_rows // block * columns, blo...  14.2 us
    all_to_all x1, waiting for transfers between devices, per_device(): lax.all_to_all(jnp.broadcast_to(quarter[None], (far, rows, hsize)), 'zh',...  13.1 us
    all_to_all x1, blocking collectives, per_device(): lax.all_to_all(pair.astype(BF16).reshape(near, rows, hsize), 'zl', 0, 0,...  13 us
    all_to_all x1, starting transfers between devices, per_device(): lax.all_to_all(jnp.broadcast_to(quarter[None], (far, rows, hsize)), 'zh',...  12.1 us
    all_to_all x1, starting transfers between devices, per_device(): lax.all_to_all(aggregate.reshape(owners, tgt_rows // block * columns, blo...  7.72 us
    ppermute x1, starting transfers between devices, per_device(): pair = keep + lax.ppermute(send, 'c', [(0, 1), (1, 0)]).astype(F32)  5.74 us
  transfers between devices with their start and end apart: 3, of which 3 were waited for; matrix products, arithmetic and copies ran while one was open for 0% of the time, Pallas kernels for 0%

profile of v1, /device:TPU:1, one launch (start us, length us, event | category | flops | bytes accessed | tf_op | source)
XLA Modules:
  0.0 128.9 jit_solution(14286826030484190661)
XLA Ops:
  1.3 0.0 copy-start
  1.3 1.2 copy-done
  2.5 0.0 copy-start.5
  2.5 0.8 copy-done.5
  3.3 0.0 copy-start.9
  3.3 0.7 copy-done.9
  4.0 2.3 %aggregate_tiles.1 = bf16[128,32,128]{2,1,0:T(8,128)(2,1)} custom-call(s32[1]{0:T(128)S(6)} %copy.15.count_ref, s32[2,32]{1,0:T(2,128)S(1)} %bitcast.16, bf16[32,128,128]{2,1,0:T(8,128)(2,1)S(1)} %copy-done, bf16[32,1024]{1,0:T(8,128)(2,1)S(1)} %bitcast.14), custom_call_target="tpu_custom_call" | custom-call | tf_op jit(solution)/shard_map/aggregate_tiles/pallas_call | solution.py:152
  6.3 0.0 copy-start.1
  6.3 0.0 copy-start.6
  6.3 0.0 copy-start.7
  6.3 7.7 %all-to-all-start = ((bf16[16,256,128]{2,1,0:T(8,128)(2,1)}), bf16[16,256,128]{2,1,0:T(8,128)(2,1)S(1)}, u32[]{:S(2)}, u32[]{:S(2)}) async-start(bf16[16,256,128]{2,1,0:T(8,128)(2,1)} %bitcast.4), calls=%async_computation | async-start | bytes 2097152 | tf_op jit(solution)/shard_map/aggregate_exchange/all_to_all | solution.py:164
  14.0 14.2 %all-to-all-done.parts_ref = bf16[16,256,128]{2,1,0:T(8,128)(2,1)S(1)} async-done(((bf16[16,256,128]{2,1,0:T(8,128)(2,1)}), bf16[16,256,128]{2,1,0:T(8,128)(2,1)S(1)}, u32[]{:S(2)}, u32[]{:S(2)}) %all-to-all-start) | async-done | bytes 1048608 | tf_op jit(solution)/shard_map/aggregate_exchange/all_to_all | solution.py:164
  28.3 0.0 copy-done.1
  28.3 0.0 copy-done.6
  28.3 0.0 copy-done.7
  28.3 0.5 partial_pre.1
  28.7 5.7 %collective-permute-start = (bf16[512,256]{1,0:T(8,128)(2,1)S(1)}, bf16[512,256]{1,0:T(8,128)(2,1)S(1)}, u32[]{:S(2)}, u32[]{:S(2)}) collective-permute-start(bf16[512,256]{1,0:T(8,128)(2,1)S(1)} %get-tuple-element.9), channel_id=1, source_target_pairs={{0,16},{16,0},{1,17},{17,1},{2,18},{18,2},{3,19},{19,3},{4,20},{20... | collective-permute-start | bytes 786440 | tf_op jit(solution)/shard_map/pre_sum_cores/ppermute | solution.py:182
  34.5 1.1 collective-permute-done
  35.6 0.1 add_convert_fusion
  35.7 13.0 %all_to_all.20 = bf16[4,128,256]{2,1,0:T(8,128)(2,1)S(1)} all-to-all(bf16[4,128,256]{2,1,0:T(8,128)(2,1)S(1)} %bitcast.18), channel_id=1, replica_groups=mesh['zh'=4,'zl'=4,'c'=2,'x'=4,'y'=4] {'zl'}, dimensions={0} | all-to-all | bytes 524288 | tf_op jit(solution)/shard_map/pre_sum_near/all_to_all | solution.py:185
  48.7 0.0 copy-start.2
  48.7 0.0 copy-start.3
  48.7 0.0 copy-start.4
  48.7 0.0 copy-start.8
  48.7 0.0 copy-start.10
  48.8 0.7 broadcast_in_dim.2
  49.5 12.1 %all-to-all-start.2 = ((bf16[4,128,256]{2,1,0:T(8,128)(2,1)}), bf16[4,128,256]{2,1,0:T(8,128)(2,1)S(1)}, u32[]{:S(2)}, u32[]{:S(2)}) async-start(bf16[4,128,256]{2,1,0:T(8,128)(2,1)} %broadcast_in_dim.2), calls=%async_computation.2 | async-start | bytes 524288 | tf_op jit(solution)/shard_map/pre_sum_far/all_to_all | solution.py:190
  61.6 13.1 %all-to-all-done.2 = bf16[4,128,256]{2,1,0:T(8,128)(2,1)S(1)} async-done(((bf16[4,128,256]{2,1,0:T(8,128)(2,1)}), bf16[4,128,256]{2,1,0:T(8,128)(2,1)S(1)}, u32[]{:S(2)}, u32[]{:S(2)}) %all-to-all-start.2) | async-done | bytes 262176 | tf_op jit(solution)/shard_map/pre_sum_far/all_to_all | solution.py:190
  74.7 34.4 %all_gather.3.pre_ref = bf16[1024,256]{1,0:T(8,128)(2,1)S(1)} all-gather(bf16[128,256]{1,0:T(8,128)(2,1)S(1)} %reduce_sum.34), channel_id=1, replica_groups=mesh['zh'=4,'zl'=4,'c'=2,'x'=4,'y'=4] {'c','zl'}, dimensions={0}, use_global_device_ids=true | all-gather | bytes 589824 | tf_op jit(solution)/shard_map/pre_gather/all_gather | solution.py:195
  109.2 0.0 copy-done.2
  109.2 0.0 copy-done.3
  109.2 0.0 copy-done.4
  109.2 0.0 copy-done.8
  109.2 0.0 copy-done.10
  109.2 3.3 %step.1 = (bf16[256,256]{1,0:T(8,128)(2,1)}, bf16[16,80,256]{2,1,0:T(8,128)(2,1)S(1)}) custom-call(s32[1]{0:T(128)} %bitcast.feat_ref, bf16[1024,256]{1,0:T(8,128)(2,1)S(1)} %all_gather.3.pre_ref, s32[10,256]{1,0:T(8,128)S(1)} %bitcast.15, s32[1,256]{1,0:T(1,128)S(1)} %bitcast.17, bf16[256,256]{1,0:T(8,128)(2,1)S(1)} %copy-done.2, ...), custom_call_target="tpu_custom_call" | custom-call | tf_op jit(solution)/shard_map/step/pallas_call | solution.py:199
  112.5 15.0 %all_to_all.21 = bf16[16,80,256]{2,1,0:T(8,128)(2,1)S(1)} all-to-all(bf16[16,80,256]{2,1,0:T(8,128)(2,1)S(1)} %get-tuple-element.12), channel_id=1, replica_groups=mesh['zh'=4,'zl'=4,'c'=2,'x'=4,'y'=4] {'x','y'}, dimensions={0} | all-to-all | bytes 1310720 | tf_op jit(solution)/shard_map/grad_sum/all_to_all | solution.py:224
  127.6 0.1 convert_reduce_fusion
  127.7 0.6 slice_bitcast_fusion
  128.3 0.6 slice.8
  (2 shorter events, 0.1 us)
Async XLA Ops:
  1.3 1.2 copy-start
  2.5 0.8 copy-start.5
  3.3 0.7 copy-start.9
  6.3 22.0 %copy-start.1 = (bf16[1024,32]{0,1:T(8,128)(2,1)S(1)}, bf16[1024,32]{0,1:T(8,128)(2,1)}, u32[]{:S(2)}) copy-start(bf16[1024,32]{0,1:T(8,128)(2,1)} %param.13) | copy-start | bytes 196612
  6.3 22.0 %copy-start.6 = (bf16[32,256]{1,0:T(8,128)(2,1)S(1)}, bf16[32,256]{1,0:T(8,128)(2,1)}, u32[]{:S(2)}) copy-start(bf16[32,256]{1,0:T(8,128)(2,1)} %self_ref.2) | copy-start | bytes 49156
  6.3 22.0 %copy-start.7 = (bf16[32,256]{1,0:T(8,128)(2,1)S(1)}, bf16[32,256]{1,0:T(8,128)(2,1)}, u32[]{:S(2)}) copy-start(bf16[32,256]{1,0:T(8,128)(2,1)} %neigh_ref.2) | copy-start | bytes 49156
  6.3 22.0 %all-to-all-start = ((bf16[16,256,128]{2,1,0:T(8,128)(2,1)}), bf16[16,256,128]{2,1,0:T(8,128)(2,1)S(1)}, u32[]{:S(2)}, u32[]{:S(2)}) async-start(bf16[16,256,128]{2,1,0:T(8,128)(2,1)} %bitcast.4), calls=%async_computation | async-start | bytes 2097152 | tf_op jit(solution)/shard_map/aggregate_exchange/all_to_all | solution.py:164
  28.7 6.9 %collective-permute-start = (bf16[512,256]{1,0:T(8,128)(2,1)S(1)}, bf16[512,256]{1,0:T(8,128)(2,1)S(1)}, u32[]{:S(2)}, u32[]{:S(2)}) collective-permute-start(bf16[512,256]{1,0:T(8,128)(2,1)S(1)} %get-tuple-element.9), channel_id=1, source_target_pairs={{0,16},{16,0},{1,17},{17,1},{2,18},{18,2},{3,19},{19,3},{4,20},{20... | collective-permute-start | bytes 786440 | tf_op jit(solution)/shard_map/pre_sum_cores/ppermute | solution.py:182
  48.7 60.5 %copy-start.2 = (bf16[256,256]{1,0:T(8,128)(2,1)S(1)}, bf16[256,256]{1,0:T(8,128)(2,1)}, u32[]{:S(2)}) copy-start(bf16[256,256]{1,0:T(8,128)(2,1)} %self_ref.3) | copy-start | bytes 393220
  48.7 60.5 %copy-start.3 = (bf16[256,256]{1,0:T(8,128)(2,1)S(1)}, bf16[256,256]{1,0:T(8,128)(2,1)}, u32[]{:S(2)}) copy-start(bf16[256,256]{1,0:T(8,128)(2,1)} %neigh_ref.3) | copy-start | bytes 393220
  48.7 60.5 %copy-start.4 = (bf16[256,256]{1,0:T(8,128)(2,1)S(1)}, bf16[256,256]{1,0:T(8,128)(2,1)}, u32[]{:S(2)}) copy-start(bf16[256,256]{1,0:T(8,128)(2,1)} %cotangent_ref.1) | copy-start | bytes 393220
  48.7 60.5 %copy-start.8 = (s32[256,10]{0,1:T(8,128)S(1)}, s32[256,10]{0,1:T(8,128)}, u32[]{:S(2)}) copy-start(s32[256,10]{0,1:T(8,128)} %param.21) | copy-start | bytes 30724
  48.7 60.5 %copy-start.10 = (s32[256]{0:T(256)S(1)}, s32[256]{0:T(256)}, u32[]{:S(2)}) copy-start(s32[256]{0:T(256)} %param.22) | copy-start | bytes 3076
  49.5 25.2 %all-to-all-start.2 = ((bf16[4,128,256]{2,1,0:T(8,128)(2,1)}), bf16[4,128,256]{2,1,0:T(8,128)(2,1)S(1)}, u32[]{:S(2)}, u32[]{:S(2)}) async-start(bf16[4,128,256]{2,1,0:T(8,128)(2,1)} %broadcast_in_dim.2), calls=%async_computation.2 | async-start | bytes 524288 | tf_op jit(solution)/shard_map/pre_sum_far/all_to_all | solution.py:190

commit v2 on v1

--- a/solution.py
+++ b/solution.py
@@ -9,10 +9,12 @@
 BF16 = jnp.bfloat16
 F32 = jnp.float32
 NODE = ("x", "y")
-FEAT = ("zh", "zl", "c")
+DEPTH = ("z",)
+FEAT = ("z", "c")
 MIB = 1 << 20
 
 VMEM = pl.BlockSpec(memory_space=pltpu.VMEM)
+HBM = pl.BlockSpec(memory_space=pltpu.HBM)
 SMEM = pl.BlockSpec(memory_space=pltpu.SMEM)
 
 
@@ -22,17 +24,31 @@
     )
 
 
-def aggregate_kernel(count_ref, index_ref, tiles_ref, feats_ref, out_ref, sources, total):
-    slots, block, _ = tiles_ref.shape
+def aggregate_kernel(
+    count_ref, index_ref, tiles_ref, feats_ref, out_ref, tiles, feats, sources, total, tile_sem, feat_sem
+):
+    slots, block, _ = tiles.shape
+    group = slots // tile_sem.shape[0]
+    feat_copy = pltpu.make_async_copy(feats_ref, feats, feat_sem)
+    feat_copy.start()
+    tile_copies = []
+    for position in range(tile_sem.shape[0]):
+        span = pl.ds(position * group, group)
+        copy = pltpu.make_async_copy(tiles_ref.at[span], tiles.at[span], tile_sem.at[position])
+        copy.start()
+        tile_copies.append(copy)
+    total[...] = jnp.zeros_like(total)
+    feat_copy.wait()
     for position in range(sources.shape[0]):
-        sources[position] = feats_ref[:, position * block : (position + 1) * block]
-    total[...] = jnp.zeros_like(total)
+        sources[position] = feats[:, position * block : (position + 1) * block]
     live_tiles = count_ref[0]
     for slot in range(slots):
+        if slot % group == 0:
+            tile_copies[slot // group].wait()
         target = index_ref[0, slot]
         source = index_ref[1, slot]
         in_use = (slot < live_tiles).astype(F32)
-        product = contract(sources[source], tiles_ref[slot], 1, 1)
+        product = contract(sources[source], tiles[slot], 1, 1)
         total[target] += product * in_use
     out_ref[...] = total[...].astype(BF16)
 
@@ -51,12 +67,31 @@
     inputs = jnp.concatenate([targets_ref[...], agg_ref[...]], axis=0)
     weights = jnp.concatenate([self_ref[...], neigh_ref[...]], axis=0)
     partial_pre = contract(inputs, weights, 0, 0)
-    half = halves.shape[1]
-    halves[0] = partial_pre[:half]
-    halves[1] = partial_pre[half:]
+    _, spans, span, _ = halves.shape
+    for position in range(2 * spans):
+        halves[position % 2, position // 2] = partial_pre[position * span : (position + 1) * span]
     core = core_ref[0]
     keep_ref[...] = halves[core]
-    send_ref[...] = halves[1 - core].astype(BF16)
+    send_ref[...] = halves[1 - core]
+
+
+def sum_kernel(parts_ref, out_ref):
+    total = parts_ref[0].astype(F32)
+    for position in range(1, parts_ref.shape[0]):
+        total += parts_ref[position].astype(F32)
+    out_ref[...] = total.astype(out_ref.dtype)
+
+
+def grads_kernel(parts_ref, one_ref, two_ref):
+    total = parts_ref[0].astype(F32)
+    for position in range(1, parts_ref.shape[0]):
+        total += parts_ref[position].astype(F32)
+    columns, part_rows = one_ref.shape[1], two_ref.shape[1]
+    one_ref[0] = total[:columns]
+    one_ref[1] = total[columns : 2 * columns]
+    two = total[2 * columns : 2 * columns + 2 * part_rows] + total[2 * columns + 2 * part_rows :]
+    two_ref[0] = two[:part_rows]
+    two_ref[1] = two[part_rows:]
 
 
 def step_kernel(
@@ -111,12 +146,14 @@
     slope_one = (back_hidden * (sigmoid * (1.0 + pre_one * (1.0 - sigmoid)))).astype(BF16)
     inputs = jnp.concatenate([targets_ref[...], agg_ref[...]], axis=0)
     grad_one = contract(inputs, slope_one, 1, 0).astype(BF16)
-    part_rows = (grads_ref.shape[1] - 2 * columns) // 2
+    part_rows = (grads_ref.shape[1] - 2 * columns) // 4
     first = pl.multiple_of(feat_ref[0] * part_rows, part_rows)
     grad_two = jnp.concatenate(
         [scratch[0, pl.ds(first, part_rows), :], scratch[1, pl.ds(first, part_rows), :]], axis=0
-    ).astype(BF16)
-    every = jnp.concatenate([grad_one, grad_two], axis=0)
+    )
+    two_high = grad_two.astype(BF16)
+    two_low = (grad_two - two_high.astype(F32)).astype(BF16)
+    every = jnp.concatenate([grad_one, two_high, two_low], axis=0)
     for position in range(grads_ref.shape[0]):
         grads_ref[position] = every
 
@@ -142,7 +179,8 @@
     owners = lax.axis_size(NODE)
     feat_count = lax.axis_size(FEAT)
     part_rows = hsize // feat_count
-    near, far = lax.axis_size("zl"), lax.axis_size("zh")
+    deep = lax.axis_size(DEPTH)
+    span = tgt_rows // feat_count
     all_blocks = tgt_rows * owners // block
     targets = target_feats.T
     core = lax.axis_index("c").reshape(1)
@@ -151,12 +189,16 @@
     with jax.named_scope("aggregate_tiles"):
         aggregate = pl.pallas_call(
             aggregate_kernel,
-            out_shape=jax.ShapeDtypeStruct((all_blocks, columns, block), BF16),
-            in_specs=[SMEM, SMEM, VMEM, VMEM],
+            out_shape=pltpu.VMEM((all_blocks, columns, block), BF16),
+            in_specs=[SMEM, SMEM, HBM, HBM],
             out_specs=VMEM,
             scratch_shapes=[
+                pltpu.VMEM(tile_values.shape, BF16),
+                pltpu.VMEM((columns, src_rows), BF16),
                 pltpu.VMEM((src_rows // block, columns, block), BF16),
                 pltpu.VMEM((all_blocks, columns, block), F32),
+                pltpu.SemaphoreType.DMA((4,)),
+                pltpu.SemaphoreType.DMA,
             ],
             compiler_params=pltpu.CompilerParams(vmem_limit_bytes=16 * MIB),
         )(tile_count, tile_index.T, tile_values, features.T)
@@ -164,37 +206,33 @@
         parts = lax.all_to_all(
             aggregate.reshape(owners, tgt_rows // block * columns, block), NODE, 0, 0, tiled=True
         )
-    half = tgt_rows // 2
     with jax.named_scope("partial_pre"):
         agg_half, keep, send = pl.pallas_call(
             partial_kernel,
             out_shape=[
                 jax.ShapeDtypeStruct((columns, tgt_rows), BF16),
-                jax.ShapeDtypeStruct((half, hsize), F32),
-                jax.ShapeDtypeStruct((half, hsize), BF16),
+                jax.ShapeDtypeStruct((deep, span, hsize), F32),
+                jax.ShapeDtypeStruct((deep, span, hsize), F32),
             ],
             in_specs=[SMEM] + [VMEM] * 4,
             out_specs=[VMEM] * 3,
-            scratch_shapes=[pltpu.VMEM((2, half, hsize), F32)],
+            scratch_shapes=[pltpu.VMEM((2, deep, span, hsize), F32)],
             compiler_params=pltpu.CompilerParams(vmem_limit_bytes=16 * MIB),
         )(core, parts, targets, self_weight1, neigh_weight1)
     with jax.named_scope("pre_sum_cores"):
-        pair = keep + lax.ppermute(send, "c", [(0, 1), (1, 0)]).astype(F32)
-    with jax.named_scope("pre_sum_near"):
-        rows = half // near
-        blocks = lax.all_to_all(
-            pair.astype(BF16).reshape(near, rows, hsize), "zl", 0, 0, tiled=True
-        )
-        quarter = jnp.sum(blocks.astype(F32), axis=0).astype(BF16)
-    with jax.named_scope("pre_sum_far"):
-        copies = lax.all_to_all(
-            jnp.broadcast_to(quarter[None], (far, rows, hsize)), "zh", 0, 0, tiled=True
-        )
-        pre_rows = jnp.sum(copies.astype(F32), axis=0).astype(BF16)
+        pair = (keep + lax.ppermute(send, "c", [(0, 1), (1, 0)])).astype(BF16)
+    with jax.named_scope("pre_sum_depth"):
+        pieces = lax.all_to_all(pair, DEPTH, 0, 0, tiled=True)
+        pre_rows = pl.pallas_call(
+            sum_kernel,
+            out_shape=jax.ShapeDtypeStruct((span, hsize), BF16),
+            in_specs=[VMEM],
+            out_specs=VMEM,
+        )(pieces)
     with jax.named_scope("pre_gather"):
-        pre_one = lax.all_gather(pre_rows, ("c", "zl"), tiled=True)
-
-    grad_rows = 2 * columns + 2 * part_rows
+        pre_one = lax.all_gather(pre_rows, FEAT, tiled=True)
+
+    grad_rows = 2 * columns + 4 * part_rows
     with jax.named_scope("step"):
         output, grads = pl.pallas_call(
             step_kernel,
@@ -222,14 +260,20 @@
         )
     with jax.named_scope("grad_sum"):
         grads = lax.all_to_all(grads, NODE, 0, 0, tiled=True)
-        grads = jnp.sum(grads.astype(F32), axis=0)
-    grad_one = grads[: 2 * columns].reshape(2, columns, hsize)
-    grad_two = grads[2 * columns :].reshape(2, part_rows, hsize)
+        grad_one, grad_two = pl.pallas_call(
+            grads_kernel,
+            out_shape=[
+                jax.ShapeDtypeStruct((2, columns, hsize), F32),
+                jax.ShapeDtypeStruct((2, part_rows, hsize), F32),
+            ],
+            in_specs=[VMEM],
+            out_specs=[VMEM] * 2,
+        )(grads)
     return (output, grad_one, grad_two)
 
 
 def solution(mesh):
-    fine = Mesh(mesh.devices.reshape(4, 4, 2, 4, 4), FEAT + NODE)
+    fine = Mesh(mesh.devices.reshape(16, 2, 4, 4), FEAT + NODE)
     placed = (
         P(NODE, FEAT),
         P(NODE, FEAT),

time: 129 us -> 130 us (level)
  blocking collectives: 62.5 us -> 54.5 us
  Pallas kernels: 6.06 us -> 10.3 us
  starting transfers between devices: 25.6 us -> 29 us
    all_to_all x1 -> x0, blocking collectives: 13 us -> none  [per_device(): lax.all_to_all(pair.astype(BF16).reshape(near, rows, hsize), 'zl', 0, 0,...]
    pallas_call x1 -> x3, Pallas kernels: 2.28 us -> 6.45 us  [the longest x1 3.01 us: per_device(): pl.pallas_call(aggregate_kernel, out_shape=pltpu.VMEM((all_blocks, column...]
    all_to_all x1, starting transfers between devices: 12.1 us -> 15.5 us  [per_device(): pieces = lax.all_to_all(pair, DEPTH, 0, 0, tiled=True)]
    all_gather x1, blocking collectives: 34.4 us -> 37.7 us  [per_device(): pre_one = lax.all_gather(pre_rows, FEAT, tiled=True)]
    all_to_all x1, blocking collectives: 15 us -> 16.9 us  [per_device(): grads = lax.all_to_all(grads, NODE, 0, 0, tiled=True)]
    unnamed x22 -> x24, local copies, waits for them, and re-layouts: 2.77 us -> 4.11 us
where the time goes in v2:
time: 130 us
  blocking collectives  54.5 us (42%)
  waiting for transfers between devices  29.7 us (23%)
  starting transfers between devices  29 us (22%)
  Pallas kernels  10.3 us (8%)
  local copies, waits for them, and re-layouts  4.11 us (3%)
  between operations  1.41 us (1%)
    all_gather x1, blocking collectives, per_device(): pre_one = lax.all_gather(pre_rows, FEAT, tiled=True)  37.7 us
    all_to_all x1, blocking collectives, per_device(): grads = lax.all_to_all(grads, NODE, 0, 0, tiled=True)  16.9 us
    all_to_all x1, starting transfers between devices, per_device(): pieces = lax.all_to_all(pair, DEPTH, 0, 0, tiled=True)  15.5 us
    all_to_all x1, waiting for transfers between devices, per_device(): lax.all_to_all(aggregate.reshape(owners, tgt_rows // block * columns, blo...  14.2 us
    all_to_all x1, waiting for transfers between devices, per_device(): pieces = lax.all_to_all(pair, DEPTH, 0, 0, tiled=True)  14 us
    all_to_all x1, starting transfers between devices, per_device(): lax.all_to_all(aggregate.reshape(owners, tgt_rows // block * columns, blo...  7.73 us
    ppermute x1, starting transfers between devices, per_device(): pair = (keep + lax.ppermute(send, 'c', [(0, 1), (1, 0)])).astype(BF16)  5.74 us
    unnamed x24, local copies, waits for them, and re-layouts  4.11 us
  transfers between devices with their start and end apart: 3, of which 3 were waited for; matrix products, arithmetic and copies ran while one was open for 0% of the time, Pallas kernels for 0%

profile of v2, /device:TPU:1, one launch (start us, length us, event | category | flops | bytes accessed | tf_op | source)
XLA Modules:
  0.0 129.8 jit_solution(2658562633976561802)
XLA Ops:
  1.3 0.0 copy-start.9
  1.3 0.7 copy-done.9
  2.0 0.0 copy-start
  2.0 1.2 copy-done
  3.2 0.0 copy-start.5
  3.2 0.8 copy-done.5
  4.0 3.0 %aggregate_tiles.1 = bf16[128,32,128]{2,1,0:T(8,128)(2,1)} custom-call(s32[1]{0:T(128)S(6)} %copy.15.count_ref, s32[2,32]{1,0:T(2,128)S(1)} %bitcast.12, bf16[32,128,128]{2,1,0:T(8,128)(2,1)S(1)} %copy-done, bf16[32,1024]{1,0:T(8,128)(2,1)S(1)} %bitcast.10), custom_call_target="tpu_custom_call" | custom-call | tf_op jit(solution)/shard_map/aggregate_tiles/pallas_call | solution.py:190
  7.0 0.0 copy-start.1
  7.1 0.0 copy-start.6
  7.1 0.0 copy-start.7
  7.1 7.7 %all-to-all-start = ((bf16[16,256,128]{2,1,0:T(8,128)(2,1)}), bf16[16,256,128]{2,1,0:T(8,128)(2,1)S(1)}, u32[]{:S(2)}, u32[]{:S(2)}) async-start(bf16[16,256,128]{2,1,0:T(8,128)(2,1)} %bitcast.4), calls=%async_computation | async-start | bytes 2097152 | tf_op jit(solution)/shard_map/aggregate_exchange/all_to_all | solution.py:206
  14.8 14.2 %all-to-all-done.parts_ref = bf16[16,256,128]{2,1,0:T(8,128)(2,1)S(1)} async-done(((bf16[16,256,128]{2,1,0:T(8,128)(2,1)}), bf16[16,256,128]{2,1,0:T(8,128)(2,1)S(1)}, u32[]{:S(2)}, u32[]{:S(2)}) %all-to-all-start) | async-done | bytes 1048608 | tf_op jit(solution)/shard_map/aggregate_exchange/all_to_all | solution.py:206
  29.0 0.0 copy-done.1
  29.0 0.0 copy-done.6
  29.1 0.0 copy-done.7
  29.1 0.5 partial_pre.1
  29.5 5.7 %collective-permute-start = (f32[16,32,256]{2,1,0:T(8,128)S(1)}, f32[16,32,256]{2,1,0:T(8,128)S(1)}, u32[]{:S(2)}, u32[]{:S(2)}) collective-permute-start(f32[16,32,256]{2,1,0:T(8,128)S(1)} %get-tuple-element.11), channel_id=1, source_target_pairs={{0,16},{16,0},{1,17},{17,1},{2,18},{18,2},{3,19},{19,3},{4,20},{20... | collective-permute-start | bytes 1572872 | tf_op jit(solution)/shard_map/pre_sum_cores/ppermute | solution.py:223
  35.3 1.5 %collective-permute-done = f32[16,32,256]{2,1,0:T(8,128)S(1)} collective-permute-done((f32[16,32,256]{2,1,0:T(8,128)S(1)}, f32[16,32,256]{2,1,0:T(8,128)S(1)}, u32[]{:S(2)}, u32[]{:S(2)}) %collective-permute-start) | collective-permute-done | bytes 524320 | tf_op jit(solution)/shard_map/pre_sum_cores/ppermute | solution.py:223
  36.8 0.8 add_convert_fusion
  37.6 15.5 %all-to-all-start.1 = ((bf16[16,32,256]{2,1,0:T(8,128)(2,1)}), bf16[16,32,256]{2,1,0:T(8,128)(2,1)S(1)}, u32[]{:S(2)}, u32[]{:S(2)}) async-start(bf16[16,32,256]{2,1,0:T(8,128)(2,1)} %add_convert_fusion), calls=%async_computation.1 | async-start | bytes 524288 | tf_op jit(solution)/shard_map/pre_sum_depth/all_to_all | solution.py:225
  53.1 14.0 %all-to-all-done.1.parts_ref = bf16[16,32,256]{2,1,0:T(8,128)(2,1)S(1)} async-done(((bf16[16,32,256]{2,1,0:T(8,128)(2,1)}), bf16[16,32,256]{2,1,0:T(8,128)(2,1)S(1)}, u32[]{:S(2)}, u32[]{:S(2)}) %all-to-all-start.1) | async-done | bytes 262176 | tf_op jit(solution)/shard_map/pre_sum_depth/all_to_all | solution.py:225
  67.1 0.0 copy-start.11
  67.1 0.7 copy-done.11
  67.8 1.6 %pre_sum_depth.1 = bf16[32,256]{1,0:T(8,128)(2,1)} custom-call(bf16[16,32,256]{2,1,0:T(8,128)(2,1)} %copy-done.11), custom_call_target="tpu_custom_call" | custom-call | tf_op jit(solution)/shard_map/pre_sum_depth/pallas_call | solution.py:226
  69.4 0.0 copy-start.2
  69.4 0.0 copy-start.3
  69.4 0.0 copy-start.4
  69.4 0.0 copy-start.8
  69.4 37.7 %all_gather.3.pre_ref = bf16[1024,256]{1,0:T(8,128)(2,1)S(1)} all-gather(bf16[32,256]{1,0:T(8,128)(2,1)} %pre_sum_depth.1), channel_id=1, replica_groups=mesh['z'=16,'c'=2,'x'=4,'y'=4] {'z','c'}, dimensions={0}, use_global_device_ids=true | all-gather | bytes 540672 | tf_op jit(solution)/shard_map/pre_gather/all_gather | solution.py:233
  107.1 0.0 copy-start.10
  107.1 0.0 copy-done.2
  107.1 0.0 copy-done.3
  107.1 0.0 copy-done.4
  107.1 0.0 copy-done.8
  107.1 0.7 copy-done.10
  107.7 3.3 %step.1 = (bf16[256,256]{1,0:T(8,128)(2,1)}, bf16[16,96,256]{2,1,0:T(8,128)(2,1)S(1)}) custom-call(s32[1]{0:T(128)} %bitcast.feat_ref, bf16[1024,256]{1,0:T(8,128)(2,1)S(1)} %all_gather.3.pre_ref, s32[10,256]{1,0:T(8,128)S(1)} %bitcast.11, s32[1,256]{1,0:T(1,128)S(1)} %bitcast.13, bf16[256,256]{1,0:T(8,128)(2,1)S(1)} %copy-done.2, ...), custom_call_target="tpu_custom_call" | custom-call | tf_op jit(solution)/shard_map/step/pallas_call | solution.py:237
  111.1 16.9 %all_to_all.15.parts_ref = bf16[16,96,256]{2,1,0:T(8,128)(2,1)} all-to-all(bf16[16,96,256]{2,1,0:T(8,128)(2,1)S(1)} %get-tuple-element.14), channel_id=1, replica_groups=mesh['z'=16,'c'=2,'x'=4,'y'=4] {'x','y'}, dimensions={0} | all-to-all | bytes 1572864 | tf_op jit(solution)/shard_map/grad_sum/all_to_all | solution.py:262
  127.9 1.8 %grad_sum.1 = (f32[2,32,256]{2,1,0:T(8,128)}, f32[2,8,256]{2,1,0:T(8,128)}) custom-call(bf16[16,96,256]{2,1,0:T(8,128)(2,1)} %all_to_all.15.parts_ref), custom_call_target="tpu_custom_call" | custom-call | tf_op jit(solution)/shard_map/grad_sum/pallas_call | solution.py:263
Async XLA Ops:
  1.3 0.7 copy-start.9
  2.0 1.2 copy-start
  3.2 0.8 copy-start.5
  7.0 22.0 %copy-start.1 = (bf16[1024,32]{0,1:T(8,128)(2,1)S(1)}, bf16[1024,32]{0,1:T(8,128)(2,1)}, u32[]{:S(2)}) copy-start(bf16[1024,32]{0,1:T(8,128)(2,1)} %param.13) | copy-start | bytes 196612
  7.1 22.0 %copy-start.6 = (bf16[32,256]{1,0:T(8,128)(2,1)S(1)}, bf16[32,256]{1,0:T(8,128)(2,1)}, u32[]{:S(2)}) copy-start(bf16[32,256]{1,0:T(8,128)(2,1)} %self_ref.2) | copy-start | bytes 49156
  7.1 22.0 %copy-start.7 = (bf16[32,256]{1,0:T(8,128)(2,1)S(1)}, bf16[32,256]{1,0:T(8,128)(2,1)}, u32[]{:S(2)}) copy-start(bf16[32,256]{1,0:T(8,128)(2,1)} %neigh_ref.2) | copy-start | bytes 49156
  7.1 22.0 %all-to-all-start = ((bf16[16,256,128]{2,1,0:T(8,128)(2,1)}), bf16[16,256,128]{2,1,0:T(8,128)(2,1)S(1)}, u32[]{:S(2)}, u32[]{:S(2)}) async-start(bf16[16,256,128]{2,1,0:T(8,128)(2,1)} %bitcast.4), calls=%async_computation | async-start | bytes 2097152 | tf_op jit(solution)/shard_map/aggregate_exchange/all_to_all | solution.py:206
  29.5 7.3 %collective-permute-start = (f32[16,32,256]{2,1,0:T(8,128)S(1)}, f32[16,32,256]{2,1,0:T(8,128)S(1)}, u32[]{:S(2)}, u32[]{:S(2)}) collective-permute-start(f32[16,32,256]{2,1,0:T(8,128)S(1)} %get-tuple-element.11), channel_id=1, source_target_pairs={{0,16},{16,0},{1,17},{17,1},{2,18},{18,2},{3,19},{19,3},{4,20},{20... | collective-permute-start | bytes 1572872 | tf_op jit(solution)/shard_map/pre_sum_cores/ppermute | solution.py:223
  37.6 29.5 %all-to-all-start.1 = ((bf16[16,32,256]{2,1,0:T(8,128)(2,1)}), bf16[16,32,256]{2,1,0:T(8,128)(2,1)S(1)}, u32[]{:S(2)}, u32[]{:S(2)}) async-start(bf16[16,32,256]{2,1,0:T(8,128)(2,1)} %add_convert_fusion), calls=%async_computation.1 | async-start | bytes 524288 | tf_op jit(solution)/shard_map/pre_sum_depth/all_to_all | solution.py:225
  67.1 0.7 copy-start.11
  69.4 37.7 %copy-start.2 = (bf16[256,256]{1,0:T(8,128)(2,1)S(1)}, bf16[256,256]{1,0:T(8,128)(2,1)}, u32[]{:S(2)}) copy-start(bf16[256,256]{1,0:T(8,128)(2,1)} %self_ref.3) | copy-start | bytes 393220
  69.4 37.7 %copy-start.3 = (bf16[256,256]{1,0:T(8,128)(2,1)S(1)}, bf16[256,256]{1,0:T(8,128)(2,1)}, u32[]{:S(2)}) copy-start(bf16[256,256]{1,0:T(8,128)(2,1)} %neigh_ref.3) | copy-start | bytes 393220
  69.4 37.7 %copy-start.4 = (bf16[256,256]{1,0:T(8,128)(2,1)S(1)}, bf16[256,256]{1,0:T(8,128)(2,1)}, u32[]{:S(2)}) copy-start(bf16[256,256]{1,0:T(8,128)(2,1)} %cotangent_ref.1) | copy-start | bytes 393220
  69.4 37.7 %copy-start.8 = (s32[256,10]{0,1:T(8,128)S(1)}, s32[256,10]{0,1:T(8,128)}, u32[]{:S(2)}) copy-start(s32[256,10]{0,1:T(8,128)} %param.21) | copy-start | bytes 30724
  107.1 0.7 copy-start.10

commit v3 on v2

--- a/solution.py
+++ b/solution.py
@@ -9,8 +9,8 @@
 BF16 = jnp.bfloat16
 F32 = jnp.float32
 NODE = ("x", "y")
-DEPTH = ("z",)
-FEAT = ("z", "c")
+FEAT = ("zh", "zl", "c")
+FAN = 10
 MIB = 1 << 20
 
 VMEM = pl.BlockSpec(memory_space=pltpu.VMEM)
@@ -79,7 +79,8 @@
     total = parts_ref[0].astype(F32)
     for position in range(1, parts_ref.shape[0]):
         total += parts_ref[position].astype(F32)
-    out_ref[...] = total.astype(out_ref.dtype)
+    for position in range(out_ref.shape[0]):
+        out_ref[position] = total.astype(out_ref.dtype)
 
 
 def grads_kernel(parts_ref, one_ref, two_ref):
@@ -94,11 +95,21 @@
     two_ref[1] = two[part_rows:]
 
 
+def picks_kernel(neighbors_ref, seeds_ref, picks_ref):
+    fanout, seeds = neighbors_ref.shape
+    rows = picks_ref.shape[0]
+    row_of = lax.broadcasted_iota(jnp.int32, (rows, seeds), 0)
+    counts = jnp.zeros((rows, seeds), F32)
+    for entry in range(fanout):
+        counts += (row_of == neighbors_ref[entry : entry + 1, :]).astype(F32)
+    picks_ref[:, :seeds] = counts.astype(BF16)
+    picks_ref[:, seeds:] = (row_of == seeds_ref[...]).astype(F32).astype(BF16)
+
+
 def step_kernel(
     feat_ref,
     pre_ref,
-    neighbors_ref,
-    seeds_ref,
+    picks_ref,
     self_ref,
     neigh_ref,
     cotangent_ref,
@@ -106,24 +117,15 @@
     agg_ref,
     output_ref,
     grads_ref,
-    picks,
     scratch,
 ):
-    rows = pre_ref.shape[0]
-    fanout, seeds = neighbors_ref.shape
+    seeds = cotangent_ref.shape[0]
     columns = targets_ref.shape[0]
-    row_of = lax.broadcasted_iota(jnp.int32, (rows, seeds), 0)
-    counts = jnp.zeros((rows, seeds), F32)
-    for entry in range(fanout):
-        counts += (row_of == neighbors_ref[entry : entry + 1, :]).astype(F32)
-    picks[:, :seeds] = counts.astype(BF16)
-    picks[:, seeds:] = (row_of == seeds_ref[...]).astype(F32).astype(BF16)
-
     pre_one = pre_ref[...].astype(F32)
     sigmoid = jax.nn.sigmoid(pre_one)
     hidden = (pre_one * sigmoid).astype(BF16)
-    gathered = contract(picks[...], hidden, 0, 0)
-    nbr_mean = (gathered[:seeds] / fanout).astype(BF16)
+    gathered = contract(picks_ref[...], hidden, 0, 0)
+    nbr_mean = (gathered[:seeds] / FAN).astype(BF16)
     own = gathered[seeds:].astype(BF16)
     pre_two = contract(own, self_ref[...], 1, 0) + contract(nbr_mean, neigh_ref[...], 1, 0)
     gate = jax.nn.sigmoid(pre_two)
@@ -136,12 +138,12 @@
     scratch[1] = contract(nbr_mean, slope_two, 0, 0)
 
     back = jnp.concatenate(
-        [contract(slope_two, neigh_ref[...], 1, 1) / fanout, contract(slope_two, self_ref[...], 1, 1)],
+        [contract(slope_two, neigh_ref[...], 1, 1) / FAN, contract(slope_two, self_ref[...], 1, 1)],
         axis=0,
     )
     back_high = back.astype(BF16)
     back_low = (back - back_high.astype(F32)).astype(BF16)
-    chosen = picks[...]
+    chosen = picks_ref[...]
     back_hidden = contract(chosen, back_high, 1, 0) + contract(chosen, back_low, 1, 0)
     slope_one = (back_hidden * (sigmoid * (1.0 + pre_one * (1.0 - sigmoid)))).astype(BF16)
     inputs = jnp.concatenate([targets_ref[...], agg_ref[...]], axis=0)
@@ -156,6 +158,16 @@
     every = jnp.concatenate([grad_one, two_high, two_low], axis=0)
     for position in range(grads_ref.shape[0]):
         grads_ref[position] = every
+
+
+def sum_pieces(pieces, copies):
+    return pl.pallas_call(
+        sum_kernel,
+        out_shape=jax.ShapeDtypeStruct((copies,) + pieces.shape[1:], BF16),
+        in_specs=[VMEM],
+        out_specs=VMEM,
+        compiler_params=pltpu.CompilerParams(vmem_limit_bytes=8 * MIB),
+    )(pieces)
 
 
 def per_device(
@@ -176,11 +188,12 @@
     tgt_rows = target_feats.shape[0]
     slots, block, _ = tile_values.shape
     hsize = self_weight2.shape[0]
+    seed_count = seed_index.shape[0]
     owners = lax.axis_size(NODE)
     feat_count = lax.axis_size(FEAT)
     part_rows = hsize // feat_count
-    deep = lax.axis_size(DEPTH)
-    span = tgt_rows // feat_count
+    near, far = lax.axis_size("zl"), lax.axis_size("zh")
+    span = tgt_rows // near // 2
     all_blocks = tgt_rows * owners // block
     targets = target_feats.T
     core = lax.axis_index("c").reshape(1)
@@ -200,7 +213,7 @@
                 pltpu.SemaphoreType.DMA((4,)),
                 pltpu.SemaphoreType.DMA,
             ],
-            compiler_params=pltpu.CompilerParams(vmem_limit_bytes=16 * MIB),
+            compiler_params=pltpu.CompilerParams(vmem_limit_bytes=56 * MIB),
         )(tile_count, tile_index.T, tile_values, features.T)
     with jax.named_scope("aggregate_exchange"):
         parts = lax.all_to_all(
@@ -211,26 +224,35 @@
             partial_kernel,
             out_shape=[
                 jax.ShapeDtypeStruct((columns, tgt_rows), BF16),
-                jax.ShapeDtypeStruct((deep, span, hsize), F32),
-                jax.ShapeDtypeStruct((deep, span, hsize), F32),
+                jax.ShapeDtypeStruct((near, span, hsize), F32),
+                jax.ShapeDtypeStruct((near, span, hsize), F32),
             ],
             in_specs=[SMEM] + [VMEM] * 4,
             out_specs=[VMEM] * 3,
-            scratch_shapes=[pltpu.VMEM((2, deep, span, hsize), F32)],
+            scratch_shapes=[pltpu.VMEM((2, near, span, hsize), F32)],
             compiler_params=pltpu.CompilerParams(vmem_limit_bytes=16 * MIB),
         )(core, parts, targets, self_weight1, neigh_weight1)
     with jax.named_scope("pre_sum_cores"):
         pair = (keep + lax.ppermute(send, "c", [(0, 1), (1, 0)])).astype(BF16)
-    with jax.named_scope("pre_sum_depth"):
-        pieces = lax.all_to_all(pair, DEPTH, 0, 0, tiled=True)
-        pre_rows = pl.pallas_call(
-            sum_kernel,
-            out_shape=jax.ShapeDtypeStruct((span, hsize), BF16),
-            in_specs=[VMEM],
+    with jax.named_scope("pre_sum_near"):
+        pieces = lax.all_to_all(pair, "zl", 0, 0, tiled=True)
+        copies = sum_pieces(pieces, far)
+    with jax.named_scope("pre_sum_far"):
+        copies = lax.all_to_all(copies, "zh", 0, 0, tiled=True)
+        pre_rows = sum_pieces(copies, 1)[0]
+    with jax.named_scope("pre_gather"):
+        pre_one = lax.all_gather(pre_rows, ("zl", "c"), tiled=True)
+    with jax.named_scope("picks"):
+        picks = pl.pallas_call(
+            picks_kernel,
+            out_shape=jax.ShapeDtypeStruct((tgt_rows, 2 * seed_count), BF16),
+            in_specs=[VMEM] * 2,
             out_specs=VMEM,
-        )(pieces)
-    with jax.named_scope("pre_gather"):
-        pre_one = lax.all_gather(pre_rows, FEAT, tiled=True)
+            cost_estimate=pl.CostEstimate(
+                flops=20 * tgt_rows * seed_count, bytes_accessed=4 * tgt_rows * seed_count, transcendentals=0
+            ),
+            compiler_params=pltpu.CompilerParams(vmem_limit_bytes=16 * MIB),
+        )(neighbors.T, seed_index.reshape(1, -1))
 
     grad_rows = 2 * columns + 4 * part_rows
     with jax.named_scope("step"):
@@ -240,18 +262,14 @@
                 jax.ShapeDtypeStruct(cotangent.shape, BF16),
                 jax.ShapeDtypeStruct((owners, grad_rows, hsize), BF16),
             ],
-            in_specs=[SMEM] + [VMEM] * 8,
+            in_specs=[SMEM] + [VMEM] * 7,
             out_specs=[VMEM] * 2,
-            scratch_shapes=[
-                pltpu.VMEM((tgt_rows, 2 * neighbors.shape[0]), BF16),
-                pltpu.VMEM((2, hsize, hsize), F32),
-            ],
-            compiler_params=pltpu.CompilerParams(vmem_limit_bytes=32 * MIB),
+            scratch_shapes=[pltpu.VMEM((2, hsize, hsize), F32)],
+            compiler_params=pltpu.CompilerParams(vmem_limit_bytes=24 * MIB),
         )(
             feat,
             pre_one,
-            neighbors.T,
-            seed_index.reshape(1, -1),
+            picks,
             self_weight2,
             neigh_weight2,
             cotangent,
@@ -268,12 +286,13 @@
             ],
             in_specs=[VMEM],
             out_specs=[VMEM] * 2,
+            compiler_params=pltpu.CompilerParams(vmem_limit_bytes=8 * MIB),
         )(grads)
     return (output, grad_one, grad_two)
 
 
 def solution(mesh):
-    fine = Mesh(mesh.devices.reshape(16, 2, 4, 4), FEAT + NODE)
+    fine = Mesh(mesh.devices.reshape(4, 4, 2, 4, 4), FEAT + NODE)
     placed = (
         P(NODE, FEAT),
         P(NODE, FEAT),

time: 130 us -> 118 us (0.908)
  starting transfers between devices: 29 us -> 25.6 us
  local copies, waits for them, and re-layouts: 4.11 us -> 0.76 us
  waiting for transfers between devices: 29.7 us -> 27 us
  blocking collectives: 54.5 us -> 52.9 us
    all_gather x1, blocking collectives: 37.7 us -> 23.6 us  [per_device(): pre_one = lax.all_gather(pre_rows, ('zl', 'c'), tiled=True)]
    all_to_all x0 -> x1, blocking collectives: none -> 13 us  [per_device(): pieces = lax.all_to_all(pair, 'zl', 0, 0, tiled=True)]
    all_to_all x1, starting transfers between devices: 15.5 us -> 12.1 us  [per_device(): copies = lax.all_to_all(copies, 'zh', 0, 0, tiled=True)]
    unnamed x24 -> x16, local copies, waits for them, and re-layouts: 4.11 us -> 0.76 us
    all_to_all x1, waiting for transfers between devices: 14 us -> 11.2 us  [per_device(): copies = lax.all_to_all(copies, 'zh', 0, 0, tiled=True)]
  transfers between devices with their start and end apart: 3 -> 3, of which waited for: 3 -> 3; matrix products, arithmetic and copies ran while one was open for 0% -> 0% of each run, Pallas kernels for 0% -> 1%
where the time goes in v3:
time: 118 us; the launch traced here: 117 us
  blocking collectives  52.9 us (45%)
  waiting for transfers between devices  27 us (23%)
  starting transfers between devices  25.6 us (22%)
  Pallas kernels  9.63 us (8%)
  between operations  1.39 us (1%)
    all_gather x1, blocking collectives, per_device(): pre_one = lax.all_gather(pre_rows, ('zl', 'c'), tiled=True)  23.6 us
    all_to_all x1, blocking collectives, per_device(): grads = lax.all_to_all(grads, NODE, 0, 0, tiled=True)  16.3 us
    all_to_all x1, waiting for transfers between devices, per_device(): lax.all_to_all(aggregate.reshape(owners, tgt_rows // block * columns, blo...  14.2 us
    all_to_all x1, blocking collectives, per_device(): pieces = lax.all_to_all(pair, 'zl', 0, 0, tiled=True)  13 us
    all_to_all x1, starting transfers between devices, per_device(): copies = lax.all_to_all(copies, 'zh', 0, 0, tiled=True)  12.1 us
    all_to_all x1, waiting for transfers between devices, per_device(): copies = lax.all_to_all(copies, 'zh', 0, 0, tiled=True)  11.2 us
    all_to_all x1, starting transfers between devices, per_device(): lax.all_to_all(aggregate.reshape(owners, tgt_rows // block * columns, blo...  7.73 us
    ppermute x1, starting transfers between devices, per_device(): pair = (keep + lax.ppermute(send, 'c', [(0, 1), (1, 0)])).astype(BF16)  5.73 us
  transfers between devices with their start and end apart: 3, of which 3 were waited for; matrix products, arithmetic and copies ran while one was open for 0% of the time, Pallas kernels for 1%

profile of v3, /device:TPU:1, one launch (start us, length us, event | category | flops | bytes accessed | tf_op | source)
XLA Modules:
  0.0 117.3 jit_solution(16103618012355548120)
XLA Ops:
  1.3 3.9 %aggregate_tiles.1 = bf16[128,32,128]{2,1,0:T(8,128)(2,1)} custom-call(s32[1]{0:T(128)S(6)} %copy.15.count_ref, s32[2,32]{1,0:T(2,128)} %bitcast.15, bf16[32,128,128]{2,1,0:T(8,128)(2,1)} %tiles_ref.1, bf16[32,1024]{1,0:T(8,128)(2,1)} %bitcast.14), custom_call_target="tpu_custom_call" | custom-call | tf_op jit(solution)/shard_map/aggregate_tiles/pallas_call | solution.py:203
  5.2 0.0 copy-start
  5.2 0.0 copy-start.4
  5.2 0.0 copy-start.5
  5.3 7.7 %all-to-all-start = ((bf16[16,256,128]{2,1,0:T(8,128)(2,1)}), bf16[16,256,128]{2,1,0:T(8,128)(2,1)S(1)}, u32[]{:S(2)}, u32[]{:S(2)}) async-start(bf16[16,256,128]{2,1,0:T(8,128)(2,1)} %bitcast.4), calls=%async_computation | async-start | bytes 2097152 | tf_op jit(solution)/shard_map/aggregate_exchange/all_to_all | solution.py:219
  13.0 14.2 %all-to-all-done.parts_ref = bf16[16,256,128]{2,1,0:T(8,128)(2,1)S(1)} async-done(((bf16[16,256,128]{2,1,0:T(8,128)(2,1)}), bf16[16,256,128]{2,1,0:T(8,128)(2,1)S(1)}, u32[]{:S(2)}, u32[]{:S(2)}) %all-to-all-start) | async-done | bytes 1048608 | tf_op jit(solution)/shard_map/aggregate_exchange/all_to_all | solution.py:219
  27.2 0.0 copy-done
  27.2 0.0 copy-done.4
  27.2 0.0 copy-done.5
  27.2 0.5 partial_pre.1
  27.7 5.7 %collective-permute-start = (f32[4,128,256]{2,1,0:T(8,128)S(1)}, f32[4,128,256]{2,1,0:T(8,128)S(1)}, u32[]{:S(2)}, u32[]{:S(2)}) collective-permute-start(f32[4,128,256]{2,1,0:T(8,128)S(1)} %get-tuple-element.11), channel_id=1, source_target_pairs={{0,16},{16,0},{1,17},{17,1},{2,18},{18,2},{3,19},{19,3},{4,20},{20... | collective-permute-start | bytes 1572872 | tf_op jit(solution)/shard_map/pre_sum_cores/ppermute | solution.py:236
  33.4 1.5 %collective-permute-done = f32[4,128,256]{2,1,0:T(8,128)S(1)} collective-permute-done((f32[4,128,256]{2,1,0:T(8,128)S(1)}, f32[4,128,256]{2,1,0:T(8,128)S(1)}, u32[]{:S(2)}, u32[]{:S(2)}) %collective-permute-start) | collective-permute-done | bytes 524320 | tf_op jit(solution)/shard_map/pre_sum_cores/ppermute | solution.py:236
  35.0 0.1 add_convert_fusion
  35.0 13.0 %all_to_all.20.parts_ref = bf16[4,128,256]{2,1,0:T(8,128)(2,1)S(1)} all-to-all(bf16[4,128,256]{2,1,0:T(8,128)(2,1)S(1)} %add_convert_fusion), channel_id=1, replica_groups=mesh['zh'=4,'zl'=4,'c'=2,'x'=4,'y'=4] {'zl'}, dimensions={0} | all-to-all | bytes 524288 | tf_op jit(solution)/shard_map/pre_sum_near/all_to_all | solution.py:238
  48.1 0.7 pre_sum_near.1
  48.8 12.1 %all-to-all-start.2 = ((bf16[4,128,256]{2,1,0:T(8,128)(2,1)}), bf16[4,128,256]{2,1,0:T(8,128)(2,1)S(1)}, u32[]{:S(2)}, u32[]{:S(2)}) async-start(bf16[4,128,256]{2,1,0:T(8,128)(2,1)} %pre_sum_near.1), calls=%async_computation.2 | async-start | bytes 524288 | tf_op jit(solution)/shard_map/pre_sum_far/all_to_all | solution.py:241
  60.9 0.0 copy-start.6
  60.9 0.0 copy-start.7
  60.9 0.7 copy-done.6
  61.6 0.0 copy-done.7
  61.6 1.1 picks.1.picks_ref
  62.8 11.2 %all-to-all-done.2.parts_ref = bf16[4,128,256]{2,1,0:T(8,128)(2,1)S(1)} async-done(((bf16[4,128,256]{2,1,0:T(8,128)(2,1)}), bf16[4,128,256]{2,1,0:T(8,128)(2,1)S(1)}, u32[]{:S(2)}, u32[]{:S(2)}) %all-to-all-start.2) | async-done | bytes 262176 | tf_op jit(solution)/shard_map/pre_sum_far/all_to_all | solution.py:241
  74.0 0.0 copy-start.1
  74.0 0.0 copy-start.2
  74.1 0.0 copy-start.3
  74.1 23.6 %all-gather = bf16[1,1024,256]{2,1,0:T(8,128)(2,1)S(1)} all-gather(bf16[1,128,256]{2,1,0:T(8,128)(2,1)S(1)} %pre_sum_far.1), channel_id=2, replica_groups=mesh['zh'=4,'zl'=4,'c'=2,'x'=4,'y'=4] {'zl','c'}, dimensions={1}, use_global_device_ids=true | all-gather | bytes 589824 | tf_op jit(solution)/shard_map/pre_gather/all_gather | solution.py:244
  97.7 0.0 copy-done.1
  97.7 0.0 copy-done.2
  97.7 0.0 copy-done.3
  97.7 2.6 %step.1 = (bf16[256,256]{1,0:T(8,128)(2,1)}, bf16[16,96,256]{2,1,0:T(8,128)(2,1)S(1)}) custom-call(s32[1]{0:T(128)} %bitcast.feat_ref, bf16[1024,256]{1,0:T(8,128)(2,1)S(1)} %bitcast.9, bf16[1024,512]{1,0:T(8,128)(2,1)S(1)} %picks.1.picks_ref, bf16[256,256]{1,0:T(8,128)(2,1)S(1)} %copy-done.1, bf16[256,256]{1,0:T(8,128)(2,1)S(1)} %copy-done.2, ...), custom_call_target="tpu_custom_call" | custom-call | tf_op jit(solution)/shard_map/step/pallas_call | solution.py:259
  100.3 16.3 %all_to_all.21.parts_ref = bf16[16,96,256]{2,1,0:T(8,128)(2,1)S(1)} all-to-all(bf16[16,96,256]{2,1,0:T(8,128)(2,1)S(1)} %get-tuple-element.14), channel_id=1, replica_groups=mesh['zh'=4,'zl'=4,'c'=2,'x'=4,'y'=4] {'x','y'}, dimensions={0} | all-to-all | bytes 1572864 | tf_op jit(solution)/shard_map/grad_sum/all_to_all | solution.py:280
  116.6 0.7 grad_sum.1
  (1 shorter events, 0.0 us)
Async XLA Ops:
  5.2 22.0 %copy-start = (bf16[1024,32]{0,1:T(8,128)(2,1)S(1)}, bf16[1024,32]{0,1:T(8,128)(2,1)}, u32[]{:S(2)}) copy-start(bf16[1024,32]{0,1:T(8,128)(2,1)} %param.13) | copy-start | bytes 196612
  5.2 22.0 %copy-start.4 = (bf16[32,256]{1,0:T(8,128)(2,1)S(1)}, bf16[32,256]{1,0:T(8,128)(2,1)}, u32[]{:S(2)}) copy-start(bf16[32,256]{1,0:T(8,128)(2,1)} %self_ref.2) | copy-start | bytes 49156
  5.2 22.0 %copy-start.5 = (bf16[32,256]{1,0:T(8,128)(2,1)S(1)}, bf16[32,256]{1,0:T(8,128)(2,1)}, u32[]{:S(2)}) copy-start(bf16[32,256]{1,0:T(8,128)(2,1)} %neigh_ref.2) | copy-start | bytes 49156
  5.3 22.0 %all-to-all-start = ((bf16[16,256,128]{2,1,0:T(8,128)(2,1)}), bf16[16,256,128]{2,1,0:T(8,128)(2,1)S(1)}, u32[]{:S(2)}, u32[]{:S(2)}) async-start(bf16[16,256,128]{2,1,0:T(8,128)(2,1)} %bitcast.4), calls=%async_computation | async-start | bytes 2097152 | tf_op jit(solution)/shard_map/aggregate_exchange/all_to_all | solution.py:219
  27.7 7.3 %collective-permute-start = (f32[4,128,256]{2,1,0:T(8,128)S(1)}, f32[4,128,256]{2,1,0:T(8,128)S(1)}, u32[]{:S(2)}, u32[]{:S(2)}) collective-permute-start(f32[4,128,256]{2,1,0:T(8,128)S(1)} %get-tuple-element.11), channel_id=1, source_target_pairs={{0,16},{16,0},{1,17},{17,1},{2,18},{18,2},{3,19},{19,3},{4,20},{20... | collective-permute-start | bytes 1572872 | tf_op jit(solution)/shard_map/pre_sum_cores/ppermute | solution.py:236
  48.8 25.2 %all-to-all-start.2 = ((bf16[4,128,256]{2,1,0:T(8,128)(2,1)}), bf16[4,128,256]{2,1,0:T(8,128)(2,1)S(1)}, u32[]{:S(2)}, u32[]{:S(2)}) async-start(bf16[4,128,256]{2,1,0:T(8,128)(2,1)} %pre_sum_near.1), calls=%async_computation.2 | async-start | bytes 524288 | tf_op jit(solution)/shard_map/pre_sum_far/all_to_all | solution.py:241
  60.9 0.7 copy-start.6
  60.9 0.7 copy-start.7
  74.0 23.6 %copy-start.1 = (bf16[256,256]{1,0:T(8,128)(2,1)S(1)}, bf16[256,256]{1,0:T(8,128)(2,1)}, u32[]{:S(2)}) copy-start(bf16[256,256]{1,0:T(8,128)(2,1)} %self_ref.3) | copy-start | bytes 393220
  74.0 23.6 %copy-start.2 = (bf16[256,256]{1,0:T(8,128)(2,1)S(1)}, bf16[256,256]{1,0:T(8,128)(2,1)}, u32[]{:S(2)}) copy-start(bf16[256,256]{1,0:T(8,128)(2,1)} %neigh_ref.3) | copy-start | bytes 393220
  74.1 23.6 %copy-start.3 = (bf16[256,256]{1,0:T(8,128)(2,1)S(1)}, bf16[256,256]{1,0:T(8,128)(2,1)}, u32[]{:S(2)}) copy-start(bf16[256,256]{1,0:T(8,128)(2,1)} %cotangent_ref.1) | copy-start | bytes 393220

commit v4 on v3

v4 whole, which is shorter than its diff:
```python
import jax
import jax.numpy as jnp
from jax import lax
from jax.experimental import pallas as pl
from jax.experimental.pallas import tpu as pltpu
from jax.sharding import Mesh
from jax.sharding import PartitionSpec as P

BF16 = jnp.bfloat16
F32 = jnp.float32
NODE = ("x", "y")
FEAT = ("zh", "zl", "c")
FAN = 10
MIB = 1 << 20

VMEM = pl.BlockSpec(memory_space=pltpu.VMEM)
HBM = pl.BlockSpec(memory_space=pltpu.HBM)
ANY = pl.BlockSpec(memory_space=pl.ANY)
SMEM = pl.BlockSpec(memory_space=pltpu.SMEM)


def contract(left, right, left_dim, right_dim):
    return lax.dot_general(
        left, right, (((left_dim,), (right_dim,)), ((), ())), preferred_element_type=F32
    )


def aggregate_kernel(
    count_ref, index_ref, tiles_ref, feats_ref, out_ref, tiles, feats, sources, products, total, tile_sem, feat_sem
):
    slots, block, _ = tiles.shape
    group = slots // tile_sem.shape[0]
    feat_copy = pltpu.make_async_copy(feats_ref, feats, feat_sem)
    feat_copy.start()
    tile_copies = []
    for position in range(tile_sem.shape[0]):
        span = pl.ds(position * group, group)
        copy = pltpu.make_async_copy(tiles_ref.at[span], tiles.at[span], tile_sem.at[position])
        copy.start()
        tile_copies.append(copy)
    total[...] = jnp.zeros_like(total)
    feat_copy.wait()
    for position in range(sources.shape[0]):
        sources[position] = feats[:, position * block : (position + 1) * block]
    live_tiles = count_ref[0]
    for slot in range(slots):
        if slot % group == 0:
            tile_copies[slot // group].wait()
        in_use = (slot < live_tiles).astype(F32)
        products[slot] = contract(sources[index_ref[1, slot]], tiles[slot], 1, 1) * in_use
    for slot in range(slots):
        target = index_ref[0, slot]
        total[target] += products[slot]
    out_ref[...] = total[...].astype(BF16)


def split_blocks(core, halves, mine_ref, other_ref):
    block = halves.shape[3]
    for position in range(halves.shape[0]):
        span = slice(position * block, (position + 1) * block)
        mine_ref[:, span] = halves[position, core]
        other_ref[:, span] = halves[position, 1 - core]


def pack_kernel(core_ref, targets_ref, self_ref, neigh_ref, mine_ref, pack_ref, halves):
    columns = targets_ref.shape[0]
    near, _, _, block = halves.shape
    for position in range(2 * near):
        halves[position // 2, position % 2] = targets_ref[:, position * block : (position + 1) * block]
    split_blocks(core_ref[0], halves, mine_ref, pack_ref.at[:columns])
    hsize = self_ref.shape[1]
    pack_ref[columns:, :hsize] = self_ref[...]
    pack_ref[columns:, hsize:] = neigh_ref[...]


def owned_kernel(core_ref, parts_ref, mine_ref, other_ref, halves):
    near, _, columns, _ = halves.shape
    for position in range(2 * near):
        span = slice(position * columns, (position + 1) * columns)
        block = parts_ref[0, span].astype(F32)
        for source in range(1, parts_ref.shape[0]):
            block += parts_ref[source, span].astype(F32)
        halves[position // 2, position % 2] = block.astype(BF16)
    split_blocks(core_ref[0], halves, mine_ref, other_ref)


def partial_kernel(targets_ref, pack_ref, mine_ref, arrived_ref, self_ref, neigh_ref, out_ref):
    columns, hsize = self_ref.shape
    inputs = jnp.concatenate(
        [targets_ref[...], pack_ref[:columns], mine_ref[...], arrived_ref[...]], axis=0
    )
    weights = jnp.concatenate(
        [self_ref[...], pack_ref[columns:, :hsize], neigh_ref[...], pack_ref[columns:, hsize:]], axis=0
    )
    out_ref[...] = contract(inputs, weights, 0, 0).reshape(out_ref.shape).astype(BF16)


def near_kernel(parts_ref, out_ref):
    total = parts_ref[0].astype(F32)
    for position in range(1, parts_ref.shape[0]):
        total += parts_ref[position].astype(F32)
    out_ref[...] = total.astype(BF16)


def far_kernel(far_ref, own_ref, two_ref, one_ref, three_ref, picks_ref, out_ref, slots):
    far = far_ref[0]
    slots[far] = own_ref[...].astype(F32)
    for step, ref in ((2, two_ref), (1, one_ref), (3, three_ref)):
        slots[lax.rem(far + slots.shape[0] - step, slots.shape[0])] = ref[...].astype(F32)
    total = slots[0]
    for position in range(1, slots.shape[0]):
        total += slots[position]
    for position in range(out_ref.shape[0]):
        out_ref[position] = total.astype(BF16)


def picks_kernel(core_ref, neighbors_ref, seeds_ref, spread_ref, pick_ref):
    fanout, seeds = neighbors_ref.shape
    rows = spread_ref.shape[0]
    step = lax.broadcasted_iota(jnp.int32, (rows, seeds), 0)
    half = rows // 2
    first = step // half
    lane = step % 128
    side = jnp.where(first == 0, core_ref[0], 1 - core_ref[0])
    row_of = ((step % half) // 128) * 256 + side * 128 + lane
    counts = jnp.zeros((rows, seeds), F32)
    for entry in range(fanout):
        counts += (row_of == neighbors_ref[entry : entry + 1, :]).astype(F32)
    own = (row_of == seeds_ref[...]).astype(F32)
    spread_ref[:, :seeds] = counts.astype(BF16)
    spread_ref[:, seeds:] = own.astype(BF16)
    pick_ref[:seeds] = counts.T.astype(BF16)
    pick_ref[seeds:] = own.T.astype(BF16)


def activate(pre_ref, hidden_shape):
    pre_one = pre_ref[...].reshape(hidden_shape).astype(F32)
    sigmoid = jax.nn.sigmoid(pre_one)
    hidden = (pre_one * sigmoid).astype(BF16)
    return hidden, sigmoid * (1.0 + pre_one * (1.0 - sigmoid))


def mine_kernel(pre_ref, pick_ref, gathered_ref, slope_ref):
    half = slope_ref.shape[0]
    hidden, slope = activate(pre_ref, slope_ref.shape)
    gathered_ref[...] = contract(pick_ref[:, :half], hidden, 1, 0)
    slope_ref[...] = slope


def step_kernel(
    feat_ref,
    pre_ref,
    gathered_ref,
    slope_ref,
    pick_ref,
    spread_ref,
    self_ref,
    neigh_ref,
    cotangent_ref,
    targets_ref,
    pack_ref,
    mine_ref,
    other_ref,
    output_ref,
    grads_ref,
    gathered,
    scratch,
):
    seeds = cotangent_ref.shape[0]
    columns = targets_ref.shape[0]
    half = slope_ref.shape[0]
    hidden, slope_other = activate(pre_ref, slope_ref.shape)
    gathered[...] = contract(pick_ref[:, half:], hidden, 1, 0)
    picked = gathered_ref[...] + gathered[...]
    nbr_mean = (picked[:seeds] / FAN).astype(BF16)
    own = picked[seeds:].astype(BF16)
    pre_two = contract(own, self_ref[...], 1, 0) + contract(nbr_mean, neigh_ref[...], 1, 0)
    gate = jax.nn.sigmoid(pre_two)
    output_ref[...] = (pre_two * gate).astype(BF16)
    slope_two = (
        cotangent_ref[...].astype(F32) * (gate * (1.0 + pre_two * (1.0 - gate)))
    ).astype(BF16)

    scratch[0] = contract(own, slope_two, 0, 0)
    scratch[1] = contract(nbr_mean, slope_two, 0, 0)

    back = jnp.concatenate(
        [contract(slope_two, neigh_ref[...], 1, 1) / FAN, contract(slope_two, self_ref[...], 1, 1)],
        axis=0,
    )
    back_high = back.astype(BF16)
    back_low = (back - back_high.astype(F32)).astype(BF16)
    spread = spread_ref[...]
    back_hidden = contract(spread, back_high, 1, 0) + contract(spread, back_low, 1, 0)
    slope_one = jnp.concatenate(
        [
            (back_hidden[:half] * slope_ref[...]).astype(BF16),
            (back_hidden[half:] * slope_other).astype(BF16),
        ],
        axis=0,
    )
    inputs = jnp.concatenate(
        [
            jnp.concatenate([targets_ref[...], pack_ref[:columns]], axis=1),
            jnp.concatenate([mine_ref[...], other_ref[...]], axis=1),
        ],
        axis=0,
    )
    grad_one = contract(inputs, slope_one, 1, 0).astype(BF16)
    part_rows = (grads_ref.shape[1] - 2 * columns) // 4
    first = pl.multiple_of(feat_ref[0] * part_rows, part_rows)
    grad_two = jnp.concatenate(
        [scratch[0, pl.ds(first, part_rows), :], scratch[1, pl.ds(first, part_rows), :]], axis=0
    )
    two_high = grad_two.astype(BF16)
    two_low = (grad_two - two_high.astype(F32)).astype(BF16)
    every = jnp.concatenate([grad_one, two_high, two_low], axis=0)
    for position in range(grads_ref.shape[0]):
        grads_ref[position] = every


def grads_kernel(parts_ref, one_ref, two_ref):
    total = parts_ref[0].astype(F32)
    for position in range(1, parts_ref.shape[0]):
        total += parts_ref[position].astype(F32)
    columns, part_rows = one_ref.shape[1], two_ref.shape[1]
    one_ref[0] = total[:columns]
    one_ref[1] = total[columns : 2 * columns]
    two = total[2 * columns : 2 * columns + 2 * part_rows] + total[2 * columns + 2 * part_rows :]
    two_ref[0] = two[:part_rows]
    two_ref[1] = two[part_rows:]


def run(kernel, outs, operands, scratch=(), limit=8, flops=0, specs=None):
    shapes = [jax.ShapeDtypeStruct(shape, dtype) for shape, dtype in outs]
    moved = sum(x.size * x.dtype.itemsize for x in operands) + sum(
        x.size * x.dtype.itemsize for x in shapes
    )
    if specs is None:
        specs = [SMEM if x.dtype == jnp.int32 and x.size == 1 else VMEM for x in operands]
    results = pl.pallas_call(
        kernel,
        out_shape=shapes,
        in_specs=specs,
        out_specs=[VMEM] * len(shapes),
        scratch_shapes=list(scratch),
        cost_estimate=pl.CostEstimate(flops=flops, bytes_accessed=moved, transcendentals=0),
        compiler_params=pltpu.CompilerParams(vmem_limit_bytes=limit * MIB),
    )(*operands)
    return results[0] if len(shapes) == 1 else results


def per_device(
    features,
    target_feats,
    tile_values,
    tile_index,
    tile_count,
    self_weight1,
    neigh_weight1,
    self_weight2,
    neigh_weight2,
    neighbors,
    seed_index,
    cotangent,
):
    src_rows, columns = features.shape
    tgt_rows = target_feats.shape[0]
    slots, block, _ = tile_values.shape
    hsize = self_weight2.shape[0]
    seeds = seed_index.shape[0]
    owners = lax.axis_size(NODE)
    near, far = lax.axis_size("zl"), lax.axis_size("zh")
    part_rows = hsize // lax.axis_size(FEAT)
    all_blocks = tgt_rows * owners // block
    half = tgt_rows // 2
    span = half // near
    core = lax.axis_index("c").reshape(1)
    feat = lax.axis_index(FEAT).reshape(1)
    halves = pltpu.VMEM((near, 2, columns, block), BF16)
    swap = [(0, 1), (1, 0)]

    with jax.named_scope("aggregate_tiles"):
        aggregate = run(
            aggregate_kernel,
            [((all_blocks, columns, block), BF16)],
            (tile_count, tile_index.T, tile_values, features.T),
            [
                pltpu.VMEM(tile_values.shape, BF16),
                pltpu.VMEM((columns, src_rows), BF16),
                pltpu.VMEM((src_rows // block, columns, block), BF16),
                pltpu.VMEM((slots, columns, block), F32),
                pltpu.VMEM((all_blocks, columns, block), F32),
                pltpu.SemaphoreType.DMA((4,)),
                pltpu.SemaphoreType.DMA,
            ],
            limit=56,
            specs=[SMEM, SMEM, HBM, HBM],
        )
    with jax.named_scope("aggregate_exchange"):
        parts = lax.all_to_all(
            aggregate.reshape(owners, tgt_rows // block * columns, block), NODE, 0, 0, tiled=True
        )
    with jax.named_scope("inputs_exchange"):
        targets_mine, pack = run(
            pack_kernel,
            [((columns, half), BF16), ((2 * columns, half), BF16)],
            (core, target_feats.T, self_weight1, neigh_weight1),
            [halves],
        )
        pack_other = lax.ppermute(pack, "c", swap)
    with jax.named_scope("owned_sum"):
        agg_mine, agg_other = run(
            owned_kernel,
            [((columns, half), BF16), ((columns, half), BF16)],
            (core, parts),
            [halves],
        )
        agg_arrived = lax.ppermute(agg_other, "c", swap)
    with jax.named_scope("partial_pre"):
        pieces = run(
            partial_kernel,
            [((near, span, hsize), BF16)],
            (targets_mine, pack_other, agg_mine, agg_arrived, self_weight1, neigh_weight1),
        )
    with jax.named_scope("pre_sum_near"):
        pieces = lax.all_to_all(pieces, "zl", 0, 0, tiled=True)
        quarter = run(near_kernel, [((span, hsize), BF16)], (pieces,))
    with jax.named_scope("picks"):
        spread, pick = run(
            picks_kernel,
            [((tgt_rows, 2 * seeds), BF16), ((2 * seeds, tgt_rows), BF16)],
            (core, neighbors.T, seed_index.reshape(1, -1)),
            limit=16,
            flops=20 * tgt_rows * seeds,
        )
    with jax.named_scope("pre_sum_far"):
        arrived = [
            lax.ppermute(quarter, "zh", [(i, (i + step) % far) for i in range(far)])
            for step in (2, 1, 3)
        ]
        copies = run(
            far_kernel,
            [((near, span, hsize), BF16)],
            (lax.axis_index("zh").reshape(1), quarter, *arrived, pick),
            [pltpu.VMEM((far, span, hsize), F32)],
            specs=[SMEM] + [VMEM] * 4 + [ANY],
        )
    with jax.named_scope("pre_gather"):
        pre_mine = lax.all_to_all(copies, "zl", 0, 0, tiled=True)
        pre_other = lax.ppermute(pre_mine, "c", swap)
    with jax.named_scope("step_mine"):
        gathered, slope = run(
            mine_kernel,
            [((2 * seeds, hsize), F32), ((half, hsize), F32)],
            (pre_mine, pick),
            limit=12,
            flops=4 * seeds * half * hsize,
        )
    with jax.named_scope("step"):
        output, grads = run(
            step_kernel,
            [(cotangent.shape, BF16), ((owners, 2 * columns + 4 * part_rows, hsize), BF16)],
            (
                feat,
                pre_other,
                gathered,
                slope,
                pick,
                spread,
                self_weight2,
                neigh_weight2,
                cotangent,
                targets_mine,
                pack,
                agg_mine,
                agg_other,
            ),
            [pltpu.VMEM((2 * seeds, hsize), F32), pltpu.VMEM((2, hsize, hsize), F32)],
            limit=24,
        )
    with jax.named_scope("grad_sum"):
        grads = lax.all_to_all(grads, NODE, 0, 0, tiled=True)
        grad_one, grad_two = run(
            grads_kernel,
            [((2, columns, hsize), F32), ((2, part_rows, hsize), F32)],
            (grads,),
        )
    return (output, grad_one, grad_two)


def solution(mesh):
    fine = Mesh(mesh.devices.reshape(4, 4, 2, 4, 4), FEAT + NODE)
    placed = (
        P(NODE, FEAT),
        P(NODE, FEAT),
        P(NODE, None, None),
        P(NODE, None),
        P(NODE),
        P(FEAT, None),
        P(FEAT, None),
        P(),
        P(),
        P(NODE, None),
        P(NODE),
        P(NODE, None),
    )
    return jax.shard_map(
        per_device,
        mesh=fine,
        in_specs=placed,
        out_specs=(P(NODE, None), P(None, FEAT, None), P(None, FEAT, None)),
        check_vma=False,
    )
```

time: 118 us -> 111 us (0.941)
  starting transfers between devices: 25.6 us -> 46.4 us
  blocking collectives: 52.9 us -> 37.6 us
  waiting for transfers between devices: 27 us -> 14.5 us
    ppermute x1 -> x6, starting transfers between devices: 5.73 us -> 38.7 us  [the longest x3 21.9 us: per_device(): lax.ppermute(quarter, 'zh', [(i, (i + step) % far) for i in range(far)])]
    all_gather x1 -> x0, blocking collectives: 23.6 us -> none  [per_device(): pre_one = lax.all_gather(pre_rows, ('zl', 'c'), tiled=True)]
    all_to_all x1 -> x0, starting transfers between devices: 12.1 us -> none  [per_device(): copies = lax.all_to_all(copies, 'zh', 0, 0, tiled=True)]
    all_to_all x1 -> x0, waiting for transfers between devices: 11.2 us -> none  [per_device(): copies = lax.all_to_all(copies, 'zh', 0, 0, tiled=True)]
    all_to_all x1 -> x2, blocking collectives: 13 us -> 21.4 us  [the longest x1 13 us: per_device(): pieces = lax.all_to_all(pieces, 'zl', 0, 0, tiled=True)]
    all_to_all x1, waiting for transfers between devices: 14.2 us -> 9.29 us  [per_device(): lax.all_to_all(aggregate.reshape(owners, tgt_rows // block * columns, blo...]
    ppermute x1 -> x6, waiting for transfers between devices: 1.51 us -> 5.18 us  [the longest x3 3.69 us: per_device(): lax.ppermute(quarter, 'zh', [(i, (i + step) % far) for i in range(far)])]
    pallas_call x7 -> x10, Pallas kernels: 9.63 us -> 9.32 us  [run(): pl.pallas_call(kernel, out_shape=shapes, in_specs=specs, out_specs=[VMEM]...]
  transfers between devices with their start and end apart: 3 -> 7, of which waited for: 3 -> 4; matrix products, arithmetic and copies ran while one was open for 0% -> 0% of each run, Pallas kernels for 1% -> 2%
where the time goes in v4:
time: 111 us; the launch traced here: 110 us
  starting transfers between devices  46.4 us (42%)
  blocking collectives  37.6 us (34%)
  waiting for transfers between devices  14.5 us (13%)
  Pallas kernels  9.32 us (8%)
  between operations  1.52 us (1%)
    ppermute x3, starting transfers between devices, per_device(): lax.ppermute(quarter, 'zh', [(i, (i + step) % far) for i in range(far)])  21.9 us
    all_to_all x1, blocking collectives, per_device(): grads = lax.all_to_all(grads, NODE, 0, 0, tiled=True)  16.2 us
    all_to_all x1, blocking collectives, per_device(): pieces = lax.all_to_all(pieces, 'zl', 0, 0, tiled=True)  13 us
    pallas_call x10, Pallas kernels, run(): pl.pallas_call(kernel, out_shape=shapes, in_specs=specs, out_specs=[VMEM]...  9.32 us
    all_to_all x1, waiting for transfers between devices, per_device(): lax.all_to_all(aggregate.reshape(owners, tgt_rows // block * columns, blo...  9.29 us
    all_to_all x1, blocking collectives, per_device(): pre_mine = lax.all_to_all(copies, 'zl', 0, 0, tiled=True)  8.36 us
    all_to_all x1, starting transfers between devices, per_device(): lax.all_to_all(aggregate.reshape(owners, tgt_rows // block * columns, blo...  7.72 us
    ppermute x1, starting transfers between devices, per_device(): pre_other = lax.ppermute(pre_mine, 'c', swap)  6.19 us
  transfers between devices with their start and end apart: 7, of which 4 were waited for; matrix products, arithmetic and copies ran while one was open for 0% of the time, Pallas kernels for 2%

profile of v4, /device:TPU:1, one launch (start us, length us, event | category | flops | bytes accessed | tf_op | source)
XLA Modules:
  0.0 110.1 jit_solution(13342844693462272339)
XLA Ops:
  1.3 3.9 %aggregate_tiles.1 = bf16[128,32,128]{2,1,0:T(8,128)(2,1)} custom-call(s32[1]{0:T(128)S(6)} %copy.15.count_ref, s32[2,32]{1,0:T(2,128)} %bitcast.14, bf16[32,128,128]{2,1,0:T(8,128)(2,1)} %tiles_ref.1, bf16[32,1024]{1,0:T(8,128)(2,1)} %bitcast.13), custom_call_target="tpu_custom_call" | custom-call | bytes 2162948 | tf_op jit(solution)/shard_map/aggregate_tiles/pallas_call | solution.py:241
  5.2 0.0 copy-start.3
  5.2 0.0 copy-start.4
  5.2 0.0 copy-start.5
  5.2 7.7 %all-to-all-start = ((bf16[16,256,128]{2,1,0:T(8,128)(2,1)}), bf16[16,256,128]{2,1,0:T(8,128)(2,1)S(1)}, u32[]{:S(2)}, u32[]{:S(2)}) async-start(bf16[16,256,128]{2,1,0:T(8,128)(2,1)} %bitcast.12), calls=%async_computation | async-start | bytes 2097152 | tf_op jit(solution)/shard_map/aggregate_exchange/all_to_all | solution.py:301
  13.0 0.0 copy-done.3
  13.0 0.0 copy-done.4
  13.0 0.0 copy-done.5
  13.1 4.9 %collective-permute-start = (bf16[64,512]{1,0:T(8,128)(2,1)S(1)}, bf16[64,512]{1,0:T(8,128)(2,1)S(1)}, u32[]{:S(2)}, u32[]{:S(2)}) collective-permute-start(bf16[64,512]{1,0:T(8,128)(2,1)S(1)} %get-tuple-element.16.pack_ref), channel_id=1, source_target_pairs={{0,16},{16,0},{1,17},{17,1},{2,18},{18,2},{3,19},{19,3},{4,20},{20... | collective-permute-start | bytes 196616 | tf_op jit(solution)/shard_map/inputs_exchange/ppermute | solution.py:311
  17.9 9.3 %all-to-all-done.parts_ref = bf16[16,256,128]{2,1,0:T(8,128)(2,1)S(1)} async-done(((bf16[16,256,128]{2,1,0:T(8,128)(2,1)}), bf16[16,256,128]{2,1,0:T(8,128)(2,1)S(1)}, u32[]{:S(2)}, u32[]{:S(2)}) %all-to-all-start) | async-done | bytes 1048608 | tf_op jit(solution)/shard_map/aggregate_exchange/all_to_all | solution.py:301
  27.2 0.1 owned_sum.1
  27.4 5.7 %collective-permute-start.1 = (bf16[32,512]{1,0:T(8,128)(2,1)S(1)}, bf16[32,512]{1,0:T(8,128)(2,1)S(1)}, u32[]{:S(2)}, u32[]{:S(2)}) collective-permute-start(bf16[32,512]{1,0:T(8,128)(2,1)S(1)} %get-tuple-element.18.other_ref), channel_id=1, source_target_pairs={{0,16},{16,0},{1,17},{17,1},{2,18},{18,2},{3,19},{19,3},{4,20},{20... | collective-permute-start | bytes 98312 | tf_op jit(solution)/shard_map/owned_sum/ppermute | solution.py:319
  33.1 0.0 collective-permute-done.pack_ref
  33.1 0.8 collective-permute-done.1.arrived_ref
  33.9 0.2 partial_pre.1
  34.2 13.0 %all_to_all.20.parts_ref = bf16[4,128,256]{2,1,0:T(8,128)(2,1)S(1)} all-to-all(bf16[4,128,256]{2,1,0:T(8,128)(2,1)S(1)} %partial_pre.1), channel_id=1, replica_groups=mesh['zh'=4,'zl'=4,'c'=2,'x'=4,'y'=4] {'zl'}, dimensions={0} | all-to-all | bytes 524288 | tf_op jit(solution)/shard_map/pre_sum_near/all_to_all | solution.py:327
  47.2 0.0 copy-start.6
  47.3 9.8 %collective-permute-start.4 = (bf16[128,256]{1,0:T(8,128)(2,1)S(1)}, bf16[128,256]{1,0:T(8,128)(2,1)S(1)}, u32[]{:S(2)}, u32[]{:S(2)}) collective-permute-start(bf16[128,256]{1,0:T(8,128)(2,1)S(1)} %pre_sum_near.1.own_ref), channel_id=1, source_target_pairs={{0,384},{128,0},{256,128},{384,256},{1,385},{129,1},{257,129},{385... | collective-permute-start | bytes 196616 | tf_op jit(solution)/shard_map/pre_sum_far/ppermute | solution.py:339
  57.0 1.9 %collective-permute-start.3 = (bf16[128,256]{1,0:T(8,128)(2,1)S(1)}, bf16[128,256]{1,0:T(8,128)(2,1)S(1)}, u32[]{:S(2)}, u32[]{:S(2)}) collective-permute-start(bf16[128,256]{1,0:T(8,128)(2,1)S(1)} %pre_sum_near.1.own_ref), channel_id=1, source_target_pairs={{0,128},{128,256},{256,384},{384,0},{1,129},{129,257},{257,385},{3... | collective-permute-start | bytes 196616 | tf_op jit(solution)/shard_map/pre_sum_far/ppermute | solution.py:339
  59.0 10.3 %collective-permute-start.2 = (bf16[128,256]{1,0:T(8,128)(2,1)S(1)}, bf16[128,256]{1,0:T(8,128)(2,1)S(1)}, u32[]{:S(2)}, u32[]{:S(2)}) collective-permute-start(bf16[128,256]{1,0:T(8,128)(2,1)S(1)} %pre_sum_near.1.own_ref), channel_id=1, source_target_pairs={{0,256},{128,384},{256,0},{384,128},{1,257},{129,385},{257,1},{385... | collective-permute-start | bytes 196616 | tf_op jit(solution)/shard_map/pre_sum_far/ppermute | solution.py:339
  69.2 0.0 copy-start.7
  69.2 0.0 copy-done.6
  69.2 0.7 copy-done.7
  69.9 1.4 %picks.1 = (bf16[1024,512]{1,0:T(8,128)(2,1)S(1)}, bf16[512,1024]{1,0:T(8,128)(2,1)S(1)}) custom-call(s32[1]{0:T(128)} %bitcast.2.core_ref, s32[10,256]{1,0:T(8,128)S(1)} %bitcast.10, s32[1,256]{1,0:T(1,128)S(1)} %bitcast.11), custom_call_target="tpu_custom_call" | custom-call | flops 5242880 | bytes 2108420 | tf_op jit(solution)/shard_map/picks/pallas_call | solution.py:241
  71.3 0.0 collective-permute-done.4.three_ref
  71.4 0.0 collective-permute-done.3.one_ref
  71.4 3.7 %collective-permute-done.2.two_ref = bf16[128,256]{1,0:T(8,128)(2,1)S(1)} collective-permute-done((bf16[128,256]{1,0:T(8,128)(2,1)S(1)}, bf16[128,256]{1,0:T(8,128)(2,1)S(1)}, u32[]{:S(2)}, u32[]{:S(2)}) %collective-permute-start.2) | collective-permute-done | bytes 65568 | tf_op jit(solution)/shard_map/pre_sum_far/ppermute | solution.py:339
  75.0 0.1 pre_sum_far.1
  75.1 8.4 %all_to_all.21.pre_ref = bf16[4,128,256]{2,1,0:T(8,128)(2,1)S(1)} all-to-all(bf16[4,128,256]{2,1,0:T(8,128)(2,1)S(1)} %pre_sum_far.1), channel_id=1, replica_groups=mesh['zh'=4,'zl'=4,'c'=2,'x'=4,'y'=4] {'zl'}, dimensions={0} | all-to-all | bytes 524288 | tf_op jit(solution)/shard_map/pre_gather/all_to_all | solution.py:350
  83.5 6.2 %collective-permute-start.5 = (bf16[4,128,256]{2,1,0:T(8,128)(2,1)S(1)}, bf16[4,128,256]{2,1,0:T(8,128)(2,1)S(1)}, u32[]{:S(2)}, u32[]{:S(2)}) collective-permute-start(bf16[4,128,256]{2,1,0:T(8,128)(2,1)S(1)} %all_to_all.21.pre_ref), channel_id=1, source_target_pairs={{0,16},{16,0},{1,17},{17,1},{2,18},{18,2},{3,19},{19,3},{4,20},{20... | collective-permute-start | bytes 786440 | tf_op jit(solution)/shard_map/pre_gather/ppermute | solution.py:351
  89.7 0.0 copy-start
  89.7 0.0 copy-start.1
  89.7 0.0 copy-start.2
  89.7 0.4 step_mine.1
  90.2 0.7 collective-permute-done.5.pre_ref
  90.8 0.0 copy-done
  90.8 0.0 copy-done.1
  90.8 0.0 copy-done.2
  90.8 2.3 %step.1 = (bf16[256,256]{1,0:T(8,128)(2,1)}, bf16[16,96,256]{2,1,0:T(8,128)(2,1)S(1)}) custom-call(s32[1]{0:T(128)} %bitcast.feat_ref, bf16[4,128,256]{2,1,0:T(8,128)(2,1)S(1)} %collective-permute-done.5.pre_ref, f32[512,256]{1,0:T(8,128)S(1)} %get-tuple-element.20.gathered_ref, f32[512,256]{1,0:T(8,128)S(1)} %get-tuple-element.21.slope_ref, ...), custom_call_target="tpu_custom_call" | custom-call | bytes 4882436 | tf_op jit(solution)/shard_map/step/pallas_call | solution.py:241
  93.1 16.2 %all_to_all.22.parts_ref = bf16[16,96,256]{2,1,0:T(8,128)(2,1)S(1)} all-to-all(bf16[16,96,256]{2,1,0:T(8,128)(2,1)S(1)} %get-tuple-element.24), channel_id=1, replica_groups=mesh['zh'=4,'zl'=4,'c'=2,'x'=4,'y'=4] {'x','y'}, dimensions={0} | all-to-all | bytes 1572864 | tf_op jit(solution)/shard_map/grad_sum/all_to_all | solution.py:383
  109.3 0.7 grad_sum.1
  (2 shorter events, 0.1 us)
Async XLA Ops:
  5.2 7.8 %copy-start.3 = (bf16[1024,32]{0,1:T(8,128)(2,1)S(1)}, bf16[1024,32]{0,1:T(8,128)(2,1)}, u32[]{:S(2)}) copy-start(bf16[1024,32]{0,1:T(8,128)(2,1)} %param.13) | copy-start | bytes 196612
  5.2 7.8 %copy-start.4 = (bf16[32,256]{1,0:T(8,128)(2,1)S(1)}, bf16[32,256]{1,0:T(8,128)(2,1)}, u32[]{:S(2)}) copy-start(bf16[32,256]{1,0:T(8,128)(2,1)} %self_ref.4) | copy-start | bytes 49156
  5.2 7.8 %copy-start.5 = (bf16[32,256]{1,0:T(8,128)(2,1)S(1)}, bf16[32,256]{1,0:T(8,128)(2,1)}, u32[]{:S(2)}) copy-start(bf16[32,256]{1,0:T(8,128)(2,1)} %neigh_ref.4) | copy-start | bytes 49156
  5.2 22.0 %all-to-all-start = ((bf16[16,256,128]{2,1,0:T(8,128)(2,1)}), bf16[16,256,128]{2,1,0:T(8,128)(2,1)S(1)}, u32[]{:S(2)}, u32[]{:S(2)}) async-start(bf16[16,256,128]{2,1,0:T(8,128)(2,1)} %bitcast.12), calls=%async_computation | async-start | bytes 2097152 | tf_op jit(solution)/shard_map/aggregate_exchange/all_to_all | solution.py:301
  13.1 20.1 %collective-permute-start = (bf16[64,512]{1,0:T(8,128)(2,1)S(1)}, bf16[64,512]{1,0:T(8,128)(2,1)S(1)}, u32[]{:S(2)}, u32[]{:S(2)}) collective-permute-start(bf16[64,512]{1,0:T(8,128)(2,1)S(1)} %get-tuple-element.16.pack_ref), channel_id=1, source_target_pairs={{0,16},{16,0},{1,17},{17,1},{2,18},{18,2},{3,19},{19,3},{4,20},{20... | collective-permute-start | bytes 196616 | tf_op jit(solution)/shard_map/inputs_exchange/ppermute | solution.py:311
  27.4 6.6 %collective-permute-start.1 = (bf16[32,512]{1,0:T(8,128)(2,1)S(1)}, bf16[32,512]{1,0:T(8,128)(2,1)S(1)}, u32[]{:S(2)}, u32[]{:S(2)}) collective-permute-start(bf16[32,512]{1,0:T(8,128)(2,1)S(1)} %get-tuple-element.18.other_ref), channel_id=1, source_target_pairs={{0,16},{16,0},{1,17},{17,1},{2,18},{18,2},{3,19},{19,3},{4,20},{20... | collective-permute-start | bytes 98312 | tf_op jit(solution)/shard_map/owned_sum/ppermute | solution.py:319
  47.2 22.0 %copy-start.6 = (s32[256,10]{0,1:T(8,128)S(1)}, s32[256,10]{0,1:T(8,128)}, u32[]{:S(2)}) copy-start(s32[256,10]{0,1:T(8,128)} %param.21) | copy-start | bytes 30724
  47.3 24.1 %collective-permute-start.4 = (bf16[128,256]{1,0:T(8,128)(2,1)S(1)}, bf16[128,256]{1,0:T(8,128)(2,1)S(1)}, u32[]{:S(2)}, u32[]{:S(2)}) collective-permute-start(bf16[128,256]{1,0:T(8,128)(2,1)S(1)} %pre_sum_near.1.own_ref), channel_id=1, source_target_pairs={{0,384},{128,0},{256,128},{384,256},{1,385},{129,1},{257,129},{385... | collective-permute-start | bytes 196616 | tf_op jit(solution)/shard_map/pre_sum_far/ppermute | solution.py:339
  57.0 14.3 %collective-permute-start.3 = (bf16[128,256]{1,0:T(8,128)(2,1)S(1)}, bf16[128,256]{1,0:T(8,128)(2,1)S(1)}, u32[]{:S(2)}, u32[]{:S(2)}) collective-permute-start(bf16[128,256]{1,0:T(8,128)(2,1)S(1)} %pre_sum_near.1.own_ref), channel_id=1, source_target_pairs={{0,128},{128,256},{256,384},{384,0},{1,129},{129,257},{257,385},{3... | collective-permute-start | bytes 196616 | tf_op jit(solution)/shard_map/pre_sum_far/ppermute | solution.py:339
  59.0 16.1 %collective-permute-start.2 = (bf16[128,256]{1,0:T(8,128)(2,1)S(1)}, bf16[128,256]{1,0:T(8,128)(2,1)S(1)}, u32[]{:S(2)}, u32[]{:S(2)}) collective-permute-start(bf16[128,256]{1,0:T(8,128)(2,1)S(1)} %pre_sum_near.1.own_ref), channel_id=1, source_target_pairs={{0,256},{128,384},{256,0},{384,128},{1,257},{129,385},{257,1},{385... | collective-permute-start | bytes 196616 | tf_op jit(solution)/shard_map/pre_sum_far/ppermute | solution.py:339
  69.2 0.7 copy-start.7
  83.5 7.3 %collective-permute-start.5 = (bf16[4,128,256]{2,1,0:T(8,128)(2,1)S(1)}, bf16[4,128,256]{2,1,0:T(8,128)(2,1)S(1)}, u32[]{:S(2)}, u32[]{:S(2)}) collective-permute-start(bf16[4,128,256]{2,1,0:T(8,128)(2,1)S(1)} %all_to_all.21.pre_ref), channel_id=1, source_target_pairs={{0,16},{16,0},{1,17},{17,1},{2,18},{18,2},{3,19},{19,3},{4,20},{20... | collective-permute-start | bytes 786440 | tf_op jit(solution)/shard_map/pre_gather/ppermute | solution.py:351
  89.7 1.1 %copy-start = (bf16[256,256]{1,0:T(8,128)(2,1)S(1)}, bf16[256,256]{1,0:T(8,128)(2,1)}, u32[]{:S(2)}) copy-start(bf16[256,256]{1,0:T(8,128)(2,1)} %self_ref.5) | copy-start | bytes 393220
  89.7 1.1 %copy-start.1 = (bf16[256,256]{1,0:T(8,128)(2,1)S(1)}, bf16[256,256]{1,0:T(8,128)(2,1)}, u32[]{:S(2)}) copy-start(bf16[256,256]{1,0:T(8,128)(2,1)} %neigh_ref.5) | copy-start | bytes 393220
  89.7 1.1 %copy-start.2 = (bf16[256,256]{1,0:T(8,128)(2,1)S(1)}, bf16[256,256]{1,0:T(8,128)(2,1)}, u32[]{:S(2)}) copy-start(bf16[256,256]{1,0:T(8,128)(2,1)} %cotangent_ref.1) | copy-start | bytes 393220

commit v5 on v4

--- a/solution.py
+++ b/solution.py
@@ -1,3 +1,5 @@
+import functools
+
 import jax
 import jax.numpy as jnp
 from jax import lax
@@ -25,33 +27,25 @@
     )
 
 
-def aggregate_kernel(
-    count_ref, index_ref, tiles_ref, feats_ref, out_ref, tiles, feats, sources, products, total, tile_sem, feat_sem
-):
-    slots, block, _ = tiles.shape
-    group = slots // tile_sem.shape[0]
-    feat_copy = pltpu.make_async_copy(feats_ref, feats, feat_sem)
-    feat_copy.start()
-    tile_copies = []
-    for position in range(tile_sem.shape[0]):
-        span = pl.ds(position * group, group)
-        copy = pltpu.make_async_copy(tiles_ref.at[span], tiles.at[span], tile_sem.at[position])
-        copy.start()
-        tile_copies.append(copy)
-    total[...] = jnp.zeros_like(total)
-    feat_copy.wait()
+def aggregate_kernel(owners, near, count_ref, index_ref, tiles_ref, feats_ref, out_ref, sources, products, total):
+    slots, block, _ = tiles_ref.shape
     for position in range(sources.shape[0]):
-        sources[position] = feats[:, position * block : (position + 1) * block]
-    live_tiles = count_ref[0]
-    for slot in range(slots):
-        if slot % group == 0:
-            tile_copies[slot // group].wait()
-        in_use = (slot < live_tiles).astype(F32)
-        products[slot] = contract(sources[index_ref[1, slot]], tiles[slot], 1, 1) * in_use
+        sources[position] = feats_ref[:, position * block : (position + 1) * block]
+    out_ref[...] = jnp.zeros_like(out_ref)
+    places = []
     for slot in range(slots):
         target = index_ref[0, slot]
-        total[target] += products[slot]
-    out_ref[...] = total[...].astype(BF16)
+        place = ((target & 1) * owners + (target >> 3)) * near + ((target & 7) >> 1)
+        places.append(place)
+        total[place] = jnp.zeros(total.shape[1:], F32)
+    live_tiles = count_ref[...]
+    for slot in range(slots):
+        in_use = (slot < live_tiles).astype(F32)
+        products[slot] = contract(sources[index_ref[1, slot]], tiles_ref[slot], 1, 1) * in_use
+    for slot in range(slots):
+        total[places[slot]] += products[slot]
+    for slot in range(slots):
+        out_ref[places[slot]] = total[places[slot]].astype(BF16)
 
 
 def split_blocks(core, halves, mine_ref, other_ref):
@@ -73,36 +67,45 @@
     pack_ref[columns:, hsize:] = neigh_ref[...]
 
 
-def owned_kernel(core_ref, parts_ref, mine_ref, other_ref, halves):
-    near, _, columns, _ = halves.shape
-    for position in range(2 * near):
-        span = slice(position * columns, (position + 1) * columns)
-        block = parts_ref[0, span].astype(F32)
-        for source in range(1, parts_ref.shape[0]):
-            block += parts_ref[source, span].astype(F32)
-        halves[position // 2, position % 2] = block.astype(BF16)
-    split_blocks(core_ref[0], halves, mine_ref, other_ref)
-
-
-def partial_kernel(targets_ref, pack_ref, mine_ref, arrived_ref, self_ref, neigh_ref, out_ref):
+def partial_kernel(
+    core_ref, near_ref, parts_ref, targets_ref, pack_ref, self_ref, neigh_ref,
+    out_ref, own_ref, mine_ref, other_ref, owned, total
+):
     columns, hsize = self_ref.shape
+    block = parts_ref.shape[2]
+    owners = parts_ref.shape[0] // 2
+    for side in range(2):
+        block_sum = parts_ref[side * owners].astype(F32)
+        for source in range(1, owners):
+            block_sum += parts_ref[side * owners + source].astype(F32)
+        block_sum = block_sum.astype(BF16)
+        for position in range(block_sum.shape[0] // columns):
+            owned[side, :, position * block : (position + 1) * block] = block_sum[
+                position * columns : (position + 1) * columns
+            ]
+    core = core_ref[0]
+    mine_ref[...] = owned[core]
+    other_ref[...] = owned[1 - core]
     inputs = jnp.concatenate(
-        [targets_ref[...], pack_ref[:columns], mine_ref[...], arrived_ref[...]], axis=0
+        [targets_ref[...], pack_ref[:columns], mine_ref[...], other_ref[...]], axis=0
     )
     weights = jnp.concatenate(
         [self_ref[...], pack_ref[columns:, :hsize], neigh_ref[...], pack_ref[columns:, hsize:]], axis=0
     )
-    out_ref[...] = contract(inputs, weights, 0, 0).reshape(out_ref.shape).astype(BF16)
-
-
-def near_kernel(parts_ref, out_ref):
-    total = parts_ref[0].astype(F32)
+    total[...] = contract(inputs, weights, 0, 0).reshape(total.shape)
+    out_ref[...] = total[...].astype(BF16)
+    own_ref[...] = total[near_ref[0]]
+
+
+def near_kernel(near_ref, own_ref, parts_ref, agg_ref, out_ref):
+    near = near_ref[0]
+    total = own_ref[...]
     for position in range(1, parts_ref.shape[0]):
-        total += parts_ref[position].astype(F32)
+        total += parts_ref[(near + position) & (parts_ref.shape[0] - 1)].astype(F32)
     out_ref[...] = total.astype(BF16)
 
 
-def far_kernel(far_ref, own_ref, two_ref, one_ref, three_ref, picks_ref, out_ref, slots):
+def far_kernel(far_ref, own_ref, one_ref, three_ref, two_ref, picks_ref, out_ref, slots):
     far = far_ref[0]
     slots[far] = own_ref[...].astype(F32)
     for step, ref in ((2, two_ref), (1, one_ref), (3, three_ref)):
@@ -165,6 +168,8 @@
     grads_ref,
     gathered,
     scratch,
+    output,
+    output_sem,
 ):
     seeds = cotangent_ref.shape[0]
     columns = targets_ref.shape[0]
@@ -176,7 +181,9 @@
     own = picked[seeds:].astype(BF16)
     pre_two = contract(own, self_ref[...], 1, 0) + contract(nbr_mean, neigh_ref[...], 1, 0)
     gate = jax.nn.sigmoid(pre_two)
-    output_ref[...] = (pre_two * gate).astype(BF16)
+    output[...] = (pre_two * gate).astype(BF16)
+    copy = pltpu.make_async_copy(output, output_ref, output_sem)
+    copy.start()
     slope_two = (
         cotangent_ref[...].astype(F32) * (gate * (1.0 + pre_two * (1.0 - gate)))
     ).astype(BF16)
@@ -217,6 +224,7 @@
     every = jnp.concatenate([grad_one, two_high, two_low], axis=0)
     for position in range(grads_ref.shape[0]):
         grads_ref[position] = every
+    copy.wait()
 
 
 def grads_kernel(parts_ref, one_ref, two_ref):
@@ -231,7 +239,7 @@
     two_ref[1] = two[part_rows:]
 
 
-def run(kernel, outs, operands, scratch=(), limit=8, flops=0, specs=None):
+def run(kernel, outs, operands, scratch=(), limit=8, flops=0, specs=None, out_specs=None):
     shapes = [jax.ShapeDtypeStruct(shape, dtype) for shape, dtype in outs]
     moved = sum(x.size * x.dtype.itemsize for x in operands) + sum(
         x.size * x.dtype.itemsize for x in shapes
@@ -242,7 +250,7 @@
         kernel,
         out_shape=shapes,
         in_specs=specs,
-        out_specs=[VMEM] * len(shapes),
+        out_specs=out_specs or [VMEM] * len(shapes),
         scratch_shapes=list(scratch),
         cost_estimate=pl.CostEstimate(flops=flops, bytes_accessed=moved, transcendentals=0),
         compiler_params=pltpu.CompilerParams(vmem_limit_bytes=limit * MIB),
@@ -278,28 +286,25 @@
     core = lax.axis_index("c").reshape(1)
     feat = lax.axis_index(FEAT).reshape(1)
     halves = pltpu.VMEM((near, 2, columns, block), BF16)
+    position = lax.axis_index("zl").reshape(1)
     swap = [(0, 1), (1, 0)]
 
     with jax.named_scope("aggregate_tiles"):
         aggregate = run(
-            aggregate_kernel,
+            functools.partial(aggregate_kernel, owners, near),
             [((all_blocks, columns, block), BF16)],
-            (tile_count, tile_index.T, tile_values, features.T),
+            (tile_count.reshape(1, 1), tile_index.T, tile_values, features.T),
             [
-                pltpu.VMEM(tile_values.shape, BF16),
-                pltpu.VMEM((columns, src_rows), BF16),
                 pltpu.VMEM((src_rows // block, columns, block), BF16),
                 pltpu.VMEM((slots, columns, block), F32),
                 pltpu.VMEM((all_blocks, columns, block), F32),
-                pltpu.SemaphoreType.DMA((4,)),
-                pltpu.SemaphoreType.DMA,
             ],
             limit=56,
-            specs=[SMEM, SMEM, HBM, HBM],
+            specs=[VMEM, SMEM, VMEM, VMEM],
         )
     with jax.named_scope("aggregate_exchange"):
         parts = lax.all_to_all(
-            aggregate.reshape(owners, tgt_rows // block * columns, block), NODE, 0, 0, tiled=True
+            aggregate.reshape(2 * owners, near * columns, block), ("c",) + NODE, 0, 0, tiled=True
         )
     with jax.named_scope("inputs_exchange"):
         targets_mine, pack = run(
@@ -309,23 +314,17 @@
             [halves],
         )
         pack_other = lax.ppermute(pack, "c", swap)
-    with jax.named_scope("owned_sum"):
-        agg_mine, agg_other = run(
-            owned_kernel,
-            [((columns, half), BF16), ((columns, half), BF16)],
-            (core, parts),
-            [halves],
-        )
-        agg_arrived = lax.ppermute(agg_other, "c", swap)
     with jax.named_scope("partial_pre"):
-        pieces = run(
+        pieces, own, agg_mine, agg_send = run(
             partial_kernel,
-            [((near, span, hsize), BF16)],
-            (targets_mine, pack_other, agg_mine, agg_arrived, self_weight1, neigh_weight1),
-        )
+            [((near, span, hsize), BF16), ((span, hsize), F32), ((columns, half), BF16), ((columns, half), BF16)],
+            (core, position, parts, targets_mine, pack_other, self_weight1, neigh_weight1),
+            [pltpu.VMEM((2, columns, half), BF16), pltpu.VMEM((near, span, hsize), F32)],
+        )
+        agg_other = lax.ppermute(agg_send, "c", swap)
     with jax.named_scope("pre_sum_near"):
         pieces = lax.all_to_all(pieces, "zl", 0, 0, tiled=True)
-        quarter = run(near_kernel, [((span, hsize), BF16)], (pieces,))
+        quarter = run(near_kernel, [((span, hsize), BF16)], (position, own, pieces, agg_other), specs=[SMEM, VMEM, VMEM, ANY])
     with jax.named_scope("picks"):
         spread, pick = run(
             picks_kernel,
@@ -337,7 +336,7 @@
     with jax.named_scope("pre_sum_far"):
         arrived = [
             lax.ppermute(quarter, "zh", [(i, (i + step) % far) for i in range(far)])
-            for step in (2, 1, 3)
+            for step in (1, 3, 2)
         ]
         copies = run(
             far_kernel,
@@ -376,8 +375,14 @@
                 agg_mine,
                 agg_other,
             ),
-            [pltpu.VMEM((2 * seeds, hsize), F32), pltpu.VMEM((2, hsize, hsize), F32)],
+            [
+                pltpu.VMEM((2 * seeds, hsize), F32),
+                pltpu.VMEM((2, hsize, hsize), F32),
+                pltpu.VMEM(cotangent.shape, BF16),
+                pltpu.SemaphoreType.DMA,
+            ],
             limit=24,
+            out_specs=[HBM, VMEM],
         )
     with jax.named_scope("grad_sum"):
         grads = lax.all_to_all(grads, NODE, 0, 0, tiled=True)

time: 111 us -> 108 us (0.973)
  blocking collectives: 37.6 us -> 26.4 us
  starting transfers between devices: 46.4 us -> 51.1 us
  waiting for transfers between devices: 14.5 us -> 18.9 us
    all_to_all x1 -> x0, blocking collectives: 13 us -> none  [per_device(): pieces = lax.all_to_all(pieces, 'zl', 0, 0, tiled=True)]
    all_to_all x1 -> x2, starting transfers between devices: 7.72 us -> 14.3 us  [the longest x1 10.7 us: per_device(): lax.all_to_all(aggregate.reshape(2 * owners, near * columns, block), ('c'...]
    all_to_all x1 -> x2, waiting for transfers between devices: 9.29 us -> 15.1 us  [the longest x1 13.4 us: per_device(): lax.all_to_all(aggregate.reshape(2 * owners, near * columns, block), ('c'...]
    ppermute x1, starting transfers between devices: 4.86 us -> 2.15 us  [per_device(): pack_other = lax.ppermute(pack, 'c', swap)]
    ppermute x1, starting transfers between devices: 5.74 us -> 3.31 us  [per_device(): agg_other = lax.ppermute(agg_send, 'c', swap)]
    ppermute x3, waiting for transfers between devices: 3.69 us -> 1.37 us  [per_device(): lax.ppermute(quarter, 'zh', [(i, (i + step) % far) for i in range(far)])]
    ppermute x3, starting transfers between devices: 21.9 us -> 24.2 us  [per_device(): lax.ppermute(quarter, 'zh', [(i, (i + step) % far) for i in range(far)])]
    all_to_all x1, blocking collectives: 16.2 us -> 17.7 us  [per_device(): grads = lax.all_to_all(grads, NODE, 0, 0, tiled=True)]
  transfers between devices with their start and end apart: 7 -> 8, of which waited for: 4 -> 6; matrix products, arithmetic and copies ran while one was open for 0% -> 0% of each run, Pallas kernels for 2% -> 2%
where the time goes in v5:
time: 108 us
  starting transfers between devices  51.1 us (47%)
  blocking collectives  26.4 us (24%)
  waiting for transfers between devices  18.9 us (17%)
  Pallas kernels  9.09 us (8%)
  between operations  1.48 us (1%)
    ppermute x3, starting transfers between devices, per_device(): lax.ppermute(quarter, 'zh', [(i, (i + step) % far) for i in range(far)])  24.2 us
    all_to_all x1, blocking collectives, per_device(): grads = lax.all_to_all(grads, NODE, 0, 0, tiled=True)  17.7 us
    all_to_all x1, waiting for transfers between devices, per_device(): lax.all_to_all(aggregate.reshape(2 * owners, near * columns, block), ('c'...  13.4 us
    all_to_all x1, starting transfers between devices, per_device(): lax.all_to_all(aggregate.reshape(2 * owners, near * columns, block), ('c'...  10.7 us
    pallas_call x9, Pallas kernels, run(): pl.pallas_call(kernel, out_shape=shapes, in_specs=specs, out_specs=out_sp...  9.09 us
    all_to_all x1, blocking collectives, per_device(): pre_mine = lax.all_to_all(copies, 'zl', 0, 0, tiled=True)  8.71 us
    ppermute x1, starting transfers between devices, per_device(): pre_other = lax.ppermute(pre_mine, 'c', swap)  7.18 us
    all_to_all x1, starting transfers between devices, per_device(): pieces = lax.all_to_all(pieces, 'zl', 0, 0, tiled=True)  3.57 us
  transfers between devices with their start and end apart: 8, of which 6 were waited for; matrix products, arithmetic and copies ran while one was open for 0% of the time, Pallas kernels for 2%

profile of v5, /device:TPU:1, one launch (start us, length us, event | category | flops | bytes accessed | tf_op | source)
XLA Modules:
  0.0 107.6 jit_solution(7462503565316504787)
XLA Ops:
  1.3 3.0 %aggregate_tiles.1 = bf16[128,32,128]{2,1,0:T(8,128)(2,1)} custom-call(s32[1,1]{1,0:T(1,128)} %bitcast.11.count_ref, s32[2,32]{1,0:T(2,128)} %bitcast.17, bf16[32,128,128]{2,1,0:T(8,128)(2,1)} %tiles_ref.1, bf16[32,1024]{1,0:T(8,128)(2,1)} %bitcast.16), custom_call_target="tpu_custom_call" | custom-call | bytes 2162948 | tf_op jit(solution)/shard_map/aggregate_tiles/pallas_call | solution.py:249
  4.3 0.0 copy-start.3
  4.3 0.0 copy-start.4
  4.3 0.0 copy-start.5
  4.3 10.7 %all-to-all-start = ((bf16[32,128,128]{2,1,0:T(8,128)(2,1)}), bf16[32,128,128]{2,1,0:T(8,128)(2,1)S(1)}, u32[]{:S(2)}, u32[]{:S(2)}) async-start(bf16[32,128,128]{2,1,0:T(8,128)(2,1)} %bitcast.15), calls=%async_computation | async-start | bytes 2097152 | tf_op jit(solution)/shard_map/aggregate_exchange/all_to_all | solution.py:306
  15.0 0.0 copy-done.3
  15.0 0.0 copy-done.4
  15.0 0.0 copy-done.5
  15.1 2.2 %collective-permute-start = (bf16[64,512]{1,0:T(8,128)(2,1)S(1)}, bf16[64,512]{1,0:T(8,128)(2,1)S(1)}, u32[]{:S(2)}, u32[]{:S(2)}) collective-permute-start(bf16[64,512]{1,0:T(8,128)(2,1)S(1)} %get-tuple-element.18.pack_ref), channel_id=1, source_target_pairs={{0,16},{16,0},{1,17},{17,1},{2,18},{18,2},{3,19},{19,3},{4,20},{20... | collective-permute-start | bytes 196616 | tf_op jit(solution)/shard_map/inputs_exchange/ppermute | solution.py:316
  17.2 1.0 collective-permute-done.pack_ref
  18.2 13.4 %all-to-all-done.parts_ref = bf16[32,128,128]{2,1,0:T(8,128)(2,1)S(1)} async-done(((bf16[32,128,128]{2,1,0:T(8,128)(2,1)}), bf16[32,128,128]{2,1,0:T(8,128)(2,1)S(1)}, u32[]{:S(2)}, u32[]{:S(2)}) %all-to-all-start) | async-done | bytes 1048608 | tf_op jit(solution)/shard_map/aggregate_exchange/all_to_all | solution.py:306
  31.6 1.1 %partial_pre.1 = (bf16[4,128,256]{2,1,0:T(8,128)(2,1)}, f32[128,256]{1,0:T(8,128)S(1)}, bf16[32,512]{1,0:T(8,128)(2,1)S(1)}, bf16[32,512]{1,0:T(8,128)(2,1)S(1)}) custom-call(s32[1]{0:T(128)} %bitcast.3.core_ref, s32[1]{0:T(128)} %bitcast.2.near_ref, bf16[32,128,128]{2,1,0:T(8,128)(2,1)S(1)} %all-to-all-done.parts_ref, ...), custom_call_target="tpu_custom_call" | custom-call | bytes 1638408 | tf_op jit(solution)/shard_map/partial_pre/pallas_call | solution.py:249
  32.7 3.6 %all-to-all-start.1 = ((bf16[4,128,256]{2,1,0:T(8,128)(2,1)}), bf16[4,128,256]{2,1,0:T(8,128)(2,1)S(1)}, u32[]{:S(2)}, u32[]{:S(2)}) async-start(bf16[4,128,256]{2,1,0:T(8,128)(2,1)} %get-tuple-element.20), calls=%async_computation.1 | async-start | bytes 524288 | tf_op jit(solution)/shard_map/pre_sum_near/all_to_all | solution.py:326
  36.3 3.3 %collective-permute-start.1 = (bf16[32,512]{1,0:T(8,128)(2,1)S(1)}, bf16[32,512]{1,0:T(8,128)(2,1)S(1)}, u32[]{:S(2)}, u32[]{:S(2)}) collective-permute-start(bf16[32,512]{1,0:T(8,128)(2,1)S(1)} %get-tuple-element.21), channel_id=1, source_target_pairs={{0,16},{16,0},{1,17},{17,1},{2,18},{18,2},{3,19},{19,3},{4,20},{20... | collective-permute-start | bytes 98312 | tf_op jit(solution)/shard_map/partial_pre/ppermute | solution.py:324
  39.6 0.8 collective-permute-done.1.agg_ref.other_ref
  40.4 1.6 %all-to-all-done.1.parts_ref = bf16[4,128,256]{2,1,0:T(8,128)(2,1)S(1)} async-done(((bf16[4,128,256]{2,1,0:T(8,128)(2,1)}), bf16[4,128,256]{2,1,0:T(8,128)(2,1)S(1)}, u32[]{:S(2)}, u32[]{:S(2)}) %all-to-all-start.1) | async-done | bytes 262176 | tf_op jit(solution)/shard_map/pre_sum_near/all_to_all | solution.py:326
  42.1 0.0 copy-start.6
  42.1 15.0 %collective-permute-start.4 = (bf16[128,256]{1,0:T(8,128)(2,1)S(1)}, bf16[128,256]{1,0:T(8,128)(2,1)S(1)}, u32[]{:S(2)}, u32[]{:S(2)}) collective-permute-start(bf16[128,256]{1,0:T(8,128)(2,1)S(1)} %pre_sum_near.1.own_ref), channel_id=1, source_target_pairs={{0,256},{128,384},{256,0},{384,128},{1,257},{129,385},{257,1},{385... | collective-permute-start | bytes 196616 | tf_op jit(solution)/shard_map/pre_sum_far/ppermute | solution.py:338
  57.1 1.9 %collective-permute-start.3 = (bf16[128,256]{1,0:T(8,128)(2,1)S(1)}, bf16[128,256]{1,0:T(8,128)(2,1)S(1)}, u32[]{:S(2)}, u32[]{:S(2)}) collective-permute-start(bf16[128,256]{1,0:T(8,128)(2,1)S(1)} %pre_sum_near.1.own_ref), channel_id=1, source_target_pairs={{0,384},{128,0},{256,128},{384,256},{1,385},{129,1},{257,129},{385... | collective-permute-start | bytes 196616 | tf_op jit(solution)/shard_map/pre_sum_far/ppermute | solution.py:338
  59.0 7.3 %collective-permute-start.2 = (bf16[128,256]{1,0:T(8,128)(2,1)S(1)}, bf16[128,256]{1,0:T(8,128)(2,1)S(1)}, u32[]{:S(2)}, u32[]{:S(2)}) collective-permute-start(bf16[128,256]{1,0:T(8,128)(2,1)S(1)} %pre_sum_near.1.own_ref), channel_id=1, source_target_pairs={{0,128},{128,256},{256,384},{384,0},{1,129},{129,257},{257,385},{3... | collective-permute-start | bytes 196616 | tf_op jit(solution)/shard_map/pre_sum_far/ppermute | solution.py:338
  66.3 0.0 copy-start.7
  66.3 0.0 copy-done.6
  66.3 0.7 copy-done.7
  67.0 1.4 %picks.1 = (bf16[1024,512]{1,0:T(8,128)(2,1)S(1)}, bf16[512,1024]{1,0:T(8,128)(2,1)S(1)}) custom-call(s32[1]{0:T(128)} %bitcast.3.core_ref, s32[10,256]{1,0:T(8,128)S(1)} %bitcast.13, s32[1,256]{1,0:T(1,128)S(1)} %bitcast.14), custom_call_target="tpu_custom_call" | custom-call | flops 5242880 | bytes 2108420 | tf_op jit(solution)/shard_map/picks/pallas_call | solution.py:249
  68.4 0.0 collective-permute-done.4.two_ref
  68.4 0.0 collective-permute-done.3.three_ref
  68.5 1.4 %collective-permute-done.2.one_ref = bf16[128,256]{1,0:T(8,128)(2,1)S(1)} collective-permute-done((bf16[128,256]{1,0:T(8,128)(2,1)S(1)}, bf16[128,256]{1,0:T(8,128)(2,1)S(1)}, u32[]{:S(2)}, u32[]{:S(2)}) %collective-permute-start.2) | collective-permute-done | bytes 65568 | tf_op jit(solution)/shard_map/pre_sum_far/ppermute | solution.py:338
  69.8 0.1 pre_sum_far.1
  69.9 8.7 %all_to_all.20.pre_ref = bf16[4,128,256]{2,1,0:T(8,128)(2,1)S(1)} all-to-all(bf16[4,128,256]{2,1,0:T(8,128)(2,1)S(1)} %pre_sum_far.1), channel_id=1, replica_groups=mesh['zh'=4,'zl'=4,'c'=2,'x'=4,'y'=4] {'zl'}, dimensions={0} | all-to-all | bytes 524288 | tf_op jit(solution)/shard_map/pre_gather/all_to_all | solution.py:349
  78.6 7.2 %collective-permute-start.5 = (bf16[4,128,256]{2,1,0:T(8,128)(2,1)S(1)}, bf16[4,128,256]{2,1,0:T(8,128)(2,1)S(1)}, u32[]{:S(2)}, u32[]{:S(2)}) collective-permute-start(bf16[4,128,256]{2,1,0:T(8,128)(2,1)S(1)} %all_to_all.20.pre_ref), channel_id=1, source_target_pairs={{0,16},{16,0},{1,17},{17,1},{2,18},{18,2},{3,19},{19,3},{4,20},{20... | collective-permute-start | bytes 786440 | tf_op jit(solution)/shard_map/pre_gather/ppermute | solution.py:350
  85.8 0.0 copy-start
  85.8 0.0 copy-start.1
  85.8 0.0 copy-start.2
  85.8 0.4 step_mine.1
  86.3 0.7 collective-permute-done.5.pre_ref
  86.9 0.0 copy-done
  86.9 0.0 copy-done.1
  86.9 0.0 copy-done.2
  86.9 2.3 %step.1 = (bf16[256,256]{1,0:T(8,128)(2,1)}, bf16[16,96,256]{2,1,0:T(8,128)(2,1)S(1)}) custom-call(s32[1]{0:T(128)} %bitcast.feat_ref, bf16[4,128,256]{2,1,0:T(8,128)(2,1)S(1)} %collective-permute-done.5.pre_ref, f32[512,256]{1,0:T(8,128)S(1)} %get-tuple-element.23.gathered_ref, f32[512,256]{1,0:T(8,128)S(1)} %get-tuple-element.24.slope_ref, ...), custom_call_target="tpu_custom_call" | custom-call | bytes 4882436 | tf_op jit(solution)/shard_map/step/pallas_call | solution.py:249
  89.2 17.7 %all_to_all.21.parts_ref = bf16[16,96,256]{2,1,0:T(8,128)(2,1)S(1)} all-to-all(bf16[16,96,256]{2,1,0:T(8,128)(2,1)S(1)} %get-tuple-element.28), channel_id=1, replica_groups=mesh['zh'=4,'zl'=4,'c'=2,'x'=4,'y'=4] {'x','y'}, dimensions={0} | all-to-all | bytes 1572864 | tf_op jit(solution)/shard_map/grad_sum/all_to_all | solution.py:388
  106.9 0.7 grad_sum.1
  (2 shorter events, 0.1 us)
Async XLA Ops:
  4.3 10.7 %copy-start.3 = (bf16[32,256]{1,0:T(8,128)(2,1)S(1)}, bf16[32,256]{1,0:T(8,128)(2,1)}, u32[]{:S(2)}) copy-start(bf16[32,256]{1,0:T(8,128)(2,1)} %self_ref.4) | copy-start | bytes 49156
  4.3 10.7 %copy-start.4 = (bf16[32,256]{1,0:T(8,128)(2,1)S(1)}, bf16[32,256]{1,0:T(8,128)(2,1)}, u32[]{:S(2)}) copy-start(bf16[32,256]{1,0:T(8,128)(2,1)} %neigh_ref.4) | copy-start | bytes 49156
  4.3 10.7 %copy-start.5 = (bf16[1024,32]{0,1:T(8,128)(2,1)S(1)}, bf16[1024,32]{0,1:T(8,128)(2,1)}, u32[]{:S(2)}) copy-start(bf16[1024,32]{0,1:T(8,128)(2,1)} %param.13) | copy-start | bytes 196612
  4.3 27.3 %all-to-all-start = ((bf16[32,128,128]{2,1,0:T(8,128)(2,1)}), bf16[32,128,128]{2,1,0:T(8,128)(2,1)S(1)}, u32[]{:S(2)}, u32[]{:S(2)}) async-start(bf16[32,128,128]{2,1,0:T(8,128)(2,1)} %bitcast.15), calls=%async_computation | async-start | bytes 2097152 | tf_op jit(solution)/shard_map/aggregate_exchange/all_to_all | solution.py:306
  15.1 3.1 %collective-permute-start = (bf16[64,512]{1,0:T(8,128)(2,1)S(1)}, bf16[64,512]{1,0:T(8,128)(2,1)S(1)}, u32[]{:S(2)}, u32[]{:S(2)}) collective-permute-start(bf16[64,512]{1,0:T(8,128)(2,1)S(1)} %get-tuple-element.18.pack_ref), channel_id=1, source_target_pairs={{0,16},{16,0},{1,17},{17,1},{2,18},{18,2},{3,19},{19,3},{4,20},{20... | collective-permute-start | bytes 196616 | tf_op jit(solution)/shard_map/inputs_exchange/ppermute | solution.py:316
  32.7 9.4 %all-to-all-start.1 = ((bf16[4,128,256]{2,1,0:T(8,128)(2,1)}), bf16[4,128,256]{2,1,0:T(8,128)(2,1)S(1)}, u32[]{:S(2)}, u32[]{:S(2)}) async-start(bf16[4,128,256]{2,1,0:T(8,128)(2,1)} %get-tuple-element.20), calls=%async_computation.1 | async-start | bytes 524288 | tf_op jit(solution)/shard_map/pre_sum_near/all_to_all | solution.py:326
  36.3 4.2 %collective-permute-start.1 = (bf16[32,512]{1,0:T(8,128)(2,1)S(1)}, bf16[32,512]{1,0:T(8,128)(2,1)S(1)}, u32[]{:S(2)}, u32[]{:S(2)}) collective-permute-start(bf16[32,512]{1,0:T(8,128)(2,1)S(1)} %get-tuple-element.21), channel_id=1, source_target_pairs={{0,16},{16,0},{1,17},{17,1},{2,18},{18,2},{3,19},{19,3},{4,20},{20... | collective-permute-start | bytes 98312 | tf_op jit(solution)/shard_map/partial_pre/ppermute | solution.py:324
  42.1 24.3 %copy-start.6 = (s32[256,10]{0,1:T(8,128)S(1)}, s32[256,10]{0,1:T(8,128)}, u32[]{:S(2)}) copy-start(s32[256,10]{0,1:T(8,128)} %param.21) | copy-start | bytes 30724
  42.1 26.3 %collective-permute-start.4 = (bf16[128,256]{1,0:T(8,128)(2,1)S(1)}, bf16[128,256]{1,0:T(8,128)(2,1)S(1)}, u32[]{:S(2)}, u32[]{:S(2)}) collective-permute-start(bf16[128,256]{1,0:T(8,128)(2,1)S(1)} %pre_sum_near.1.own_ref), channel_id=1, source_target_pairs={{0,256},{128,384},{256,0},{384,128},{1,257},{129,385},{257,1},{385... | collective-permute-start | bytes 196616 | tf_op jit(solution)/shard_map/pre_sum_far/ppermute | solution.py:338
  57.1 11.3 %collective-permute-start.3 = (bf16[128,256]{1,0:T(8,128)(2,1)S(1)}, bf16[128,256]{1,0:T(8,128)(2,1)S(1)}, u32[]{:S(2)}, u32[]{:S(2)}) collective-permute-start(bf16[128,256]{1,0:T(8,128)(2,1)S(1)} %pre_sum_near.1.own_ref), channel_id=1, source_target_pairs={{0,384},{128,0},{256,128},{384,256},{1,385},{129,1},{257,129},{385... | collective-permute-start | bytes 196616 | tf_op jit(solution)/shard_map/pre_sum_far/ppermute | solution.py:338
  59.0 10.8 %collective-permute-start.2 = (bf16[128,256]{1,0:T(8,128)(2,1)S(1)}, bf16[128,256]{1,0:T(8,128)(2,1)S(1)}, u32[]{:S(2)}, u32[]{:S(2)}) collective-permute-start(bf16[128,256]{1,0:T(8,128)(2,1)S(1)} %pre_sum_near.1.own_ref), channel_id=1, source_target_pairs={{0,128},{128,256},{256,384},{384,0},{1,129},{129,257},{257,385},{3... | collective-permute-start | bytes 196616 | tf_op jit(solution)/shard_map/pre_sum_far/ppermute | solution.py:338
  66.3 0.7 copy-start.7
  78.6 8.3 %collective-permute-start.5 = (bf16[4,128,256]{2,1,0:T(8,128)(2,1)S(1)}, bf16[4,128,256]{2,1,0:T(8,128)(2,1)S(1)}, u32[]{:S(2)}, u32[]{:S(2)}) collective-permute-start(bf16[4,128,256]{2,1,0:T(8,128)(2,1)S(1)} %all_to_all.20.pre_ref), channel_id=1, source_target_pairs={{0,16},{16,0},{1,17},{17,1},{2,18},{18,2},{3,19},{19,3},{4,20},{20... | collective-permute-start | bytes 786440 | tf_op jit(solution)/shard_map/pre_gather/ppermute | solution.py:350
  85.8 1.1 %copy-start = (bf16[256,256]{1,0:T(8,128)(2,1)S(1)}, bf16[256,256]{1,0:T(8,128)(2,1)}, u32[]{:S(2)}) copy-start(bf16[256,256]{1,0:T(8,128)(2,1)} %self_ref.5) | copy-start | bytes 393220
  85.8 1.1 %copy-start.1 = (bf16[256,256]{1,0:T(8,128)(2,1)S(1)}, bf16[256,256]{1,0:T(8,128)(2,1)}, u32[]{:S(2)}) copy-start(bf16[256,256]{1,0:T(8,128)(2,1)} %neigh_ref.5) | copy-start | bytes 393220
  85.8 1.1 %copy-start.2 = (bf16[256,256]{1,0:T(8,128)(2,1)S(1)}, bf16[256,256]{1,0:T(8,128)(2,1)}, u32[]{:S(2)}) copy-start(bf16[256,256]{1,0:T(8,128)(2,1)} %cotangent_ref.1) | copy-start | bytes 393220

commit v6 on v5

--- a/solution.py
+++ b/solution.py
@@ -1,5 +1,3 @@
-import functools
-
 import jax
 import jax.numpy as jnp
 from jax import lax
@@ -12,6 +10,7 @@
 F32 = jnp.float32
 NODE = ("x", "y")
 FEAT = ("zh", "zl", "c")
+NEAR = ("zl", "c")
 FAN = 10
 MIB = 1 << 20
 
@@ -27,15 +26,14 @@
     )
 
 
-def aggregate_kernel(owners, near, count_ref, index_ref, tiles_ref, feats_ref, out_ref, sources, products, total):
+def aggregate_kernel(count_ref, index_ref, tiles_ref, feats_ref, out_ref, sources, products, total):
     slots, block, _ = tiles_ref.shape
     for position in range(sources.shape[0]):
         sources[position] = feats_ref[:, position * block : (position + 1) * block]
     out_ref[...] = jnp.zeros_like(out_ref)
     places = []
     for slot in range(slots):
-        target = index_ref[0, slot]
-        place = ((target & 1) * owners + (target >> 3)) * near + ((target & 7) >> 1)
+        place = index_ref[0, slot]
         places.append(place)
         total[place] = jnp.zeros(total.shape[1:], F32)
     live_tiles = count_ref[...]
@@ -56,53 +54,60 @@
         other_ref[:, span] = halves[position, 1 - core]
 
 
-def pack_kernel(core_ref, targets_ref, self_ref, neigh_ref, mine_ref, pack_ref, halves):
-    columns = targets_ref.shape[0]
-    near, _, _, block = halves.shape
+def pack_kernel(core_ref, targets_ref, self_ref, neigh_ref, pack_ref, mine_ref, other_ref, halves):
+    near, _, columns, block = halves.shape
     for position in range(2 * near):
         halves[position // 2, position % 2] = targets_ref[:, position * block : (position + 1) * block]
-    split_blocks(core_ref[0], halves, mine_ref, pack_ref.at[:columns])
+    split_blocks(core_ref[0], halves, mine_ref, other_ref)
     hsize = self_ref.shape[1]
+    pack_ref[:columns] = other_ref[...]
     pack_ref[columns:, :hsize] = self_ref[...]
     pack_ref[columns:, hsize:] = neigh_ref[...]
 
 
-def partial_kernel(
-    core_ref, near_ref, parts_ref, targets_ref, pack_ref, self_ref, neigh_ref,
-    out_ref, own_ref, mine_ref, other_ref, owned, total
-):
-    columns, hsize = self_ref.shape
-    block = parts_ref.shape[2]
-    owners = parts_ref.shape[0] // 2
-    for side in range(2):
-        block_sum = parts_ref[side * owners].astype(F32)
-        for source in range(1, owners):
-            block_sum += parts_ref[side * owners + source].astype(F32)
-        block_sum = block_sum.astype(BF16)
-        for position in range(block_sum.shape[0] // columns):
-            owned[side, :, position * block : (position + 1) * block] = block_sum[
-                position * columns : (position + 1) * columns
-            ]
+def pieces_kernel(near_ref, targets_ref, pack_ref, arrived_ref, *rest):
+    piece_refs, pieces = rest[:-1], rest[-1]
+    near, columns, block = pieces.shape[0], targets_ref.shape[0], pieces.shape[2]
+    for position in range(near):
+        span = slice(position * block, (position + 1) * block)
+        pieces[position, :columns] = targets_ref[:, span]
+        pieces[position, columns:] = arrived_ref[:columns, span]
+    for step, ref in enumerate(piece_refs):
+        ref[:, :block] = pieces[(near_ref[0] + step) & (near - 1)]
+        ref[:columns, block:] = pack_ref[columns:]
+        ref[columns:, block:] = arrived_ref[columns:]
+
+
+def owned_kernel(core_ref, parts_ref, one_ref, two_ref, three_ref, blocks_ref, mine_ref, other_ref, halves):
+    near, _, columns, _ = halves.shape
+    for position in range(2 * near):
+        span = slice(position * columns, (position + 1) * columns)
+        block = parts_ref[0, span].astype(F32)
+        for source in range(1, parts_ref.shape[0]):
+            block += parts_ref[source, span].astype(F32)
+        block = block.astype(BF16)
+        blocks_ref[position] = block
+        halves[position // 2, position % 2] = block
+    split_blocks(core_ref[0], halves, mine_ref, other_ref)
+
+
+def partial_kernel(core_ref, near_ref, blocks_ref, *rest):
+    piece_refs, (out_ref, inputs, weights, sides) = rest[:-4], rest[-4:]
+    group, columns, block = blocks_ref.shape
+    near, hsize = len(piece_refs), out_ref.shape[1]
     core = core_ref[0]
-    mine_ref[...] = owned[core]
-    other_ref[...] = owned[1 - core]
-    inputs = jnp.concatenate(
-        [targets_ref[...], pack_ref[:columns], mine_ref[...], other_ref[...]], axis=0
-    )
-    weights = jnp.concatenate(
-        [self_ref[...], pack_ref[columns:, :hsize], neigh_ref[...], pack_ref[columns:, hsize:]], axis=0
-    )
-    total[...] = contract(inputs, weights, 0, 0).reshape(total.shape)
-    out_ref[...] = total[...].astype(BF16)
-    own_ref[...] = total[near_ref[0]]
-
-
-def near_kernel(near_ref, own_ref, parts_ref, agg_ref, out_ref):
-    near = near_ref[0]
-    total = own_ref[...]
-    for position in range(1, parts_ref.shape[0]):
-        total += parts_ref[(near + position) & (parts_ref.shape[0] - 1)].astype(F32)
-    out_ref[...] = total.astype(BF16)
+    for step, ref in enumerate(piece_refs):
+        span = slice(step * 2 * columns, (step + 1) * 2 * columns)
+        inputs[span] = ref[:, :block]
+        weights[span] = ref[:, block : block + hsize]
+        source = (near_ref[0] + near - step) & (near - 1)
+        sides[source, core] = ref[:columns, block + hsize :]
+        sides[source, 1 - core] = ref[columns:, block + hsize :]
+    for position in range(group):
+        span = slice((group + position) * columns, (group + position + 1) * columns)
+        inputs[span] = blocks_ref[position]
+        weights[span] = sides[position // 2, position % 2]
+    out_ref[...] = contract(inputs[...], weights[...], 0, 0).astype(BF16)
 
 
 def far_kernel(far_ref, own_ref, one_ref, three_ref, two_ref, picks_ref, out_ref, slots):
@@ -161,7 +166,7 @@
     neigh_ref,
     cotangent_ref,
     targets_ref,
-    pack_ref,
+    targets_other_ref,
     mine_ref,
     other_ref,
     output_ref,
@@ -208,20 +213,18 @@
     )
     inputs = jnp.concatenate(
         [
-            jnp.concatenate([targets_ref[...], pack_ref[:columns]], axis=1),
+            jnp.concatenate([targets_ref[...], targets_other_ref[...]], axis=1),
             jnp.concatenate([mine_ref[...], other_ref[...]], axis=1),
         ],
         axis=0,
     )
     grad_one = contract(inputs, slope_one, 1, 0).astype(BF16)
-    part_rows = (grads_ref.shape[1] - 2 * columns) // 4
+    part_rows = (grads_ref.shape[1] - 2 * columns) // 2
     first = pl.multiple_of(feat_ref[0] * part_rows, part_rows)
     grad_two = jnp.concatenate(
         [scratch[0, pl.ds(first, part_rows), :], scratch[1, pl.ds(first, part_rows), :]], axis=0
     )
-    two_high = grad_two.astype(BF16)
-    two_low = (grad_two - two_high.astype(F32)).astype(BF16)
-    every = jnp.concatenate([grad_one, two_high, two_low], axis=0)
+    every = jnp.concatenate([grad_one, grad_two.astype(BF16)], axis=0)
     for position in range(grads_ref.shape[0]):
         grads_ref[position] = every
     copy.wait()
@@ -234,9 +237,8 @@
     columns, part_rows = one_ref.shape[1], two_ref.shape[1]
     one_ref[0] = total[:columns]
     one_ref[1] = total[columns : 2 * columns]
-    two = total[2 * columns : 2 * columns + 2 * part_rows] + total[2 * columns + 2 * part_rows :]
-    two_ref[0] = two[:part_rows]
-    two_ref[1] = two[part_rows:]
+    two_ref[0] = total[2 * columns : 2 * columns + part_rows]
+    two_ref[1] = total[2 * columns + part_rows :]
 
 
 def run(kernel, outs, operands, scratch=(), limit=8, flops=0, specs=None, out_specs=None):
@@ -291,7 +293,7 @@
 
     with jax.named_scope("aggregate_tiles"):
         aggregate = run(
-            functools.partial(aggregate_kernel, owners, near),
+            aggregate_kernel,
             [((all_blocks, columns, block), BF16)],
             (tile_count.reshape(1, 1), tile_index.T, tile_values, features.T),
             [
@@ -304,27 +306,47 @@
         )
     with jax.named_scope("aggregate_exchange"):
         parts = lax.all_to_all(
-            aggregate.reshape(2 * owners, near * columns, block), ("c",) + NODE, 0, 0, tiled=True
+            aggregate.reshape(owners, tgt_rows // block * columns, block), NODE, 0, 0, tiled=True
         )
     with jax.named_scope("inputs_exchange"):
-        targets_mine, pack = run(
+        pack, targets_mine, targets_other = run(
             pack_kernel,
-            [((columns, half), BF16), ((2 * columns, half), BF16)],
+            [((2 * columns, half), BF16), ((columns, half), BF16), ((columns, half), BF16)],
             (core, target_feats.T, self_weight1, neigh_weight1),
             [halves],
         )
-        pack_other = lax.ppermute(pack, "c", swap)
+        arrived = lax.ppermute(pack, "c", swap)
+        sends = run(
+            pieces_kernel,
+            [((2 * columns, block + 2 * hsize), BF16)] * near,
+            (position, targets_mine, pack, arrived),
+            [pltpu.VMEM((near, 2 * columns, block), BF16)],
+        )
+        pieces = [sends[0]] + [
+            lax.ppermute(sends[step], "zl", [(i, (i + step) % near) for i in range(near)])
+            for step in range(1, near)
+        ]
+    with jax.named_scope("owned_sum"):
+        blocks, agg_mine, agg_other = run(
+            owned_kernel,
+            [((2 * near, columns, block), BF16), ((columns, half), BF16), ((columns, half), BF16)],
+            (core, parts, *pieces[1:]),
+            [halves],
+            specs=[SMEM, VMEM] + [ANY] * (near - 1),
+        )
+    with jax.named_scope("near_exchange"):
+        blocks = lax.all_to_all(blocks, NEAR, 0, 0, tiled=True)
     with jax.named_scope("partial_pre"):
-        pieces, own, agg_mine, agg_send = run(
+        quarter = run(
             partial_kernel,
-            [((near, span, hsize), BF16), ((span, hsize), F32), ((columns, half), BF16), ((columns, half), BF16)],
-            (core, position, parts, targets_mine, pack_other, self_weight1, neigh_weight1),
-            [pltpu.VMEM((2, columns, half), BF16), pltpu.VMEM((near, span, hsize), F32)],
-        )
-        agg_other = lax.ppermute(agg_send, "c", swap)
-    with jax.named_scope("pre_sum_near"):
-        pieces = lax.all_to_all(pieces, "zl", 0, 0, tiled=True)
-        quarter = run(near_kernel, [((span, hsize), BF16)], (position, own, pieces, agg_other), specs=[SMEM, VMEM, VMEM, ANY])
+            [((span, hsize), BF16)],
+            (core, position, blocks, *pieces),
+            [
+                pltpu.VMEM((4 * near * columns, span), BF16),
+                pltpu.VMEM((4 * near * columns, hsize), BF16),
+                pltpu.VMEM((near, 2, columns, hsize), BF16),
+            ],
+        )
     with jax.named_scope("picks"):
         spread, pick = run(
             picks_kernel,
@@ -359,7 +381,7 @@
     with jax.named_scope("step"):
         output, grads = run(
             step_kernel,
-            [(cotangent.shape, BF16), ((owners, 2 * columns + 4 * part_rows, hsize), BF16)],
+            [(cotangent.shape, BF16), ((owners, 2 * columns + 2 * part_rows, hsize), BF16)],
             (
                 feat,
                 pre_other,
@@ -371,7 +393,7 @@
                 neigh_weight2,
                 cotangent,
                 targets_mine,
-                pack,
+                targets_other,
                 agg_mine,
                 agg_other,
             ),

time: 108 us -> 106 us (0.981)
  waiting for transfers between devices: 18.9 us -> 7.48 us
  blocking collectives: 26.4 us -> 37 us
    all_to_all x2 -> x1, waiting for transfers between devices: 15.1 us -> 0.01 us  [per_device(): lax.all_to_all(aggregate.reshape(owners, tgt_rows // block * columns, blo...]
    all_to_all x0 -> x1, blocking collectives: none -> 11 us  [per_device(): blocks = lax.all_to_all(blocks, NEAR, 0, 0, tiled=True)]
    ppermute x2 -> x4, starting transfers between devices: 5.46 us -> 13.9 us  [the longest x3 9.09 us: per_device(): lax.ppermute(sends[step], 'zl', [(i, (i + step) % near) for i in range(ne...]
    all_to_all x2 -> x1, starting transfers between devices: 14.3 us -> 7.72 us  [per_device(): lax.all_to_all(aggregate.reshape(owners, tgt_rows // block * columns, blo...]
    ppermute x2 -> x4, waiting for transfers between devices: 1.82 us -> 4.35 us  [the longest x3 3.47 us: per_device(): lax.ppermute(sends[step], 'zl', [(i, (i + step) % near) for i in range(ne...]
    ppermute x3, starting transfers between devices: 24.2 us -> 21.9 us  [per_device(): lax.ppermute(quarter, 'zh', [(i, (i + step) % far) for i in range(far)])]
    ppermute x3, waiting for transfers between devices: 1.37 us -> 2.47 us  [per_device(): lax.ppermute(quarter, 'zh', [(i, (i + step) % far) for i in range(far)])]
    pallas_call x9 -> x10, Pallas kernels: 9.09 us -> 8.36 us  [run(): pl.pallas_call(kernel, out_shape=shapes, in_specs=specs, out_specs=out_sp...]
  transfers between devices with their start and end apart: 8 -> 9, of which waited for: 6 -> 5; matrix products, arithmetic and copies ran while one was open for 0% -> 0% of each run, Pallas kernels for 2% -> 2%
where the time goes in v6:
time: 106 us
  starting transfers between devices  50.5 us (48%)
  blocking collectives  37 us (35%)
  Pallas kernels  8.36 us (8%)
  waiting for transfers between devices  7.48 us (7%)
  between operations  1.51 us (1%)
    ppermute x3, starting transfers between devices, per_device(): lax.ppermute(quarter, 'zh', [(i, (i + step) % far) for i in range(far)])  21.9 us
    all_to_all x1, blocking collectives, per_device(): grads = lax.all_to_all(grads, NODE, 0, 0, tiled=True)  17.7 us
    all_to_all x1, blocking collectives, per_device(): blocks = lax.all_to_all(blocks, NEAR, 0, 0, tiled=True)  11 us
    ppermute x3, starting transfers between devices, per_device(): lax.ppermute(sends[step], 'zl', [(i, (i + step) % near) for i in range(ne...  9.09 us
    all_to_all x1, blocking collectives, per_device(): pre_mine = lax.all_to_all(copies, 'zl', 0, 0, tiled=True)  8.36 us
    pallas_call x10, Pallas kernels, run(): pl.pallas_call(kernel, out_shape=shapes, in_specs=specs, out_specs=out_sp...  8.36 us
    all_to_all x1, starting transfers between devices, per_device(): lax.all_to_all(aggregate.reshape(owners, tgt_rows // block * columns, blo...  7.72 us
    ppermute x1, starting transfers between devices, per_device(): pre_other = lax.ppermute(pre_mine, 'c', swap)  6.86 us
  transfers between devices with their start and end apart: 9, of which 5 were waited for; matrix products, arithmetic and copies ran while one was open for 0% of the time, Pallas kernels for 2%

profile of v6, /device:TPU:1, one launch (start us, length us, event | category | flops | bytes accessed | tf_op | source)
XLA Modules:
  0.0 105.6 jit_solution(1563012214612256819)
XLA Ops:
  1.3 3.0 %aggregate_tiles.1 = bf16[128,32,128]{2,1,0:T(8,128)(2,1)} custom-call(s32[1,1]{1,0:T(1,128)} %bitcast.11.count_ref, s32[2,32]{1,0:T(2,128)} %bitcast.17, bf16[32,128,128]{2,1,0:T(8,128)(2,1)} %tiles_ref.1, bf16[32,1024]{1,0:T(8,128)(2,1)} %bitcast.16), custom_call_target="tpu_custom_call" | custom-call | bytes 2162948 | tf_op jit(solution)/shard_map/aggregate_tiles/pallas_call | solution.py:251
  4.3 0.0 copy-start.3
  4.3 0.0 copy-start.4
  4.3 0.0 copy-start.5
  4.3 7.7 %all-to-all-start = ((bf16[16,256,128]{2,1,0:T(8,128)(2,1)}), bf16[16,256,128]{2,1,0:T(8,128)(2,1)S(1)}, u32[]{:S(2)}, u32[]{:S(2)}) async-start(bf16[16,256,128]{2,1,0:T(8,128)(2,1)} %bitcast.15), calls=%async_computation | async-start | bytes 2097152 | tf_op jit(solution)/shard_map/aggregate_exchange/all_to_all | solution.py:308
  12.0 0.0 copy-done.3
  12.0 0.0 copy-done.4
  12.0 0.0 copy-done.5
  12.1 4.9 %collective-permute-start = (bf16[64,512]{1,0:T(8,128)(2,1)S(1)}, bf16[64,512]{1,0:T(8,128)(2,1)S(1)}, u32[]{:S(2)}, u32[]{:S(2)}) collective-permute-start(bf16[64,512]{1,0:T(8,128)(2,1)S(1)} %get-tuple-element.22.pack_ref), channel_id=1, source_target_pairs={{0,16},{16,0},{1,17},{17,1},{2,18},{18,2},{3,19},{19,3},{4,20},{20... | collective-permute-start | bytes 196616 | tf_op jit(solution)/shard_map/inputs_exchange/ppermute | solution.py:318
  16.9 0.9 collective-permute-done.arrived_ref
  17.8 1.9 %collective-permute-start.1 = (bf16[64,640]{1,0:T(8,128)(2,1)S(1)}, bf16[64,640]{1,0:T(8,128)(2,1)S(1)}, u32[]{:S(2)}, u32[]{:S(2)}) collective-permute-start(bf16[64,640]{1,0:T(8,128)(2,1)S(1)} %get-tuple-element.23), channel_id=1, source_target_pairs={{0,32},{32,64},{64,96},{96,0},{1,33},{33,65},{65,97},{97,1},{2,34}... | collective-permute-start | bytes 245768 | tf_op jit(solution)/shard_map/inputs_exchange/ppermute | solution.py:326
  19.8 4.5 %collective-permute-start.2 = (bf16[64,640]{1,0:T(8,128)(2,1)S(1)}, bf16[64,640]{1,0:T(8,128)(2,1)S(1)}, u32[]{:S(2)}, u32[]{:S(2)}) collective-permute-start(bf16[64,640]{1,0:T(8,128)(2,1)S(1)} %get-tuple-element.24), channel_id=1, source_target_pairs={{0,64},{32,96},{64,0},{96,32},{1,65},{33,97},{65,1},{97,33},{2,66}... | collective-permute-start | bytes 245768 | tf_op jit(solution)/shard_map/inputs_exchange/ppermute | solution.py:326
  24.3 2.6 %collective-permute-start.3 = (bf16[64,640]{1,0:T(8,128)(2,1)S(1)}, bf16[64,640]{1,0:T(8,128)(2,1)S(1)}, u32[]{:S(2)}, u32[]{:S(2)}) collective-permute-start(bf16[64,640]{1,0:T(8,128)(2,1)S(1)} %get-tuple-element.25), channel_id=1, source_target_pairs={{0,96},{32,0},{64,32},{96,64},{1,97},{33,1},{65,33},{97,65},{2,98}... | collective-permute-start | bytes 245768 | tf_op jit(solution)/shard_map/inputs_exchange/ppermute | solution.py:326
  27.0 0.0 collective-permute-done.1.one_ref.rest_1_
  27.0 2.3 %collective-permute-done.2.two_ref.rest_2_ = bf16[64,640]{1,0:T(8,128)(2,1)S(1)} collective-permute-done((bf16[64,640]{1,0:T(8,128)(2,1)S(1)}, bf16[64,640]{1,0:T(8,128)(2,1)S(1)}, u32[]{:S(2)}, u32[]{:S(2)}) %collective-permute-start.2) | collective-permute-done | bytes 81952 | tf_op jit(solution)/shard_map/inputs_exchange/ppermute | solution.py:326
  29.3 1.2 %collective-permute-done.3.three_ref.rest_3_ = bf16[64,640]{1,0:T(8,128)(2,1)S(1)} collective-permute-done((bf16[64,640]{1,0:T(8,128)(2,1)S(1)}, bf16[64,640]{1,0:T(8,128)(2,1)S(1)}, u32[]{:S(2)}, u32[]{:S(2)}) %collective-permute-start.3) | collective-permute-done | bytes 81952 | tf_op jit(solution)/shard_map/inputs_exchange/ppermute | solution.py:326
  30.4 0.0 all-to-all-done.parts_ref
  30.4 0.1 owned_sum.1
  30.6 11.0 %all_to_all.20.blocks_ref = bf16[8,32,128]{2,1,0:T(8,128)(2,1)S(1)} all-to-all(bf16[8,32,128]{2,1,0:T(8,128)(2,1)S(1)} %get-tuple-element.26), channel_id=1, replica_groups=mesh['zh'=4,'zl'=4,'c'=2,'x'=4,'y'=4] {'zl','c'}, dimensions={0} | all-to-all | bytes 131072 | tf_op jit(solution)/shard_map/near_exchange/all_to_all | solution.py:338
  41.6 0.0 copy-start.6
  41.6 0.2 partial_pre.1.own_ref
  41.8 12.8 %collective-permute-start.6 = (bf16[128,256]{1,0:T(8,128)(2,1)S(1)}, bf16[128,256]{1,0:T(8,128)(2,1)S(1)}, u32[]{:S(2)}, u32[]{:S(2)}) collective-permute-start(bf16[128,256]{1,0:T(8,128)(2,1)S(1)} %partial_pre.1.own_ref), channel_id=1, source_target_pairs={{0,256},{128,384},{256,0},{384,128},{1,257},{129,385},{257,1},{385... | collective-permute-start | bytes 196616 | tf_op jit(solution)/shard_map/pre_sum_far/ppermute | solution.py:360
  54.6 3.1 %collective-permute-start.5 = (bf16[128,256]{1,0:T(8,128)(2,1)S(1)}, bf16[128,256]{1,0:T(8,128)(2,1)S(1)}, u32[]{:S(2)}, u32[]{:S(2)}) collective-permute-start(bf16[128,256]{1,0:T(8,128)(2,1)S(1)} %partial_pre.1.own_ref), channel_id=1, source_target_pairs={{0,384},{128,0},{256,128},{384,256},{1,385},{129,1},{257,129},{385... | collective-permute-start | bytes 196616 | tf_op jit(solution)/shard_map/pre_sum_far/ppermute | solution.py:360
  57.6 6.1 %collective-permute-start.4 = (bf16[128,256]{1,0:T(8,128)(2,1)S(1)}, bf16[128,256]{1,0:T(8,128)(2,1)S(1)}, u32[]{:S(2)}, u32[]{:S(2)}) collective-permute-start(bf16[128,256]{1,0:T(8,128)(2,1)S(1)} %partial_pre.1.own_ref), channel_id=1, source_target_pairs={{0,128},{128,256},{256,384},{384,0},{1,129},{129,257},{257,385},{3... | collective-permute-start | bytes 196616 | tf_op jit(solution)/shard_map/pre_sum_far/ppermute | solution.py:360
  63.8 0.0 copy-start.7
  63.8 0.0 copy-done.6
  63.8 0.7 copy-done.7
  64.5 1.4 %picks.1 = (bf16[1024,512]{1,0:T(8,128)(2,1)S(1)}, bf16[512,1024]{1,0:T(8,128)(2,1)S(1)}) custom-call(s32[1]{0:T(128)} %bitcast.2.core_ref, s32[10,256]{1,0:T(8,128)S(1)} %bitcast.13, s32[1,256]{1,0:T(1,128)S(1)} %bitcast.14), custom_call_target="tpu_custom_call" | custom-call | flops 5242880 | bytes 2108420 | tf_op jit(solution)/shard_map/picks/pallas_call | solution.py:251
  65.9 0.0 collective-permute-done.6.two_ref
  65.9 2.5 %collective-permute-done.5.three_ref = bf16[128,256]{1,0:T(8,128)(2,1)S(1)} collective-permute-done((bf16[128,256]{1,0:T(8,128)(2,1)S(1)}, bf16[128,256]{1,0:T(8,128)(2,1)S(1)}, u32[]{:S(2)}, u32[]{:S(2)}) %collective-permute-start.5) | collective-permute-done | bytes 65568 | tf_op jit(solution)/shard_map/pre_sum_far/ppermute | solution.py:360
  68.4 0.0 collective-permute-done.4.one_ref
  68.4 0.1 pre_sum_far.1
  68.5 8.4 %all_to_all.21.pre_ref = bf16[4,128,256]{2,1,0:T(8,128)(2,1)S(1)} all-to-all(bf16[4,128,256]{2,1,0:T(8,128)(2,1)S(1)} %pre_sum_far.1), channel_id=1, replica_groups=mesh['zh'=4,'zl'=4,'c'=2,'x'=4,'y'=4] {'zl'}, dimensions={0} | all-to-all | bytes 524288 | tf_op jit(solution)/shard_map/pre_gather/all_to_all | solution.py:371
  76.8 6.9 %collective-permute-start.7 = (bf16[4,128,256]{2,1,0:T(8,128)(2,1)S(1)}, bf16[4,128,256]{2,1,0:T(8,128)(2,1)S(1)}, u32[]{:S(2)}, u32[]{:S(2)}) collective-permute-start(bf16[4,128,256]{2,1,0:T(8,128)(2,1)S(1)} %all_to_all.21.pre_ref), channel_id=1, source_target_pairs={{0,16},{16,0},{1,17},{17,1},{2,18},{18,2},{3,19},{19,3},{4,20},{20... | collective-permute-start | bytes 786440 | tf_op jit(solution)/shard_map/pre_gather/ppermute | solution.py:372
  83.7 0.0 copy-start
  83.7 0.0 copy-start.1
  83.7 0.0 copy-start.2
  83.7 0.4 step_mine.1
  84.2 0.7 collective-permute-done.7.pre_ref
  84.8 0.0 copy-done
  84.8 0.0 copy-done.1
  84.8 0.0 copy-done.2
  84.8 2.3 %step.1 = (bf16[256,256]{1,0:T(8,128)(2,1)}, bf16[16,80,256]{2,1,0:T(8,128)(2,1)S(1)}) custom-call(s32[1]{0:T(128)} %bitcast.feat_ref, bf16[4,128,256]{2,1,0:T(8,128)(2,1)S(1)} %collective-permute-done.7.pre_ref, f32[512,256]{1,0:T(8,128)S(1)} %get-tuple-element.29.gathered_ref, f32[512,256]{1,0:T(8,128)S(1)} %get-tuple-element.30.slope_ref, ...), custom_call_target="tpu_custom_call" | custom-call | bytes 4718596 | tf_op jit(solution)/shard_map/step/pallas_call | solution.py:251
  87.1 17.7 %all_to_all.22.parts_ref = bf16[16,80,256]{2,1,0:T(8,128)(2,1)S(1)} all-to-all(bf16[16,80,256]{2,1,0:T(8,128)(2,1)S(1)} %get-tuple-element.36), channel_id=1, replica_groups=mesh['zh'=4,'zl'=4,'c'=2,'x'=4,'y'=4] {'x','y'}, dimensions={0} | all-to-all | bytes 1310720 | tf_op jit(solution)/shard_map/grad_sum/all_to_all | solution.py:410
  104.9 0.7 grad_sum.1
  (2 shorter events, 0.1 us)
Async XLA Ops:
  4.3 7.7 %copy-start.3 = (bf16[1024,32]{0,1:T(8,128)(2,1)S(1)}, bf16[1024,32]{0,1:T(8,128)(2,1)}, u32[]{:S(2)}) copy-start(bf16[1024,32]{0,1:T(8,128)(2,1)} %param.13) | copy-start | bytes 196612
  4.3 7.8 %copy-start.4 = (bf16[32,256]{1,0:T(8,128)(2,1)S(1)}, bf16[32,256]{1,0:T(8,128)(2,1)}, u32[]{:S(2)}) copy-start(bf16[32,256]{1,0:T(8,128)(2,1)} %self_ref.2) | copy-start | bytes 49156
  4.3 7.8 %copy-start.5 = (bf16[32,256]{1,0:T(8,128)(2,1)S(1)}, bf16[32,256]{1,0:T(8,128)(2,1)}, u32[]{:S(2)}) copy-start(bf16[32,256]{1,0:T(8,128)(2,1)} %neigh_ref.2) | copy-start | bytes 49156
  4.3 26.2 %all-to-all-start = ((bf16[16,256,128]{2,1,0:T(8,128)(2,1)}), bf16[16,256,128]{2,1,0:T(8,128)(2,1)S(1)}, u32[]{:S(2)}, u32[]{:S(2)}) async-start(bf16[16,256,128]{2,1,0:T(8,128)(2,1)} %bitcast.15), calls=%async_computation | async-start | bytes 2097152 | tf_op jit(solution)/shard_map/aggregate_exchange/all_to_all | solution.py:308
  12.1 5.7 %collective-permute-start = (bf16[64,512]{1,0:T(8,128)(2,1)S(1)}, bf16[64,512]{1,0:T(8,128)(2,1)S(1)}, u32[]{:S(2)}, u32[]{:S(2)}) collective-permute-start(bf16[64,512]{1,0:T(8,128)(2,1)S(1)} %get-tuple-element.22.pack_ref), channel_id=1, source_target_pairs={{0,16},{16,0},{1,17},{17,1},{2,18},{18,2},{3,19},{19,3},{4,20},{20... | collective-permute-start | bytes 196616 | tf_op jit(solution)/shard_map/inputs_exchange/ppermute | solution.py:318
  17.8 9.1 %collective-permute-start.1 = (bf16[64,640]{1,0:T(8,128)(2,1)S(1)}, bf16[64,640]{1,0:T(8,128)(2,1)S(1)}, u32[]{:S(2)}, u32[]{:S(2)}) collective-permute-start(bf16[64,640]{1,0:T(8,128)(2,1)S(1)} %get-tuple-element.23), channel_id=1, source_target_pairs={{0,32},{32,64},{64,96},{96,0},{1,33},{33,65},{65,97},{97,1},{2,34}... | collective-permute-start | bytes 245768 | tf_op jit(solution)/shard_map/inputs_exchange/ppermute | solution.py:326
  19.8 9.5 %collective-permute-start.2 = (bf16[64,640]{1,0:T(8,128)(2,1)S(1)}, bf16[64,640]{1,0:T(8,128)(2,1)S(1)}, u32[]{:S(2)}, u32[]{:S(2)}) collective-permute-start(bf16[64,640]{1,0:T(8,128)(2,1)S(1)} %get-tuple-element.24), channel_id=1, source_target_pairs={{0,64},{32,96},{64,0},{96,32},{1,65},{33,97},{65,1},{97,33},{2,66}... | collective-permute-start | bytes 245768 | tf_op jit(solution)/shard_map/inputs_exchange/ppermute | solution.py:326
  24.3 6.1 %collective-permute-start.3 = (bf16[64,640]{1,0:T(8,128)(2,1)S(1)}, bf16[64,640]{1,0:T(8,128)(2,1)S(1)}, u32[]{:S(2)}, u32[]{:S(2)}) collective-permute-start(bf16[64,640]{1,0:T(8,128)(2,1)S(1)} %get-tuple-element.25), channel_id=1, source_target_pairs={{0,96},{32,0},{64,32},{96,64},{1,97},{33,1},{65,33},{97,65},{2,98}... | collective-permute-start | bytes 245768 | tf_op jit(solution)/shard_map/inputs_exchange/ppermute | solution.py:326
  41.6 22.2 %copy-start.6 = (s32[256,10]{0,1:T(8,128)S(1)}, s32[256,10]{0,1:T(8,128)}, u32[]{:S(2)}) copy-start(s32[256,10]{0,1:T(8,128)} %param.21) | copy-start | bytes 30724
  41.8 24.1 %collective-permute-start.6 = (bf16[128,256]{1,0:T(8,128)(2,1)S(1)}, bf16[128,256]{1,0:T(8,128)(2,1)S(1)}, u32[]{:S(2)}, u32[]{:S(2)}) collective-permute-start(bf16[128,256]{1,0:T(8,128)(2,1)S(1)} %partial_pre.1.own_ref), channel_id=1, source_target_pairs={{0,256},{128,384},{256,0},{384,128},{1,257},{129,385},{257,1},{385... | collective-permute-start | bytes 196616 | tf_op jit(solution)/shard_map/pre_sum_far/ppermute | solution.py:360
  54.6 13.8 %collective-permute-start.5 = (bf16[128,256]{1,0:T(8,128)(2,1)S(1)}, bf16[128,256]{1,0:T(8,128)(2,1)S(1)}, u32[]{:S(2)}, u32[]{:S(2)}) collective-permute-start(bf16[128,256]{1,0:T(8,128)(2,1)S(1)} %partial_pre.1.own_ref), channel_id=1, source_target_pairs={{0,384},{128,0},{256,128},{384,256},{1,385},{129,1},{257,129},{385... | collective-permute-start | bytes 196616 | tf_op jit(solution)/shard_map/pre_sum_far/ppermute | solution.py:360
  57.6 10.7 %collective-permute-start.4 = (bf16[128,256]{1,0:T(8,128)(2,1)S(1)}, bf16[128,256]{1,0:T(8,128)(2,1)S(1)}, u32[]{:S(2)}, u32[]{:S(2)}) collective-permute-start(bf16[128,256]{1,0:T(8,128)(2,1)S(1)} %partial_pre.1.own_ref), channel_id=1, source_target_pairs={{0,128},{128,256},{256,384},{384,0},{1,129},{129,257},{257,385},{3... | collective-permute-start | bytes 196616 | tf_op jit(solution)/shard_map/pre_sum_far/ppermute | solution.py:360
  63.8 0.7 copy-start.7
  76.8 8.0 %collective-permute-start.7 = (bf16[4,128,256]{2,1,0:T(8,128)(2,1)S(1)}, bf16[4,128,256]{2,1,0:T(8,128)(2,1)S(1)}, u32[]{:S(2)}, u32[]{:S(2)}) collective-permute-start(bf16[4,128,256]{2,1,0:T(8,128)(2,1)S(1)} %all_to_all.21.pre_ref), channel_id=1, source_target_pairs={{0,16},{16,0},{1,17},{17,1},{2,18},{18,2},{3,19},{19,3},{4,20},{20... | collective-permute-start | bytes 786440 | tf_op jit(solution)/shard_map/pre_gather/ppermute | solution.py:372
  83.7 1.1 %copy-start = (bf16[256,256]{1,0:T(8,128)(2,1)S(1)}, bf16[256,256]{1,0:T(8,128)(2,1)}, u32[]{:S(2)}) copy-start(bf16[256,256]{1,0:T(8,128)(2,1)} %self_ref.3) | copy-start | bytes 393220
  83.7 1.1 %copy-start.1 = (bf16[256,256]{1,0:T(8,128)(2,1)S(1)}, bf16[256,256]{1,0:T(8,128)(2,1)}, u32[]{:S(2)}) copy-start(bf16[256,256]{1,0:T(8,128)(2,1)} %neigh_ref.3) | copy-start | bytes 393220
  83.7 1.1 %copy-start.2 = (bf16[256,256]{1,0:T(8,128)(2,1)S(1)}, bf16[256,256]{1,0:T(8,128)(2,1)}, u32[]{:S(2)}) copy-start(bf16[256,256]{1,0:T(8,128)(2,1)} %cotangent_ref.1) | copy-start | bytes 393220

commit v7 on v6

--- a/solution.py
+++ b/solution.py
@@ -54,60 +54,37 @@
         other_ref[:, span] = halves[position, 1 - core]
 
 
-def pack_kernel(core_ref, targets_ref, self_ref, neigh_ref, pack_ref, mine_ref, other_ref, halves):
+def owned_kernel(
+    core_ref, parts_ref, targets_ref, weights_ref, blocks_ref, tmine_ref, tother_ref, mine_ref, other_ref, halves
+):
     near, _, columns, block = halves.shape
     for position in range(2 * near):
-        halves[position // 2, position % 2] = targets_ref[:, position * block : (position + 1) * block]
-    split_blocks(core_ref[0], halves, mine_ref, other_ref)
-    hsize = self_ref.shape[1]
-    pack_ref[:columns] = other_ref[...]
-    pack_ref[columns:, :hsize] = self_ref[...]
-    pack_ref[columns:, hsize:] = neigh_ref[...]
-
-
-def pieces_kernel(near_ref, targets_ref, pack_ref, arrived_ref, *rest):
-    piece_refs, pieces = rest[:-1], rest[-1]
-    near, columns, block = pieces.shape[0], targets_ref.shape[0], pieces.shape[2]
-    for position in range(near):
-        span = slice(position * block, (position + 1) * block)
-        pieces[position, :columns] = targets_ref[:, span]
-        pieces[position, columns:] = arrived_ref[:columns, span]
-    for step, ref in enumerate(piece_refs):
-        ref[:, :block] = pieces[(near_ref[0] + step) & (near - 1)]
-        ref[:columns, block:] = pack_ref[columns:]
-        ref[columns:, block:] = arrived_ref[columns:]
-
-
-def owned_kernel(core_ref, parts_ref, one_ref, two_ref, three_ref, blocks_ref, mine_ref, other_ref, halves):
-    near, _, columns, _ = halves.shape
+        piece = targets_ref[:, position * block : (position + 1) * block]
+        blocks_ref[position, :columns] = piece
+        halves[position // 2, position % 2] = piece
+    split_blocks(core_ref[0], halves, tmine_ref, tother_ref)
     for position in range(2 * near):
         span = slice(position * columns, (position + 1) * columns)
-        block = parts_ref[0, span].astype(F32)
+        total = parts_ref[0, span].astype(F32)
         for source in range(1, parts_ref.shape[0]):
-            block += parts_ref[source, span].astype(F32)
-        block = block.astype(BF16)
-        blocks_ref[position] = block
-        halves[position // 2, position % 2] = block
+            total += parts_ref[source, span].astype(F32)
+        total = total.astype(BF16)
+        blocks_ref[position, columns:] = total
+        halves[position // 2, position % 2] = total
     split_blocks(core_ref[0], halves, mine_ref, other_ref)
 
 
-def partial_kernel(core_ref, near_ref, blocks_ref, *rest):
-    piece_refs, (out_ref, inputs, weights, sides) = rest[:-4], rest[-4:]
-    group, columns, block = blocks_ref.shape
-    near, hsize = len(piece_refs), out_ref.shape[1]
-    core = core_ref[0]
-    for step, ref in enumerate(piece_refs):
-        span = slice(step * 2 * columns, (step + 1) * 2 * columns)
-        inputs[span] = ref[:, :block]
-        weights[span] = ref[:, block : block + hsize]
-        source = (near_ref[0] + near - step) & (near - 1)
-        sides[source, core] = ref[:columns, block + hsize :]
-        sides[source, 1 - core] = ref[columns:, block + hsize :]
+def partial_kernel(blocks_ref, weights_ref, out_ref, inputs):
+    group, rows, _ = blocks_ref.shape
+    columns, hsize = rows // 2, out_ref.shape[1]
+    depth = group * columns
     for position in range(group):
-        span = slice((group + position) * columns, (group + position + 1) * columns)
-        inputs[span] = blocks_ref[position]
-        weights[span] = sides[position // 2, position % 2]
-    out_ref[...] = contract(inputs[...], weights[...], 0, 0).astype(BF16)
+        first = position * columns
+        inputs[first : first + columns] = blocks_ref[position, :columns]
+        inputs[depth + first : depth + first + columns] = blocks_ref[position, columns:]
+    total = contract(inputs[:depth], weights_ref[:, :hsize], 0, 0)
+    total += contract(inputs[depth:], weights_ref[:, hsize:], 0, 0)
+    out_ref[...] = total.astype(BF16)
 
 
 def far_kernel(far_ref, own_ref, one_ref, three_ref, two_ref, picks_ref, out_ref, slots):
@@ -200,10 +177,8 @@
         [contract(slope_two, neigh_ref[...], 1, 1) / FAN, contract(slope_two, self_ref[...], 1, 1)],
         axis=0,
     )
-    back_high = back.astype(BF16)
-    back_low = (back - back_high.astype(F32)).astype(BF16)
     spread = spread_ref[...]
-    back_hidden = contract(spread, back_high, 1, 0) + contract(spread, back_low, 1, 0)
+    back_hidden = contract(spread, back.astype(BF16), 1, 0)
     slope_one = jnp.concatenate(
         [
             (back_hidden[:half] * slope_ref[...]).astype(BF16),
@@ -288,7 +263,6 @@
     core = lax.axis_index("c").reshape(1)
     feat = lax.axis_index(FEAT).reshape(1)
     halves = pltpu.VMEM((near, 2, columns, block), BF16)
-    position = lax.axis_index("zl").reshape(1)
     swap = [(0, 1), (1, 0)]
 
     with jax.named_scope("aggregate_tiles"):
@@ -308,31 +282,16 @@
         parts = lax.all_to_all(
             aggregate.reshape(owners, tgt_rows // block * columns, block), NODE, 0, 0, tiled=True
         )
-    with jax.named_scope("inputs_exchange"):
-        pack, targets_mine, targets_other = run(
-            pack_kernel,
-            [((2 * columns, half), BF16), ((columns, half), BF16), ((columns, half), BF16)],
-            (core, target_feats.T, self_weight1, neigh_weight1),
+    with jax.named_scope("weights_gather"):
+        weights = jnp.concatenate([self_weight1, neigh_weight1], axis=1)
+        weights = lax.all_gather(weights, NEAR, tiled=True)
+    with jax.named_scope("owned_sum"):
+        blocks, targets_mine, targets_other, agg_mine, agg_other = run(
+            owned_kernel,
+            [((2 * near, 2 * columns, block), BF16)] + [((columns, half), BF16)] * 4,
+            (core, parts, target_feats.T, weights),
             [halves],
-        )
-        arrived = lax.ppermute(pack, "c", swap)
-        sends = run(
-            pieces_kernel,
-            [((2 * columns, block + 2 * hsize), BF16)] * near,
-            (position, targets_mine, pack, arrived),
-            [pltpu.VMEM((near, 2 * columns, block), BF16)],
-        )
-        pieces = [sends[0]] + [
-            lax.ppermute(sends[step], "zl", [(i, (i + step) % near) for i in range(near)])
-            for step in range(1, near)
-        ]
-    with jax.named_scope("owned_sum"):
-        blocks, agg_mine, agg_other = run(
-            owned_kernel,
-            [((2 * near, columns, block), BF16), ((columns, half), BF16), ((columns, half), BF16)],
-            (core, parts, *pieces[1:]),
-            [halves],
-            specs=[SMEM, VMEM] + [ANY] * (near - 1),
+            specs=[SMEM, VMEM, VMEM, ANY],
         )
     with jax.named_scope("near_exchange"):
         blocks = lax.all_to_all(blocks, NEAR, 0, 0, tiled=True)
@@ -340,12 +299,8 @@
         quarter = run(
             partial_kernel,
             [((span, hsize), BF16)],
-            (core, position, blocks, *pieces),
-            [
-                pltpu.VMEM((4 * near * columns, span), BF16),
-                pltpu.VMEM((4 * near * columns, hsize), BF16),
-                pltpu.VMEM((near, 2, columns, hsize), BF16),
-            ],
+            (blocks, weights),
+            [pltpu.VMEM((4 * near * columns, span), BF16)],
         )
     with jax.named_scope("picks"):
         spread, pick = run(

time: 106 us -> 105 us (level)
  blocking collectives: 37 us -> 53.9 us
  starting transfers between devices: 50.5 us -> 37.1 us
  waiting for transfers between devices: 7.48 us -> 3.11 us
    all_gather x0 -> x1, blocking collectives: none -> 17.1 us  [per_device(): weights = lax.all_gather(weights, NEAR, tiled=True)]
    ppermute x4 -> x0, starting transfers between devices: 13.9 us -> none  [the longest x3 9.09 us: per_device(): lax.ppermute(sends[step], 'zl', [(i, (i + step) % near) for i in range(ne...]
    ppermute x4 -> x0, waiting for transfers between devices: 4.35 us -> none  [the longest x3 3.47 us: per_device(): lax.ppermute(sends[step], 'zl', [(i, (i + step) % near) for i in range(ne...]
    all_to_all x1, blocking collectives: 17.7 us -> 15.4 us  [per_device(): grads = lax.all_to_all(grads, NODE, 0, 0, tiled=True)]
    all_to_all x1, blocking collectives: 11 us -> 13 us  [per_device(): blocks = lax.all_to_all(blocks, NEAR, 0, 0, tiled=True)]
    pallas_call x10 -> x8, Pallas kernels: 8.36 us -> 7.97 us  [run(): pl.pallas_call(kernel, out_shape=shapes, in_specs=specs, out_specs=out_sp...]
  transfers between devices with their start and end apart: 9 -> 5, of which waited for: 5 -> 2; matrix products, arithmetic and copies ran while one was open for 0% -> 0% of each run, Pallas kernels for 2% -> 2%
where the time goes in v7:
time: 105 us; the launch traced here: 104 us
  blocking collectives  53.9 us (51%)
  starting transfers between devices  37.1 us (35%)
  Pallas kernels  7.97 us (8%)
  waiting for transfers between devices  3.11 us (3%)
  between operations  1.46 us (1%)
    ppermute x3, starting transfers between devices, per_device(): lax.ppermute(quarter, 'zh', [(i, (i + step) % far) for i in range(far)])  21.9 us
    all_gather x1, blocking collectives, per_device(): weights = lax.all_gather(weights, NEAR, tiled=True)  17.1 us
    all_to_all x1, blocking collectives, per_device(): grads = lax.all_to_all(grads, NODE, 0, 0, tiled=True)  15.4 us
    all_to_all x1, blocking collectives, per_device(): blocks = lax.all_to_all(blocks, NEAR, 0, 0, tiled=True)  13 us
    all_to_all x1, blocking collectives, per_device(): pre_mine = lax.all_to_all(copies, 'zl', 0, 0, tiled=True)  8.36 us
    pallas_call x8, Pallas kernels, run(): pl.pallas_call(kernel, out_shape=shapes, in_specs=specs, out_specs=out_sp...  7.97 us
    all_to_all x1, starting transfers between devices, per_device(): lax.all_to_all(aggregate.reshape(owners, tgt_rows // block * columns, blo...  7.72 us
    ppermute x1, starting transfers between devices, per_device(): pre_other = lax.ppermute(pre_mine, 'c', swap)  7.48 us
  transfers between devices with their start and end apart: 5, of which 2 were waited for; matrix products, arithmetic and copies ran while one was open for 0% of the time, Pallas kernels for 2%

profile of v7, /device:TPU:1, one launch (start us, length us, event | category | flops | bytes accessed | tf_op | source)
XLA Modules:
  0.0 104.2 jit_solution(11513437281890923063)
XLA Ops:
  1.3 3.0 %aggregate_tiles.1 = bf16[128,32,128]{2,1,0:T(8,128)(2,1)} custom-call(s32[1,1]{1,0:T(1,128)} %bitcast.10.count_ref, s32[2,32]{1,0:T(2,128)} %bitcast.16, bf16[32,128,128]{2,1,0:T(8,128)(2,1)} %tiles_ref.1, bf16[32,1024]{1,0:T(8,128)(2,1)} %bitcast.15), custom_call_target="tpu_custom_call" | custom-call | bytes 2162948 | tf_op jit(solution)/shard_map/aggregate_tiles/pallas_call | solution.py:226
  4.2 0.0 copy-start.6
  4.2 0.0 copy-start.7
  4.2 7.7 %all-to-all-start = ((bf16[16,256,128]{2,1,0:T(8,128)(2,1)}), bf16[16,256,128]{2,1,0:T(8,128)(2,1)S(1)}, u32[]{:S(2)}, u32[]{:S(2)}) async-start(bf16[16,256,128]{2,1,0:T(8,128)(2,1)} %bitcast.14), calls=%async_computation | async-start | bytes 2097152 | tf_op jit(solution)/shard_map/aggregate_exchange/all_to_all | solution.py:282
  12.0 0.0 copy-done.6
  12.0 0.0 copy-done.7
  12.0 0.0 copy-start.3
  12.0 17.1 %all_gather.3.weights_ref = bf16[256,512]{1,0:T(8,128)(2,1)S(1)} all-gather(bf16[32,512]{1,0:T(8,128)(2,1)S(1)} %pad_maximum_fusion), channel_id=1, replica_groups=mesh['zh'=4,'zl'=4,'c'=2,'x'=4,'y'=4] {'zl','c'}, dimensions={0}, use_global_device_ids=true | all-gather | bytes 294912 | tf_op jit(solution)/shard_map/weights_gather/all_gather | solution.py:287
  29.2 0.0 all-to-all-done.parts_ref
  29.2 0.0 copy-done.3
  29.2 0.2 owned_sum.1
  29.3 13.0 %all_to_all.20.blocks_ref = bf16[8,64,128]{2,1,0:T(8,128)(2,1)S(1)} all-to-all(bf16[8,64,128]{2,1,0:T(8,128)(2,1)S(1)} %get-tuple-element.16), channel_id=1, replica_groups=mesh['zh'=4,'zl'=4,'c'=2,'x'=4,'y'=4] {'zl','c'}, dimensions={0} | all-to-all | bytes 262144 | tf_op jit(solution)/shard_map/near_exchange/all_to_all | solution.py:297
  42.3 0.0 copy-start.4
  42.3 0.2 partial_pre.1.own_ref
  42.5 12.7 %collective-permute-start.2 = (bf16[128,256]{1,0:T(8,128)(2,1)S(1)}, bf16[128,256]{1,0:T(8,128)(2,1)S(1)}, u32[]{:S(2)}, u32[]{:S(2)}) collective-permute-start(bf16[128,256]{1,0:T(8,128)(2,1)S(1)} %partial_pre.1.own_ref), channel_id=1, source_target_pairs={{0,256},{128,384},{256,0},{384,128},{1,257},{129,385},{257,1},{385... | collective-permute-start | bytes 196616 | tf_op jit(solution)/shard_map/pre_sum_far/ppermute | solution.py:315
  55.3 3.1 %collective-permute-start.1 = (bf16[128,256]{1,0:T(8,128)(2,1)S(1)}, bf16[128,256]{1,0:T(8,128)(2,1)S(1)}, u32[]{:S(2)}, u32[]{:S(2)}) collective-permute-start(bf16[128,256]{1,0:T(8,128)(2,1)S(1)} %partial_pre.1.own_ref), channel_id=1, source_target_pairs={{0,384},{128,0},{256,128},{384,256},{1,385},{129,1},{257,129},{385... | collective-permute-start | bytes 196616 | tf_op jit(solution)/shard_map/pre_sum_far/ppermute | solution.py:315
  58.4 6.1 %collective-permute-start = (bf16[128,256]{1,0:T(8,128)(2,1)S(1)}, bf16[128,256]{1,0:T(8,128)(2,1)S(1)}, u32[]{:S(2)}, u32[]{:S(2)}) collective-permute-start(bf16[128,256]{1,0:T(8,128)(2,1)S(1)} %partial_pre.1.own_ref), channel_id=1, source_target_pairs={{0,128},{128,256},{256,384},{384,0},{1,129},{129,257},{257,385},{3... | collective-permute-start | bytes 196616 | tf_op jit(solution)/shard_map/pre_sum_far/ppermute | solution.py:315
  64.5 0.0 copy-start.5
  64.5 0.0 copy-done.4
  64.5 0.7 copy-done.5
  65.2 1.4 %picks.1 = (bf16[1024,512]{1,0:T(8,128)(2,1)S(1)}, bf16[512,1024]{1,0:T(8,128)(2,1)S(1)}) custom-call(s32[1]{0:T(128)} %bitcast.2.core_ref, s32[10,256]{1,0:T(8,128)S(1)} %bitcast.12, s32[1,256]{1,0:T(1,128)S(1)} %bitcast.13), custom_call_target="tpu_custom_call" | custom-call | flops 5242880 | bytes 2108420 | tf_op jit(solution)/shard_map/picks/pallas_call | solution.py:226
  66.6 0.0 collective-permute-done.2.two_ref
  66.6 2.4 %collective-permute-done.1.three_ref = bf16[128,256]{1,0:T(8,128)(2,1)S(1)} collective-permute-done((bf16[128,256]{1,0:T(8,128)(2,1)S(1)}, bf16[128,256]{1,0:T(8,128)(2,1)S(1)}, u32[]{:S(2)}, u32[]{:S(2)}) %collective-permute-start.1) | collective-permute-done | bytes 65568 | tf_op jit(solution)/shard_map/pre_sum_far/ppermute | solution.py:315
  69.1 0.0 collective-permute-done.one_ref
  69.1 0.1 pre_sum_far.1
  69.2 8.4 %all_to_all.21.pre_ref = bf16[4,128,256]{2,1,0:T(8,128)(2,1)S(1)} all-to-all(bf16[4,128,256]{2,1,0:T(8,128)(2,1)S(1)} %pre_sum_far.1), channel_id=1, replica_groups=mesh['zh'=4,'zl'=4,'c'=2,'x'=4,'y'=4] {'zl'}, dimensions={0} | all-to-all | bytes 524288 | tf_op jit(solution)/shard_map/pre_gather/all_to_all | solution.py:326
  77.5 7.5 %collective-permute-start.3 = (bf16[4,128,256]{2,1,0:T(8,128)(2,1)S(1)}, bf16[4,128,256]{2,1,0:T(8,128)(2,1)S(1)}, u32[]{:S(2)}, u32[]{:S(2)}) collective-permute-start(bf16[4,128,256]{2,1,0:T(8,128)(2,1)S(1)} %all_to_all.21.pre_ref), channel_id=1, source_target_pairs={{0,16},{16,0},{1,17},{17,1},{2,18},{18,2},{3,19},{19,3},{4,20},{20... | collective-permute-start | bytes 786440 | tf_op jit(solution)/shard_map/pre_gather/ppermute | solution.py:327
  85.0 0.0 copy-start
  85.0 0.0 copy-start.1
  85.0 0.0 copy-start.2
  85.1 0.4 step_mine.1
  85.5 0.7 collective-permute-done.3.pre_ref
  86.1 0.0 copy-done
  86.1 0.0 copy-done.1
  86.2 0.0 copy-done.2
  86.2 2.0 %step.1 = (bf16[256,256]{1,0:T(8,128)(2,1)}, bf16[16,80,256]{2,1,0:T(8,128)(2,1)S(1)}) custom-call(s32[1]{0:T(128)} %bitcast.feat_ref, bf16[4,128,256]{2,1,0:T(8,128)(2,1)S(1)} %collective-permute-done.3.pre_ref, f32[512,256]{1,0:T(8,128)S(1)} %get-tuple-element.18.gathered_ref, f32[512,256]{1,0:T(8,128)S(1)} %get-tuple-element.19.slope_ref, ...), custom_call_target="tpu_custom_call" | custom-call | bytes 4718596 | tf_op jit(solution)/shard_map/step/pallas_call | solution.py:226
  88.1 15.4 %all_to_all.22.parts_ref = bf16[16,80,256]{2,1,0:T(8,128)(2,1)S(1)} all-to-all(bf16[16,80,256]{2,1,0:T(8,128)(2,1)S(1)} %get-tuple-element.26), channel_id=1, replica_groups=mesh['zh'=4,'zl'=4,'c'=2,'x'=4,'y'=4] {'x','y'}, dimensions={0} | all-to-all | bytes 1310720 | tf_op jit(solution)/shard_map/grad_sum/all_to_all | solution.py:365
  103.5 0.7 grad_sum.1
  (1 shorter events, 0.0 us)
Async XLA Ops:
  4.2 7.7 %copy-start.6 = (bf16[32,256]{1,0:T(8,128)(2,1)S(1)}, bf16[32,256]{1,0:T(8,128)(2,1)}, u32[]{:S(2)}) copy-start(bf16[32,256]{1,0:T(8,128)(2,1)} %param.18) | copy-start | bytes 49156
  4.2 7.7 %copy-start.7 = (bf16[32,256]{1,0:T(8,128)(2,1)S(1)}, bf16[32,256]{1,0:T(8,128)(2,1)}, u32[]{:S(2)}) copy-start(bf16[32,256]{1,0:T(8,128)(2,1)} %param.17) | copy-start | bytes 49156
  4.2 24.9 %all-to-all-start = ((bf16[16,256,128]{2,1,0:T(8,128)(2,1)}), bf16[16,256,128]{2,1,0:T(8,128)(2,1)S(1)}, u32[]{:S(2)}, u32[]{:S(2)}) async-start(bf16[16,256,128]{2,1,0:T(8,128)(2,1)} %bitcast.14), calls=%async_computation | async-start | bytes 2097152 | tf_op jit(solution)/shard_map/aggregate_exchange/all_to_all | solution.py:282
  12.0 17.1 %copy-start.3 = (bf16[1024,32]{0,1:T(8,128)(2,1)S(1)}, bf16[1024,32]{0,1:T(8,128)(2,1)}, u32[]{:S(2)}) copy-start(bf16[1024,32]{0,1:T(8,128)(2,1)} %param.13) | copy-start | bytes 196612
  42.3 22.2 %copy-start.4 = (s32[256,10]{0,1:T(8,128)S(1)}, s32[256,10]{0,1:T(8,128)}, u32[]{:S(2)}) copy-start(s32[256,10]{0,1:T(8,128)} %param.21) | copy-start | bytes 30724
  42.5 24.1 %collective-permute-start.2 = (bf16[128,256]{1,0:T(8,128)(2,1)S(1)}, bf16[128,256]{1,0:T(8,128)(2,1)S(1)}, u32[]{:S(2)}, u32[]{:S(2)}) collective-permute-start(bf16[128,256]{1,0:T(8,128)(2,1)S(1)} %partial_pre.1.own_ref), channel_id=1, source_target_pairs={{0,256},{128,384},{256,0},{384,128},{1,257},{129,385},{257,1},{385... | collective-permute-start | bytes 196616 | tf_op jit(solution)/shard_map/pre_sum_far/ppermute | solution.py:315
  55.3 13.8 %collective-permute-start.1 = (bf16[128,256]{1,0:T(8,128)(2,1)S(1)}, bf16[128,256]{1,0:T(8,128)(2,1)S(1)}, u32[]{:S(2)}, u32[]{:S(2)}) collective-permute-start(bf16[128,256]{1,0:T(8,128)(2,1)S(1)} %partial_pre.1.own_ref), channel_id=1, source_target_pairs={{0,384},{128,0},{256,128},{384,256},{1,385},{129,1},{257,129},{385... | collective-permute-start | bytes 196616 | tf_op jit(solution)/shard_map/pre_sum_far/ppermute | solution.py:315
  58.4 10.7 %collective-permute-start = (bf16[128,256]{1,0:T(8,128)(2,1)S(1)}, bf16[128,256]{1,0:T(8,128)(2,1)S(1)}, u32[]{:S(2)}, u32[]{:S(2)}) collective-permute-start(bf16[128,256]{1,0:T(8,128)(2,1)S(1)} %partial_pre.1.own_ref), channel_id=1, source_target_pairs={{0,128},{128,256},{256,384},{384,0},{1,129},{129,257},{257,385},{3... | collective-permute-start | bytes 196616 | tf_op jit(solution)/shard_map/pre_sum_far/ppermute | solution.py:315
  64.5 0.7 copy-start.5
  77.5 8.6 %collective-permute-start.3 = (bf16[4,128,256]{2,1,0:T(8,128)(2,1)S(1)}, bf16[4,128,256]{2,1,0:T(8,128)(2,1)S(1)}, u32[]{:S(2)}, u32[]{:S(2)}) collective-permute-start(bf16[4,128,256]{2,1,0:T(8,128)(2,1)S(1)} %all_to_all.21.pre_ref), channel_id=1, source_target_pairs={{0,16},{16,0},{1,17},{17,1},{2,18},{18,2},{3,19},{19,3},{4,20},{20... | collective-permute-start | bytes 786440 | tf_op jit(solution)/shard_map/pre_gather/ppermute | solution.py:327
  85.0 1.1 %copy-start = (bf16[256,256]{1,0:T(8,128)(2,1)S(1)}, bf16[256,256]{1,0:T(8,128)(2,1)}, u32[]{:S(2)}) copy-start(bf16[256,256]{1,0:T(8,128)(2,1)} %self_ref.1) | copy-start | bytes 393220
  85.0 1.1 %copy-start.1 = (bf16[256,256]{1,0:T(8,128)(2,1)S(1)}, bf16[256,256]{1,0:T(8,128)(2,1)}, u32[]{:S(2)}) copy-start(bf16[256,256]{1,0:T(8,128)(2,1)} %neigh_ref.1) | copy-start | bytes 393220
  85.0 1.1 %copy-start.2 = (bf16[256,256]{1,0:T(8,128)(2,1)S(1)}, bf16[256,256]{1,0:T(8,128)(2,1)}, u32[]{:S(2)}) copy-start(bf16[256,256]{1,0:T(8,128)(2,1)} %cotangent_ref.1) | copy-start | bytes 393220

commit v8 on v7

--- a/solution.py
+++ b/solution.py
@@ -87,16 +87,13 @@
     out_ref[...] = total.astype(BF16)
 
 
-def far_kernel(far_ref, own_ref, one_ref, three_ref, two_ref, picks_ref, out_ref, slots):
-    far = far_ref[0]
-    slots[far] = own_ref[...].astype(F32)
-    for step, ref in ((2, two_ref), (1, one_ref), (3, three_ref)):
-        slots[lax.rem(far + slots.shape[0] - step, slots.shape[0])] = ref[...].astype(F32)
-    total = slots[0]
-    for position in range(1, slots.shape[0]):
-        total += slots[position]
+def far_kernel(parts_ref, picks_ref, out_ref):
+    total = parts_ref[0].astype(F32)
+    for position in range(1, parts_ref.shape[0]):
+        total += parts_ref[position].astype(F32)
+    total = total.astype(BF16)
     for position in range(out_ref.shape[0]):
-        out_ref[position] = total.astype(BF16)
+        out_ref[position] = total
 
 
 def picks_kernel(core_ref, neighbors_ref, seeds_ref, spread_ref, pick_ref):
@@ -311,16 +308,12 @@
             flops=20 * tgt_rows * seeds,
         )
     with jax.named_scope("pre_sum_far"):
-        arrived = [
-            lax.ppermute(quarter, "zh", [(i, (i + step) % far) for i in range(far)])
-            for step in (1, 3, 2)
-        ]
+        parts = lax.all_gather(quarter, "zh")
         copies = run(
             far_kernel,
             [((near, span, hsize), BF16)],
-            (lax.axis_index("zh").reshape(1), quarter, *arrived, pick),
-            [pltpu.VMEM((far, span, hsize), F32)],
-            specs=[SMEM] + [VMEM] * 4 + [ANY],
+            (parts, pick),
+            specs=[VMEM, ANY],
         )
     with jax.named_scope("pre_gather"):
         pre_mine = lax.all_to_all(copies, "zl", 0, 0, tiled=True)

time: 105 us -> 102 us (0.971)
  starting transfers between devices: 37.1 us -> 23 us
  blocking collectives: 53.9 us -> 63 us
  waiting for transfers between devices: 3.11 us -> 4.36 us
    all_gather x0 -> x1, blocking collectives: none -> 22.1 us  [per_device(): parts = lax.all_gather(quarter, 'zh')]
    ppermute x3 -> x0, starting transfers between devices: 21.9 us -> none  [per_device(): lax.ppermute(quarter, 'zh', [(i, (i + step) % far) for i in range(far)])]
    all_to_all x1 -> x0, blocking collectives: 13 us -> none  [per_device(): blocks = lax.all_to_all(blocks, NEAR, 0, 0, tiled=True)]
    all_to_all x0 -> x1, starting transfers between devices: none -> 7.49 us  [per_device(): blocks = lax.all_to_all(blocks, NEAR, 0, 0, tiled=True)]
    all_to_all x0 -> x1, waiting for transfers between devices: none -> 3.7 us  [per_device(): blocks = lax.all_to_all(blocks, NEAR, 0, 0, tiled=True)]
    ppermute x3 -> x0, waiting for transfers between devices: 2.44 us -> none  [per_device(): lax.ppermute(quarter, 'zh', [(i, (i + step) % far) for i in range(far)])]
  transfers between devices with their start and end apart: 5 -> 3, of which waited for: 2 -> 2; matrix products, arithmetic and copies ran while one was open for 0% -> 0% of each run, Pallas kernels for 2% -> 2%
where the time goes in v8:
time: 102 us; the launch traced here: 101 us
  blocking collectives  63 us (62%)
  starting transfers between devices  23 us (23%)
  Pallas kernels  8.58 us (8%)
  waiting for transfers between devices  4.36 us (4%)
  between operations  1.4 us (1%)
    all_gather x1, blocking collectives, per_device(): parts = lax.all_gather(quarter, 'zh')  22.1 us
    all_gather x1, blocking collectives, per_device(): weights = lax.all_gather(weights, NEAR, tiled=True)  17.1 us
    all_to_all x1, blocking collectives, per_device(): grads = lax.all_to_all(grads, NODE, 0, 0, tiled=True)  15.4 us
    pallas_call x8, Pallas kernels, run(): pl.pallas_call(kernel, out_shape=shapes, in_specs=specs, out_specs=out_sp...  8.58 us
    all_to_all x1, blocking collectives, per_device(): pre_mine = lax.all_to_all(copies, 'zl', 0, 0, tiled=True)  8.38 us
    ppermute x1, starting transfers between devices, per_device(): pre_other = lax.ppermute(pre_mine, 'c', swap)  7.8 us
    all_to_all x1, starting transfers between devices, per_device(): lax.all_to_all(aggregate.reshape(owners, tgt_rows // block * columns, blo...  7.72 us
    all_to_all x1, starting transfers between devices, per_device(): blocks = lax.all_to_all(blocks, NEAR, 0, 0, tiled=True)  7.49 us
  transfers between devices with their start and end apart: 3, of which 2 were waited for; matrix products, arithmetic and copies ran while one was open for 0% of the time, Pallas kernels for 2%

profile of v8, /device:TPU:1, one launch (start us, length us, event | category | flops | bytes accessed | tf_op | source)
XLA Modules:
  0.0 101.1 jit_solution(14037180140554529678)
XLA Ops:
  1.3 3.0 %aggregate_tiles.1 = bf16[128,32,128]{2,1,0:T(8,128)(2,1)} custom-call(s32[1,1]{1,0:T(1,128)} %bitcast.10.count_ref, s32[2,32]{1,0:T(2,128)} %bitcast.17, bf16[32,128,128]{2,1,0:T(8,128)(2,1)} %tiles_ref.1, bf16[32,1024]{1,0:T(8,128)(2,1)} %bitcast.16), custom_call_target="tpu_custom_call" | custom-call | bytes 2162948 | tf_op jit(solution)/shard_map/aggregate_tiles/pallas_call | solution.py:223
  4.2 0.0 copy-start.6
  4.2 0.0 copy-start.7
  4.3 7.7 %all-to-all-start = ((bf16[16,256,128]{2,1,0:T(8,128)(2,1)}), bf16[16,256,128]{2,1,0:T(8,128)(2,1)S(1)}, u32[]{:S(2)}, u32[]{:S(2)}) async-start(bf16[16,256,128]{2,1,0:T(8,128)(2,1)} %bitcast.15), calls=%async_computation | async-start | bytes 2097152 | tf_op jit(solution)/shard_map/aggregate_exchange/all_to_all | solution.py:279
  12.0 0.0 copy-done.6
  12.0 0.0 copy-done.7
  12.0 0.0 copy-start.3
  12.0 17.1 %all_gather.9.weights_ref = bf16[256,512]{1,0:T(8,128)(2,1)S(1)} all-gather(bf16[32,512]{1,0:T(8,128)(2,1)S(1)} %pad_maximum_fusion), channel_id=1, replica_groups=mesh['zh'=4,'zl'=4,'c'=2,'x'=4,'y'=4] {'zl','c'}, dimensions={0}, use_global_device_ids=true | all-gather | bytes 294912 | tf_op jit(solution)/shard_map/weights_gather/all_gather | solution.py:284
  29.2 0.0 all-to-all-done.parts_ref
  29.2 0.0 copy-done.3
  29.2 0.8 owned_sum.1
  30.0 0.0 copy-start.4
  30.0 7.5 %all-to-all-start.1 = ((bf16[8,64,128]{2,1,0:T(8,128)(2,1)}), bf16[8,64,128]{2,1,0:T(8,128)(2,1)S(1)}, u32[]{:S(2)}, u32[]{:S(2)}) async-start(bf16[8,64,128]{2,1,0:T(8,128)(2,1)} %get-tuple-element.16), calls=%async_computation.1 | async-start | bytes 262144 | tf_op jit(solution)/shard_map/near_exchange/all_to_all | solution.py:294
  37.5 0.0 copy-start.5
  37.5 0.0 copy-done.4
  37.5 0.7 copy-done.5
  38.2 1.4 %picks.1 = (bf16[1024,512]{1,0:T(8,128)(2,1)S(1)}, bf16[512,1024]{1,0:T(8,128)(2,1)S(1)}) custom-call(s32[1]{0:T(128)} %bitcast.1.core_ref, s32[10,256]{1,0:T(8,128)S(1)} %bitcast.13, s32[1,256]{1,0:T(1,128)S(1)} %bitcast.14), custom_call_target="tpu_custom_call" | custom-call | flops 5242880 | bytes 2108420 | tf_op jit(solution)/shard_map/picks/pallas_call | solution.py:223
  39.6 3.7 %all-to-all-done.1.blocks_ref = bf16[8,64,128]{2,1,0:T(8,128)(2,1)S(1)} async-done(((bf16[8,64,128]{2,1,0:T(8,128)(2,1)}), bf16[8,64,128]{2,1,0:T(8,128)(2,1)S(1)}, u32[]{:S(2)}, u32[]{:S(2)}) %all-to-all-start.1) | async-done | bytes 131104 | tf_op jit(solution)/shard_map/near_exchange/all_to_all | solution.py:294
  43.3 0.2 partial_pre.1
  43.5 22.1 %all-gather = bf16[512,256]{1,0:T(8,128)(2,1)S(1)} all-gather(bf16[128,256]{1,0:T(8,128)(2,1)S(1)} %partial_pre.1), channel_id=2, replica_groups=mesh['zh'=4,'zl'=4,'c'=2,'x'=4,'y'=4] {'zh'}, dimensions={0}, use_global_device_ids=true | all-gather | bytes 327680 | tf_op jit(solution)/shard_map/pre_sum_far/all_gather | solution.py:311
  65.7 8.4 %all_to_all.20.pre_ref = bf16[4,128,256]{2,1,0:T(8,128)(2,1)S(1)} all-to-all(bf16[4,128,256]{2,1,0:T(8,128)(2,1)S(1)} %pre_sum_far.1), channel_id=1, replica_groups=mesh['zh'=4,'zl'=4,'c'=2,'x'=4,'y'=4] {'zl'}, dimensions={0} | all-to-all | bytes 524288 | tf_op jit(solution)/shard_map/pre_gather/all_to_all | solution.py:319
  74.1 7.8 %collective-permute-start = (bf16[4,128,256]{2,1,0:T(8,128)(2,1)S(1)}, bf16[4,128,256]{2,1,0:T(8,128)(2,1)S(1)}, u32[]{:S(2)}, u32[]{:S(2)}) collective-permute-start(bf16[4,128,256]{2,1,0:T(8,128)(2,1)S(1)} %all_to_all.20.pre_ref), channel_id=1, source_target_pairs={{0,16},{16,0},{1,17},{17,1},{2,18},{18,2},{3,19},{19,3},{4,20},{20... | collective-permute-start | bytes 786440 | tf_op jit(solution)/shard_map/pre_gather/ppermute | solution.py:320
  81.9 0.0 copy-start
  81.9 0.0 copy-start.1
  81.9 0.0 copy-start.2
  81.9 0.4 step_mine.1
  82.4 0.7 collective-permute-done.pre_ref
  83.0 0.0 copy-done
  83.0 0.0 copy-done.1
  83.0 0.0 copy-done.2
  83.0 2.0 %step.1 = (bf16[256,256]{1,0:T(8,128)(2,1)}, bf16[16,80,256]{2,1,0:T(8,128)(2,1)S(1)}) custom-call(s32[1]{0:T(128)} %bitcast.feat_ref, bf16[4,128,256]{2,1,0:T(8,128)(2,1)S(1)} %collective-permute-done.pre_ref, f32[512,256]{1,0:T(8,128)S(1)} %get-tuple-element.18.gathered_ref, f32[512,256]{1,0:T(8,128)S(1)} %get-tuple-element.19.slope_ref, ...), custom_call_target="tpu_custom_call" | custom-call | bytes 4718596 | tf_op jit(solution)/shard_map/step/pallas_call | solution.py:223
  85.0 15.4 %all_to_all.21.parts_ref = bf16[16,80,256]{2,1,0:T(8,128)(2,1)S(1)} all-to-all(bf16[16,80,256]{2,1,0:T(8,128)(2,1)S(1)} %get-tuple-element.26), channel_id=1, replica_groups=mesh['zh'=4,'zl'=4,'c'=2,'x'=4,'y'=4] {'x','y'}, dimensions={0} | all-to-all | bytes 1310720 | tf_op jit(solution)/shard_map/grad_sum/all_to_all | solution.py:358
  100.4 0.7 grad_sum.1
  (2 shorter events, 0.0 us)
Async XLA Ops:
  4.2 7.7 %copy-start.6 = (bf16[32,256]{1,0:T(8,128)(2,1)S(1)}, bf16[32,256]{1,0:T(8,128)(2,1)}, u32[]{:S(2)}) copy-start(bf16[32,256]{1,0:T(8,128)(2,1)} %param.18) | copy-start | bytes 49156
  4.2 7.7 %copy-start.7 = (bf16[32,256]{1,0:T(8,128)(2,1)S(1)}, bf16[32,256]{1,0:T(8,128)(2,1)}, u32[]{:S(2)}) copy-start(bf16[32,256]{1,0:T(8,128)(2,1)} %param.17) | copy-start | bytes 49156
  4.3 24.9 %all-to-all-start = ((bf16[16,256,128]{2,1,0:T(8,128)(2,1)}), bf16[16,256,128]{2,1,0:T(8,128)(2,1)S(1)}, u32[]{:S(2)}, u32[]{:S(2)}) async-start(bf16[16,256,128]{2,1,0:T(8,128)(2,1)} %bitcast.15), calls=%async_computation | async-start | bytes 2097152 | tf_op jit(solution)/shard_map/aggregate_exchange/all_to_all | solution.py:279
  12.0 17.1 %copy-start.3 = (bf16[1024,32]{0,1:T(8,128)(2,1)S(1)}, bf16[1024,32]{0,1:T(8,128)(2,1)}, u32[]{:S(2)}) copy-start(bf16[1024,32]{0,1:T(8,128)(2,1)} %param.13) | copy-start | bytes 196612
  30.0 7.5 %copy-start.4 = (s32[256,10]{0,1:T(8,128)S(1)}, s32[256,10]{0,1:T(8,128)}, u32[]{:S(2)}) copy-start(s32[256,10]{0,1:T(8,128)} %param.21) | copy-start | bytes 30724
  30.0 13.3 %all-to-all-start.1 = ((bf16[8,64,128]{2,1,0:T(8,128)(2,1)}), bf16[8,64,128]{2,1,0:T(8,128)(2,1)S(1)}, u32[]{:S(2)}, u32[]{:S(2)}) async-start(bf16[8,64,128]{2,1,0:T(8,128)(2,1)} %get-tuple-element.16), calls=%async_computation.1 | async-start | bytes 262144 | tf_op jit(solution)/shard_map/near_exchange/all_to_all | solution.py:294
  37.5 0.7 copy-start.5
  74.1 8.9 %collective-permute-start = (bf16[4,128,256]{2,1,0:T(8,128)(2,1)S(1)}, bf16[4,128,256]{2,1,0:T(8,128)(2,1)S(1)}, u32[]{:S(2)}, u32[]{:S(2)}) collective-permute-start(bf16[4,128,256]{2,1,0:T(8,128)(2,1)S(1)} %all_to_all.20.pre_ref), channel_id=1, source_target_pairs={{0,16},{16,0},{1,17},{17,1},{2,18},{18,2},{3,19},{19,3},{4,20},{20... | collective-permute-start | bytes 786440 | tf_op jit(solution)/shard_map/pre_gather/ppermute | solution.py:320
  81.9 1.1 %copy-start = (bf16[256,256]{1,0:T(8,128)(2,1)S(1)}, bf16[256,256]{1,0:T(8,128)(2,1)}, u32[]{:S(2)}) copy-start(bf16[256,256]{1,0:T(8,128)(2,1)} %self_ref.1) | copy-start | bytes 393220
  81.9 1.1 %copy-start.1 = (bf16[256,256]{1,0:T(8,128)(2,1)S(1)}, bf16[256,256]{1,0:T(8,128)(2,1)}, u32[]{:S(2)}) copy-start(bf16[256,256]{1,0:T(8,128)(2,1)} %neigh_ref.1) | copy-start | bytes 393220
  81.9 1.1 %copy-start.2 = (bf16[256,256]{1,0:T(8,128)(2,1)S(1)}, bf16[256,256]{1,0:T(8,128)(2,1)}, u32[]{:S(2)}) copy-start(bf16[256,256]{1,0:T(8,128)(2,1)} %cotangent_ref.1) | copy-start | bytes 393220

commit v9 on v8

--- a/solution.py
+++ b/solution.py
@@ -15,7 +15,6 @@
 MIB = 1 << 20
 
 VMEM = pl.BlockSpec(memory_space=pltpu.VMEM)
-HBM = pl.BlockSpec(memory_space=pltpu.HBM)
 ANY = pl.BlockSpec(memory_space=pl.ANY)
 SMEM = pl.BlockSpec(memory_space=pltpu.SMEM)
 
@@ -147,8 +146,6 @@
     grads_ref,
     gathered,
     scratch,
-    output,
-    output_sem,
 ):
     seeds = cotangent_ref.shape[0]
     columns = targets_ref.shape[0]
@@ -160,9 +157,7 @@
     own = picked[seeds:].astype(BF16)
     pre_two = contract(own, self_ref[...], 1, 0) + contract(nbr_mean, neigh_ref[...], 1, 0)
     gate = jax.nn.sigmoid(pre_two)
-    output[...] = (pre_two * gate).astype(BF16)
-    copy = pltpu.make_async_copy(output, output_ref, output_sem)
-    copy.start()
+    output_ref[...] = (pre_two * gate).astype(BF16)
     slope_two = (
         cotangent_ref[...].astype(F32) * (gate * (1.0 + pre_two * (1.0 - gate)))
     ).astype(BF16)
@@ -199,10 +194,10 @@
     every = jnp.concatenate([grad_one, grad_two.astype(BF16)], axis=0)
     for position in range(grads_ref.shape[0]):
         grads_ref[position] = every
-    copy.wait()
-
-
-def grads_kernel(parts_ref, one_ref, two_ref):
+
+
+def grads_kernel(parts_ref, output_ref, one_ref, two_ref, final_ref):
+    final_ref[...] = output_ref[...]
     total = parts_ref[0].astype(F32)
     for position in range(1, parts_ref.shape[0]):
         total += parts_ref[position].astype(F32)
@@ -213,7 +208,7 @@
     two_ref[1] = total[2 * columns + part_rows :]
 
 
-def run(kernel, outs, operands, scratch=(), limit=8, flops=0, specs=None, out_specs=None):
+def run(kernel, outs, operands, scratch=(), limit=8, flops=0, specs=None):
     shapes = [jax.ShapeDtypeStruct(shape, dtype) for shape, dtype in outs]
     moved = sum(x.size * x.dtype.itemsize for x in operands) + sum(
         x.size * x.dtype.itemsize for x in shapes
@@ -224,7 +219,7 @@
         kernel,
         out_shape=shapes,
         in_specs=specs,
-        out_specs=out_specs or [VMEM] * len(shapes),
+        out_specs=[VMEM] * len(shapes),
         scratch_shapes=list(scratch),
         cost_estimate=pl.CostEstimate(flops=flops, bytes_accessed=moved, transcendentals=0),
         compiler_params=pltpu.CompilerParams(vmem_limit_bytes=limit * MIB),
@@ -348,18 +343,15 @@
             [
                 pltpu.VMEM((2 * seeds, hsize), F32),
                 pltpu.VMEM((2, hsize, hsize), F32),
-                pltpu.VMEM(cotangent.shape, BF16),
-                pltpu.SemaphoreType.DMA,
             ],
             limit=24,
-            out_specs=[HBM, VMEM],
         )
     with jax.named_scope("grad_sum"):
         grads = lax.all_to_all(grads, NODE, 0, 0, tiled=True)
-        grad_one, grad_two = run(
+        grad_one, grad_two, output = run(
             grads_kernel,
-            [((2, columns, hsize), F32), ((2, part_rows, hsize), F32)],
-            (grads,),
+            [((2, columns, hsize), F32), ((2, part_rows, hsize), F32), (cotangent.shape, BF16)],
+            (grads, output),
         )
     return (output, grad_one, grad_two)
 

time: 102 us -> 101 us (level)
  no operation moved by 1% of the time
where the time goes in v9:
time: 101 us
  blocking collectives  63 us (62%)
  starting transfers between devices  23 us (23%)
  Pallas kernels  8.09 us (8%)
  waiting for transfers between devices  4.36 us (4%)
  between operations  1.4 us (1%)
    all_gather x1, blocking collectives, per_device(): parts = lax.all_gather(quarter, 'zh')  22.1 us
    all_gather x1, blocking collectives, per_device(): weights = lax.all_gather(weights, NEAR, tiled=True)  17.1 us
    all_to_all x1, blocking collectives, per_device(): grads = lax.all_to_all(grads, NODE, 0, 0, tiled=True)  15.4 us
    all_to_all x1, blocking collectives, per_device(): pre_mine = lax.all_to_all(copies, 'zl', 0, 0, tiled=True)  8.38 us
    pallas_call x8, Pallas kernels, run(): pl.pallas_call(kernel, out_shape=shapes, in_specs=specs, out_specs=[VMEM]...  8.09 us
    ppermute x1, starting transfers between devices, per_device(): pre_other = lax.ppermute(pre_mine, 'c', swap)  7.8 us
    all_to_all x1, starting transfers between devices, per_device(): lax.all_to_all(aggregate.reshape(owners, tgt_rows // block * columns, blo...  7.71 us
    all_to_all x1, starting transfers between devices, per_device(): blocks = lax.all_to_all(blocks, NEAR, 0, 0, tiled=True)  7.49 us
  transfers between devices with their start and end apart: 3, of which 2 were waited for; matrix products, arithmetic and copies ran while one was open for 0% of the time, Pallas kernels for 2%

profile of v9, /device:TPU:1, one launch (start us, length us, event | category | flops | bytes accessed | tf_op | source)
XLA Modules:
  0.0 100.6 jit_solution(1423400343331053907)
XLA Ops:
  1.3 3.0 %aggregate_tiles.1 = bf16[128,32,128]{2,1,0:T(8,128)(2,1)} custom-call(s32[1,1]{1,0:T(1,128)} %bitcast.10.count_ref, s32[2,32]{1,0:T(2,128)} %bitcast.17, bf16[32,128,128]{2,1,0:T(8,128)(2,1)} %tiles_ref.1, bf16[32,1024]{1,0:T(8,128)(2,1)} %bitcast.16), custom_call_target="tpu_custom_call" | custom-call | bytes 2162948 | tf_op jit(solution)/shard_map/aggregate_tiles/pallas_call | solution.py:218
  4.2 0.0 copy-start.6
  4.3 0.0 copy-start.7
  4.3 7.7 %all-to-all-start = ((bf16[16,256,128]{2,1,0:T(8,128)(2,1)}), bf16[16,256,128]{2,1,0:T(8,128)(2,1)S(1)}, u32[]{:S(2)}, u32[]{:S(2)}) async-start(bf16[16,256,128]{2,1,0:T(8,128)(2,1)} %bitcast.15), calls=%async_computation | async-start | bytes 2097152 | tf_op jit(solution)/shard_map/aggregate_exchange/all_to_all | solution.py:274
  12.0 0.0 copy-done.6
  12.0 0.0 copy-done.7
  12.0 0.0 copy-start.3
  12.0 17.1 %all_gather.9.weights_ref = bf16[256,512]{1,0:T(8,128)(2,1)S(1)} all-gather(bf16[32,512]{1,0:T(8,128)(2,1)S(1)} %pad_maximum_fusion), channel_id=1, replica_groups=mesh['zh'=4,'zl'=4,'c'=2,'x'=4,'y'=4] {'zl','c'}, dimensions={0}, use_global_device_ids=true | all-gather | bytes 294912 | tf_op jit(solution)/shard_map/weights_gather/all_gather | solution.py:279
  29.2 0.0 all-to-all-done.parts_ref
  29.2 0.0 copy-done.3
  29.2 0.8 owned_sum.1
  30.0 0.0 copy-start.4
  30.0 7.5 %all-to-all-start.1 = ((bf16[8,64,128]{2,1,0:T(8,128)(2,1)}), bf16[8,64,128]{2,1,0:T(8,128)(2,1)S(1)}, u32[]{:S(2)}, u32[]{:S(2)}) async-start(bf16[8,64,128]{2,1,0:T(8,128)(2,1)} %get-tuple-element.17), calls=%async_computation.1 | async-start | bytes 262144 | tf_op jit(solution)/shard_map/near_exchange/all_to_all | solution.py:289
  37.5 0.0 copy-start.5
  37.5 0.0 copy-done.4
  37.5 0.7 copy-done.5
  38.2 1.4 %picks.1 = (bf16[1024,512]{1,0:T(8,128)(2,1)S(1)}, bf16[512,1024]{1,0:T(8,128)(2,1)S(1)}) custom-call(s32[1]{0:T(128)} %bitcast.1.core_ref, s32[10,256]{1,0:T(8,128)S(1)} %bitcast.13, s32[1,256]{1,0:T(1,128)S(1)} %bitcast.14), custom_call_target="tpu_custom_call" | custom-call | flops 5242880 | bytes 2108420 | tf_op jit(solution)/shard_map/picks/pallas_call | solution.py:218
  39.6 3.7 %all-to-all-done.1.blocks_ref = bf16[8,64,128]{2,1,0:T(8,128)(2,1)S(1)} async-done(((bf16[8,64,128]{2,1,0:T(8,128)(2,1)}), bf16[8,64,128]{2,1,0:T(8,128)(2,1)S(1)}, u32[]{:S(2)}, u32[]{:S(2)}) %all-to-all-start.1) | async-done | bytes 131104 | tf_op jit(solution)/shard_map/near_exchange/all_to_all | solution.py:289
  43.3 0.2 partial_pre.1
  43.5 22.1 %all-gather = bf16[512,256]{1,0:T(8,128)(2,1)S(1)} all-gather(bf16[128,256]{1,0:T(8,128)(2,1)S(1)} %partial_pre.1), channel_id=2, replica_groups=mesh['zh'=4,'zl'=4,'c'=2,'x'=4,'y'=4] {'zh'}, dimensions={0}, use_global_device_ids=true | all-gather | bytes 327680 | tf_op jit(solution)/shard_map/pre_sum_far/all_gather | solution.py:306
  65.7 8.4 %all_to_all.20.pre_ref = bf16[4,128,256]{2,1,0:T(8,128)(2,1)S(1)} all-to-all(bf16[4,128,256]{2,1,0:T(8,128)(2,1)S(1)} %pre_sum_far.1), channel_id=1, replica_groups=mesh['zh'=4,'zl'=4,'c'=2,'x'=4,'y'=4] {'zl'}, dimensions={0} | all-to-all | bytes 524288 | tf_op jit(solution)/shard_map/pre_gather/all_to_all | solution.py:314
  74.1 7.8 %collective-permute-start = (bf16[4,128,256]{2,1,0:T(8,128)(2,1)S(1)}, bf16[4,128,256]{2,1,0:T(8,128)(2,1)S(1)}, u32[]{:S(2)}, u32[]{:S(2)}) collective-permute-start(bf16[4,128,256]{2,1,0:T(8,128)(2,1)S(1)} %all_to_all.20.pre_ref), channel_id=1, source_target_pairs={{0,16},{16,0},{1,17},{17,1},{2,18},{18,2},{3,19},{19,3},{4,20},{20... | collective-permute-start | bytes 786440 | tf_op jit(solution)/shard_map/pre_gather/ppermute | solution.py:315
  81.9 0.0 copy-start
  81.9 0.0 copy-start.1
  81.9 0.0 copy-start.2
  81.9 0.4 step_mine.1
  82.4 0.7 collective-permute-done.pre_ref
  83.0 0.0 copy-done
  83.0 0.0 copy-done.1
  83.0 0.0 copy-done.2
  83.0 1.5 %step.1 = (bf16[256,256]{1,0:T(8,128)(2,1)S(1)}, bf16[16,80,256]{2,1,0:T(8,128)(2,1)S(1)}) custom-call(s32[1]{0:T(128)} %bitcast.feat_ref, bf16[4,128,256]{2,1,0:T(8,128)(2,1)S(1)} %collective-permute-done.pre_ref, f32[512,256]{1,0:T(8,128)S(1)} %get-tuple-element.19.gathered_ref, f32[512,256]{1,0:T(8,128)S(1)} %get-tuple-element.20.slope_ref, ...), custom_call_target="tpu_custom_call" | custom-call | bytes 4718596 | tf_op jit(solution)/shard_map/step/pallas_call | solution.py:218
  84.5 15.4 %all_to_all.21.parts_ref = bf16[16,80,256]{2,1,0:T(8,128)(2,1)S(1)} all-to-all(bf16[16,80,256]{2,1,0:T(8,128)(2,1)S(1)} %get-tuple-element.26), channel_id=1, replica_groups=mesh['zh'=4,'zl'=4,'c'=2,'x'=4,'y'=4] {'x','y'}, dimensions={0} | all-to-all | bytes 1310720 | tf_op jit(solution)/shard_map/grad_sum/all_to_all | solution.py:350
  99.9 0.7 grad_sum.1
  (2 shorter events, 0.0 us)
Async XLA Ops:
  4.2 7.7 %copy-start.6 = (bf16[32,256]{1,0:T(8,128)(2,1)S(1)}, bf16[32,256]{1,0:T(8,128)(2,1)}, u32[]{:S(2)}) copy-start(bf16[32,256]{1,0:T(8,128)(2,1)} %param.18) | copy-start | bytes 49156
  4.3 7.7 %copy-start.7 = (bf16[32,256]{1,0:T(8,128)(2,1)S(1)}, bf16[32,256]{1,0:T(8,128)(2,1)}, u32[]{:S(2)}) copy-start(bf16[32,256]{1,0:T(8,128)(2,1)} %param.17) | copy-start | bytes 49156
  4.3 24.9 %all-to-all-start = ((bf16[16,256,128]{2,1,0:T(8,128)(2,1)}), bf16[16,256,128]{2,1,0:T(8,128)(2,1)S(1)}, u32[]{:S(2)}, u32[]{:S(2)}) async-start(bf16[16,256,128]{2,1,0:T(8,128)(2,1)} %bitcast.15), calls=%async_computation | async-start | bytes 2097152 | tf_op jit(solution)/shard_map/aggregate_exchange/all_to_all | solution.py:274
  12.0 17.1 %copy-start.3 = (bf16[1024,32]{0,1:T(8,128)(2,1)S(1)}, bf16[1024,32]{0,1:T(8,128)(2,1)}, u32[]{:S(2)}) copy-start(bf16[1024,32]{0,1:T(8,128)(2,1)} %param.13) | copy-start | bytes 196612
  30.0 7.5 %copy-start.4 = (s32[256,10]{0,1:T(8,128)S(1)}, s32[256,10]{0,1:T(8,128)}, u32[]{:S(2)}) copy-start(s32[256,10]{0,1:T(8,128)} %param.21) | copy-start | bytes 30724
  30.0 13.3 %all-to-all-start.1 = ((bf16[8,64,128]{2,1,0:T(8,128)(2,1)}), bf16[8,64,128]{2,1,0:T(8,128)(2,1)S(1)}, u32[]{:S(2)}, u32[]{:S(2)}) async-start(bf16[8,64,128]{2,1,0:T(8,128)(2,1)} %get-tuple-element.17), calls=%async_computation.1 | async-start | bytes 262144 | tf_op jit(solution)/shard_map/near_exchange/all_to_all | solution.py:289
  37.5 0.7 copy-start.5
  74.1 8.9 %collective-permute-start = (bf16[4,128,256]{2,1,0:T(8,128)(2,1)S(1)}, bf16[4,128,256]{2,1,0:T(8,128)(2,1)S(1)}, u32[]{:S(2)}, u32[]{:S(2)}) collective-permute-start(bf16[4,128,256]{2,1,0:T(8,128)(2,1)S(1)} %all_to_all.20.pre_ref), channel_id=1, source_target_pairs={{0,16},{16,0},{1,17},{17,1},{2,18},{18,2},{3,19},{19,3},{4,20},{20... | collective-permute-start | bytes 786440 | tf_op jit(solution)/shard_map/pre_gather/ppermute | solution.py:315
  81.9 1.1 %copy-start = (bf16[256,256]{1,0:T(8,128)(2,1)S(1)}, bf16[256,256]{1,0:T(8,128)(2,1)}, u32[]{:S(2)}) copy-start(bf16[256,256]{1,0:T(8,128)(2,1)} %self_ref.1) | copy-start | bytes 393220
  81.9 1.1 %copy-start.1 = (bf16[256,256]{1,0:T(8,128)(2,1)S(1)}, bf16[256,256]{1,0:T(8,128)(2,1)}, u32[]{:S(2)}) copy-start(bf16[256,256]{1,0:T(8,128)(2,1)} %neigh_ref.1) | copy-start | bytes 393220
  81.9 1.1 %copy-start.2 = (bf16[256,256]{1,0:T(8,128)(2,1)S(1)}, bf16[256,256]{1,0:T(8,128)(2,1)}, u32[]{:S(2)}) copy-start(bf16[256,256]{1,0:T(8,128)(2,1)} %cotangent_ref.1) | copy-start | bytes 393220

commit v10 on v9

--- a/solution.py
+++ b/solution.py
@@ -130,6 +130,7 @@
 
 def step_kernel(
     feat_ref,
+    core_ref,
     pre_ref,
     gathered_ref,
     slope_ref,
@@ -150,7 +151,7 @@
     seeds = cotangent_ref.shape[0]
     columns = targets_ref.shape[0]
     half = slope_ref.shape[0]
-    hidden, slope_other = activate(pre_ref, slope_ref.shape)
+    hidden, slope_other = activate(pre_ref.at[1 - core_ref[0]], slope_ref.shape)
     gathered[...] = contract(pick_ref[:, half:], hidden, 1, 0)
     picked = gathered_ref[...] + gathered[...]
     nbr_mean = (picked[:seeds] / FAN).astype(BF16)
@@ -255,7 +256,6 @@
     core = lax.axis_index("c").reshape(1)
     feat = lax.axis_index(FEAT).reshape(1)
     halves = pltpu.VMEM((near, 2, columns, block), BF16)
-    swap = [(0, 1), (1, 0)]
 
     with jax.named_scope("aggregate_tiles"):
         aggregate = run(
@@ -312,7 +312,7 @@
         )
     with jax.named_scope("pre_gather"):
         pre_mine = lax.all_to_all(copies, "zl", 0, 0, tiled=True)
-        pre_other = lax.ppermute(pre_mine, "c", swap)
+        pre_both = lax.all_gather(pre_mine, "c")
     with jax.named_scope("step_mine"):
         gathered, slope = run(
             mine_kernel,
@@ -327,7 +327,8 @@
             [(cotangent.shape, BF16), ((owners, 2 * columns + 2 * part_rows, hsize), BF16)],
             (
                 feat,
-                pre_other,
+                core,
+                pre_both,
                 gathered,
                 slope,
                 pick,

time: 101 us -> 102 us (level)
  waiting for transfers between devices: 4.36 us -> 9.28 us
  starting transfers between devices: 23 us -> 18.6 us
    all_to_all x1 -> x0, blocking collectives: 8.38 us -> none  [per_device(): pre_mine = lax.all_to_all(copies, 'zl', 0, 0, tiled=True)]
    ppermute x1 -> x0, starting transfers between devices: 7.8 us -> none  [per_device(): pre_other = lax.ppermute(pre_mine, 'c', swap)]
    all_gather x0 -> x1, blocking collectives: none -> 7.71 us  [per_device(): pre_both = lax.all_gather(pre_mine, 'c')]
    all_to_all x0 -> x1, waiting for transfers between devices: none -> 5.58 us  [per_device(): pre_mine = lax.all_to_all(copies, 'zl', 0, 0, tiled=True)]
    all_to_all x0 -> x1, starting transfers between devices: none -> 3.4 us  [per_device(): pre_mine = lax.all_to_all(copies, 'zl', 0, 0, tiled=True)]
  transfers between devices with their start and end apart: 3 -> 3, of which waited for: 2 -> 2; matrix products, arithmetic and copies ran while one was open for 0% -> 0% of each run, Pallas kernels for 2% -> 1%
where the time goes in v10:
time: 102 us
  blocking collectives  62.4 us (61%)
  starting transfers between devices  18.6 us (18%)
  waiting for transfers between devices  9.28 us (9%)
  Pallas kernels  8.79 us (9%)
  between operations  1.38 us (1%)
  local copies, waits for them, and re-layouts  1.29 us (1%)
    all_gather x1, blocking collectives, per_device(): parts = lax.all_gather(quarter, 'zh')  22.1 us
    all_gather x1, blocking collectives, per_device(): weights = lax.all_gather(weights, NEAR, tiled=True)  17.1 us
    all_to_all x1, blocking collectives, per_device(): grads = lax.all_to_all(grads, NODE, 0, 0, tiled=True)  15.4 us
    pallas_call x8, Pallas kernels, run(): pl.pallas_call(kernel, out_shape=shapes, in_specs=specs, out_specs=[VMEM]...  8.79 us
    all_to_all x1, starting transfers between devices, per_device(): lax.all_to_all(aggregate.reshape(owners, tgt_rows // block * columns, blo...  7.72 us
    all_gather x1, blocking collectives, per_device(): pre_both = lax.all_gather(pre_mine, 'c')  7.71 us
    all_to_all x1, starting transfers between devices, per_device(): blocks = lax.all_to_all(blocks, NEAR, 0, 0, tiled=True)  7.49 us
    all_to_all x1, waiting for transfers between devices, per_device(): pre_mine = lax.all_to_all(copies, 'zl', 0, 0, tiled=True)  5.58 us
  transfers between devices with their start and end apart: 3, of which 2 were waited for; matrix products, arithmetic and copies ran while one was open for 0% of the time, Pallas kernels for 1%

profile of v10, /device:TPU:1, one launch (start us, length us, event | category | flops | bytes accessed | tf_op | source)
XLA Modules:
  0.0 101.7 jit_solution(17473022850761489834)
XLA Ops:
  1.3 3.0 %aggregate_tiles.1 = bf16[128,32,128]{2,1,0:T(8,128)(2,1)} custom-call(s32[1,1]{1,0:T(1,128)} %bitcast.11.count_ref, s32[2,32]{1,0:T(2,128)} %bitcast.19, bf16[32,128,128]{2,1,0:T(8,128)(2,1)} %tiles_ref.1, bf16[32,1024]{1,0:T(8,128)(2,1)} %bitcast.18), custom_call_target="tpu_custom_call" | custom-call | bytes 2162948 | tf_op jit(solution)/shard_map/aggregate_tiles/pallas_call | solution.py:219
  4.2 0.0 copy-start.6
  4.2 0.0 copy-start.7
  4.2 7.7 %all-to-all-start = ((bf16[16,256,128]{2,1,0:T(8,128)(2,1)}), bf16[16,256,128]{2,1,0:T(8,128)(2,1)S(1)}, u32[]{:S(2)}, u32[]{:S(2)}) async-start(bf16[16,256,128]{2,1,0:T(8,128)(2,1)} %bitcast.17), calls=%async_computation | async-start | bytes 2097152 | tf_op jit(solution)/shard_map/aggregate_exchange/all_to_all | solution.py:274
  12.0 0.0 copy-done.6
  12.0 0.0 copy-done.7
  12.0 0.0 copy-start.3
  12.0 17.1 %all_gather.15.weights_ref = bf16[256,512]{1,0:T(8,128)(2,1)S(1)} all-gather(bf16[32,512]{1,0:T(8,128)(2,1)S(1)} %pad_maximum_fusion), channel_id=1, replica_groups=mesh['zh'=4,'zl'=4,'c'=2,'x'=4,'y'=4] {'zl','c'}, dimensions={0}, use_global_device_ids=true | all-gather | bytes 294912 | tf_op jit(solution)/shard_map/weights_gather/all_gather | solution.py:279
  29.2 0.0 all-to-all-done.parts_ref
  29.2 0.0 copy-done.3
  29.2 0.8 owned_sum.1
  30.0 0.0 copy-start.4
  30.0 7.5 %all-to-all-start.1 = ((bf16[8,64,128]{2,1,0:T(8,128)(2,1)}), bf16[8,64,128]{2,1,0:T(8,128)(2,1)S(1)}, u32[]{:S(2)}, u32[]{:S(2)}) async-start(bf16[8,64,128]{2,1,0:T(8,128)(2,1)} %get-tuple-element.17), calls=%async_computation.1 | async-start | bytes 262144 | tf_op jit(solution)/shard_map/near_exchange/all_to_all | solution.py:289
  37.5 0.0 copy-start.5
  37.5 0.0 copy-done.4
  37.5 0.7 copy-done.5
  38.2 1.4 %picks.1 = (bf16[1024,512]{1,0:T(8,128)(2,1)S(1)}, bf16[512,1024]{1,0:T(8,128)(2,1)S(1)}) custom-call(s32[1]{0:T(128)} %bitcast.1.core_ref, s32[10,256]{1,0:T(8,128)S(1)} %bitcast.15, s32[1,256]{1,0:T(1,128)S(1)} %bitcast.16), custom_call_target="tpu_custom_call" | custom-call | flops 5242880 | bytes 2108420 | tf_op jit(solution)/shard_map/picks/pallas_call | solution.py:219
  39.6 3.7 %all-to-all-done.1.blocks_ref = bf16[8,64,128]{2,1,0:T(8,128)(2,1)S(1)} async-done(((bf16[8,64,128]{2,1,0:T(8,128)(2,1)}), bf16[8,64,128]{2,1,0:T(8,128)(2,1)S(1)}, u32[]{:S(2)}, u32[]{:S(2)}) %all-to-all-start.1) | async-done | bytes 131104 | tf_op jit(solution)/shard_map/near_exchange/all_to_all | solution.py:289
  43.3 0.2 partial_pre.1
  43.5 22.1 %all-gather = bf16[512,256]{1,0:T(8,128)(2,1)S(1)} all-gather(bf16[128,256]{1,0:T(8,128)(2,1)S(1)} %partial_pre.1), channel_id=2, replica_groups=mesh['zh'=4,'zl'=4,'c'=2,'x'=4,'y'=4] {'zh'}, dimensions={0}, use_global_device_ids=true | all-gather | bytes 327680 | tf_op jit(solution)/shard_map/pre_sum_far/all_gather | solution.py:306
  65.7 0.7 pre_sum_far.1
  66.4 3.4 %all-to-all-start.2 = ((bf16[4,128,256]{2,1,0:T(8,128)(2,1)}), bf16[4,128,256]{2,1,0:T(8,128)(2,1)S(1)}, u32[]{:S(2)}, u32[]{:S(2)}) async-start(bf16[4,128,256]{2,1,0:T(8,128)(2,1)} %pre_sum_far.1), calls=%async_computation.2 | async-start | bytes 524288 | tf_op jit(solution)/shard_map/pre_gather/all_to_all | solution.py:314
  69.8 5.6 %all-to-all-done.2.pre_ref = bf16[4,128,256]{2,1,0:T(8,128)(2,1)S(1)} async-done(((bf16[4,128,256]{2,1,0:T(8,128)(2,1)}), bf16[4,128,256]{2,1,0:T(8,128)(2,1)S(1)}, u32[]{:S(2)}, u32[]{:S(2)}) %all-to-all-start.2) | async-done | bytes 262176 | tf_op jit(solution)/shard_map/pre_gather/all_to_all | solution.py:314
  75.4 7.7 %all-gather.1 = bf16[8,128,256]{2,1,0:T(8,128)(2,1)S(1)} all-gather(bf16[4,128,256]{2,1,0:T(8,128)(2,1)S(1)} %all-to-all-done.2.pre_ref), channel_id=3, replica_groups=mesh['zh'=4,'zl'=4,'c'=2,'x'=4,'y'=4] {'c'}, dimensions={0}, use_global_device_ids=true | all-gather | bytes 786432 | tf_op jit(solution)/shard_map/pre_gather/all_gather | solution.py:315
  83.1 0.0 copy-start
  83.1 0.0 copy-start.1
  83.1 0.0 copy-start.2
  83.1 0.4 step_mine.1
  83.5 0.5 copy-done
  84.0 0.1 copy-done.1
  84.1 0.1 copy-done.2
  84.1 1.5 %step.1 = (bf16[256,256]{1,0:T(8,128)(2,1)S(1)}, bf16[16,80,256]{2,1,0:T(8,128)(2,1)S(1)}) custom-call(s32[1]{0:T(128)} %bitcast.feat_ref, s32[1]{0:T(128)} %bitcast.1.core_ref, bf16[2,4,128,256]{3,2,1,0:T(8,128)(2,1)S(1)} %bitcast.12, f32[512,256]{1,0:T(8,128)S(1)} %get-tuple-element.19.gathered_ref, f32[512,256]{1,0:T(8,128)S(1)} %get-tuple-element.20.slope_ref, ...), custom_call_target="tpu_custom_call" | custom-call | bytes 4980744 | tf_op jit(solution)/shard_map/step/pallas_call | solution.py:219
  85.6 15.4 %all_to_all.20.parts_ref = bf16[16,80,256]{2,1,0:T(8,128)(2,1)S(1)} all-to-all(bf16[16,80,256]{2,1,0:T(8,128)(2,1)S(1)} %get-tuple-element.26), channel_id=1, replica_groups=mesh['zh'=4,'zl'=4,'c'=2,'x'=4,'y'=4] {'x','y'}, dimensions={0} | all-to-all | bytes 1310720 | tf_op jit(solution)/shard_map/grad_sum/all_to_all | solution.py:351
  101.0 0.7 grad_sum.1
  (1 shorter events, 0.0 us)
Async XLA Ops:
  4.2 7.7 %copy-start.6 = (bf16[32,256]{1,0:T(8,128)(2,1)S(1)}, bf16[32,256]{1,0:T(8,128)(2,1)}, u32[]{:S(2)}) copy-start(bf16[32,256]{1,0:T(8,128)(2,1)} %param.18) | copy-start | bytes 49156
  4.2 7.7 %copy-start.7 = (bf16[32,256]{1,0:T(8,128)(2,1)S(1)}, bf16[32,256]{1,0:T(8,128)(2,1)}, u32[]{:S(2)}) copy-start(bf16[32,256]{1,0:T(8,128)(2,1)} %param.17) | copy-start | bytes 49156
  4.2 24.9 %all-to-all-start = ((bf16[16,256,128]{2,1,0:T(8,128)(2,1)}), bf16[16,256,128]{2,1,0:T(8,128)(2,1)S(1)}, u32[]{:S(2)}, u32[]{:S(2)}) async-start(bf16[16,256,128]{2,1,0:T(8,128)(2,1)} %bitcast.17), calls=%async_computation | async-start | bytes 2097152 | tf_op jit(solution)/shard_map/aggregate_exchange/all_to_all | solution.py:274
  12.0 17.1 %copy-start.3 = (bf16[1024,32]{0,1:T(8,128)(2,1)S(1)}, bf16[1024,32]{0,1:T(8,128)(2,1)}, u32[]{:S(2)}) copy-start(bf16[1024,32]{0,1:T(8,128)(2,1)} %param.13) | copy-start | bytes 196612
  30.0 7.5 %copy-start.4 = (s32[256,10]{0,1:T(8,128)S(1)}, s32[256,10]{0,1:T(8,128)}, u32[]{:S(2)}) copy-start(s32[256,10]{0,1:T(8,128)} %param.21) | copy-start | bytes 30724
  30.0 13.3 %all-to-all-start.1 = ((bf16[8,64,128]{2,1,0:T(8,128)(2,1)}), bf16[8,64,128]{2,1,0:T(8,128)(2,1)S(1)}, u32[]{:S(2)}, u32[]{:S(2)}) async-start(bf16[8,64,128]{2,1,0:T(8,128)(2,1)} %get-tuple-element.17), calls=%async_computation.1 | async-start | bytes 262144 | tf_op jit(solution)/shard_map/near_exchange/all_to_all | solution.py:289
  37.5 0.7 copy-start.5
  66.4 9.0 %all-to-all-start.2 = ((bf16[4,128,256]{2,1,0:T(8,128)(2,1)}), bf16[4,128,256]{2,1,0:T(8,128)(2,1)S(1)}, u32[]{:S(2)}, u32[]{:S(2)}) async-start(bf16[4,128,256]{2,1,0:T(8,128)(2,1)} %pre_sum_far.1), calls=%async_computation.2 | async-start | bytes 524288 | tf_op jit(solution)/shard_map/pre_gather/all_to_all | solution.py:314
  83.1 0.9 copy-start
  83.1 1.0 copy-start.1
  83.1 1.0 %copy-start.2 = (bf16[256,256]{1,0:T(8,128)(2,1)S(1)}, bf16[256,256]{1,0:T(8,128)(2,1)}, u32[]{:S(2)}) copy-start(bf16[256,256]{1,0:T(8,128)(2,1)} %cotangent_ref.1) | copy-start | bytes 393220

commit v11 on v9

--- a/solution.py
+++ b/solution.py
@@ -45,32 +45,16 @@
         out_ref[places[slot]] = total[places[slot]].astype(BF16)
 
 
-def split_blocks(core, halves, mine_ref, other_ref):
-    block = halves.shape[3]
-    for position in range(halves.shape[0]):
-        span = slice(position * block, (position + 1) * block)
-        mine_ref[:, span] = halves[position, core]
-        other_ref[:, span] = halves[position, 1 - core]
-
-
-def owned_kernel(
-    core_ref, parts_ref, targets_ref, weights_ref, blocks_ref, tmine_ref, tother_ref, mine_ref, other_ref, halves
-):
-    near, _, columns, block = halves.shape
-    for position in range(2 * near):
-        piece = targets_ref[:, position * block : (position + 1) * block]
-        blocks_ref[position, :columns] = piece
-        halves[position // 2, position % 2] = piece
-    split_blocks(core_ref[0], halves, tmine_ref, tother_ref)
-    for position in range(2 * near):
+def owned_kernel(parts_ref, targets_ref, weights_ref, blocks_ref):
+    group, rows, block = blocks_ref.shape
+    columns = rows // 2
+    for position in range(group):
+        blocks_ref[position, :columns] = targets_ref[:, position * block : (position + 1) * block]
         span = slice(position * columns, (position + 1) * columns)
         total = parts_ref[0, span].astype(F32)
         for source in range(1, parts_ref.shape[0]):
             total += parts_ref[source, span].astype(F32)
-        total = total.astype(BF16)
-        blocks_ref[position, columns:] = total
-        halves[position // 2, position % 2] = total
-    split_blocks(core_ref[0], halves, mine_ref, other_ref)
+        blocks_ref[position, columns:] = total.astype(BF16)
 
 
 def partial_kernel(blocks_ref, weights_ref, out_ref, inputs):
@@ -121,7 +105,12 @@
     return hidden, sigmoid * (1.0 + pre_one * (1.0 - sigmoid))
 
 
-def mine_kernel(pre_ref, pick_ref, gathered_ref, slope_ref):
+def mine_kernel(core_ref, pre_ref, pick_ref, blocks_ref, gathered_ref, slope_ref, inputs_ref):
+    group, _, block = blocks_ref.shape
+    for position in range(group):
+        side = core_ref[0] if 2 * position < group else 1 - core_ref[0]
+        pair = position % (group // 2)
+        inputs_ref[:, position * block : (position + 1) * block] = blocks_ref[2 * pair + side]
     half = slope_ref.shape[0]
     hidden, slope = activate(pre_ref, slope_ref.shape)
     gathered_ref[...] = contract(pick_ref[:, :half], hidden, 1, 0)
@@ -138,17 +127,14 @@
     self_ref,
     neigh_ref,
     cotangent_ref,
-    targets_ref,
-    targets_other_ref,
-    mine_ref,
-    other_ref,
+    inputs_ref,
     output_ref,
     grads_ref,
     gathered,
     scratch,
 ):
     seeds = cotangent_ref.shape[0]
-    columns = targets_ref.shape[0]
+    columns = inputs_ref.shape[0] // 2
     half = slope_ref.shape[0]
     hidden, slope_other = activate(pre_ref, slope_ref.shape)
     gathered[...] = contract(pick_ref[:, half:], hidden, 1, 0)
@@ -178,14 +164,7 @@
         ],
         axis=0,
     )
-    inputs = jnp.concatenate(
-        [
-            jnp.concatenate([targets_ref[...], targets_other_ref[...]], axis=1),
-            jnp.concatenate([mine_ref[...], other_ref[...]], axis=1),
-        ],
-        axis=0,
-    )
-    grad_one = contract(inputs, slope_one, 1, 0).astype(BF16)
+    grad_one = contract(inputs_ref[...], slope_one, 1, 0).astype(BF16)
     part_rows = (grads_ref.shape[1] - 2 * columns) // 2
     first = pl.multiple_of(feat_ref[0] * part_rows, part_rows)
     grad_two = jnp.concatenate(
@@ -254,7 +233,6 @@
     span = half // near
     core = lax.axis_index("c").reshape(1)
     feat = lax.axis_index(FEAT).reshape(1)
-    halves = pltpu.VMEM((near, 2, columns, block), BF16)
     swap = [(0, 1), (1, 0)]
 
     with jax.named_scope("aggregate_tiles"):
@@ -278,15 +256,14 @@
         weights = jnp.concatenate([self_weight1, neigh_weight1], axis=1)
         weights = lax.all_gather(weights, NEAR, tiled=True)
     with jax.named_scope("owned_sum"):
-        blocks, targets_mine, targets_other, agg_mine, agg_other = run(
+        owned = run(
             owned_kernel,
-            [((2 * near, 2 * columns, block), BF16)] + [((columns, half), BF16)] * 4,
-            (core, parts, target_feats.T, weights),
-            [halves],
-            specs=[SMEM, VMEM, VMEM, ANY],
+            [((2 * near, 2 * columns, block), BF16)],
+            (parts, target_feats.T, weights),
+            specs=[VMEM, VMEM, ANY],
         )
     with jax.named_scope("near_exchange"):
-        blocks = lax.all_to_all(blocks, NEAR, 0, 0, tiled=True)
+        blocks = lax.all_to_all(owned, NEAR, 0, 0, tiled=True)
     with jax.named_scope("partial_pre"):
         quarter = run(
             partial_kernel,
@@ -314,10 +291,10 @@
         pre_mine = lax.all_to_all(copies, "zl", 0, 0, tiled=True)
         pre_other = lax.ppermute(pre_mine, "c", swap)
     with jax.named_scope("step_mine"):
-        gathered, slope = run(
+        gathered, slope, inputs = run(
             mine_kernel,
-            [((2 * seeds, hsize), F32), ((half, hsize), F32)],
-            (pre_mine, pick),
+            [((2 * seeds, hsize), F32), ((half, hsize), F32), ((2 * columns, tgt_rows), BF16)],
+            (core, pre_mine, pick, owned),
             limit=12,
             flops=4 * seeds * half * hsize,
         )
@@ -335,10 +312,7 @@
                 self_weight2,
                 neigh_weight2,
                 cotangent,
-                targets_mine,
-                targets_other,
-                agg_mine,
-                agg_other,
+                inputs,
             ),
             [
                 pltpu.VMEM((2 * seeds, hsize), F32),

time: 101 us -> 102 us (level)
  transfers between devices with their start and end apart: 3 -> 3, of which waited for: 2 -> 1; matrix products, arithmetic and copies ran while one was open for 0% -> 0% of each run, Pallas kernels for 2% -> 3%
where the time goes in v11:
time: 102 us; the launch traced here: 101 us
  blocking collectives  63.4 us (62%)
  starting transfers between devices  23 us (23%)
  Pallas kernels  9.05 us (9%)
  waiting for transfers between devices  3.7 us (4%)
  between operations  1.43 us (1%)
    all_gather x1, blocking collectives, per_device(): parts = lax.all_gather(quarter, 'zh')  22.1 us
    all_gather x1, blocking collectives, per_device(): weights = lax.all_gather(weights, NEAR, tiled=True)  17.1 us
    all_to_all x1, blocking collectives, per_device(): grads = lax.all_to_all(grads, NODE, 0, 0, tiled=True)  15.8 us
    pallas_call x8, Pallas kernels, run(): pl.pallas_call(kernel, out_shape=shapes, in_specs=specs, out_specs=[VMEM]...  9.05 us
    all_to_all x1, blocking collectives, per_device(): pre_mine = lax.all_to_all(copies, 'zl', 0, 0, tiled=True)  8.38 us
    ppermute x1, starting transfers between devices, per_device(): pre_other = lax.ppermute(pre_mine, 'c', swap)  7.8 us
    all_to_all x1, starting transfers between devices, per_device(): lax.all_to_all(aggregate.reshape(owners, tgt_rows // block * columns, blo...  7.72 us
    all_to_all x1, starting transfers between devices, per_device(): blocks = lax.all_to_all(owned, NEAR, 0, 0, tiled=True)  7.5 us
  transfers between devices with their start and end apart: 3, of which 1 were waited for; matrix products, arithmetic and copies ran while one was open for 0% of the time, Pallas kernels for 3%

profile of v11, /device:TPU:1, one launch (start us, length us, event | category | flops | bytes accessed | tf_op | source)
XLA Modules:
  0.0 101.3 jit_solution(2202349060212238377)
XLA Ops:
  1.3 3.0 %aggregate_tiles.1 = bf16[128,32,128]{2,1,0:T(8,128)(2,1)} custom-call(s32[1,1]{1,0:T(1,128)} %bitcast.10.count_ref, s32[2,32]{1,0:T(2,128)} %bitcast.17, bf16[32,128,128]{2,1,0:T(8,128)(2,1)} %tiles_ref.1, bf16[32,1024]{1,0:T(8,128)(2,1)} %bitcast.16), custom_call_target="tpu_custom_call" | custom-call | bytes 2162948 | tf_op jit(solution)/shard_map/aggregate_tiles/pallas_call | solution.py:197
  4.2 0.0 copy-start.6
  4.2 0.0 copy-start.7
  4.2 7.7 %all-to-all-start = ((bf16[16,256,128]{2,1,0:T(8,128)(2,1)}), bf16[16,256,128]{2,1,0:T(8,128)(2,1)S(1)}, u32[]{:S(2)}, u32[]{:S(2)}) async-start(bf16[16,256,128]{2,1,0:T(8,128)(2,1)} %bitcast.15), calls=%async_computation | async-start | bytes 2097152 | tf_op jit(solution)/shard_map/aggregate_exchange/all_to_all | solution.py:252
  12.0 0.0 copy-done.6
  12.0 0.0 copy-done.7
  12.0 0.0 copy-start.3
  12.0 17.1 %all_gather.9.weights_ref = bf16[256,512]{1,0:T(8,128)(2,1)S(1)} all-gather(bf16[32,512]{1,0:T(8,128)(2,1)S(1)} %pad_maximum_fusion), channel_id=1, replica_groups=mesh['zh'=4,'zl'=4,'c'=2,'x'=4,'y'=4] {'zl','c'}, dimensions={0}, use_global_device_ids=true | all-gather | bytes 294912 | tf_op jit(solution)/shard_map/weights_gather/all_gather | solution.py:257
  29.1 0.0 all-to-all-done.parts_ref
  29.1 0.0 copy-done.3
  29.1 0.8 owned_sum.1.blocks_ref
  29.9 0.0 copy-start.4
  29.9 7.5 %all-to-all-start.1 = ((bf16[8,64,128]{2,1,0:T(8,128)(2,1)}), bf16[8,64,128]{2,1,0:T(8,128)(2,1)S(1)}, u32[]{:S(2)}, u32[]{:S(2)}) async-start(bf16[8,64,128]{2,1,0:T(8,128)(2,1)} %owned_sum.1.blocks_ref), calls=%async_computation.1 | async-start | bytes 262144 | tf_op jit(solution)/shard_map/near_exchange/all_to_all | solution.py:266
  37.5 0.0 copy-start.5
  37.5 0.0 copy-done.4
  37.5 0.7 copy-done.5
  38.1 1.4 %picks.1 = (bf16[1024,512]{1,0:T(8,128)(2,1)S(1)}, bf16[512,1024]{1,0:T(8,128)(2,1)S(1)}) custom-call(s32[1]{0:T(128)} %bitcast.7.core_ref, s32[10,256]{1,0:T(8,128)S(1)} %bitcast.13, s32[1,256]{1,0:T(1,128)S(1)} %bitcast.14), custom_call_target="tpu_custom_call" | custom-call | flops 5242880 | bytes 2108420 | tf_op jit(solution)/shard_map/picks/pallas_call | solution.py:197
  39.6 3.7 %all-to-all-done.1.blocks_ref = bf16[8,64,128]{2,1,0:T(8,128)(2,1)S(1)} async-done(((bf16[8,64,128]{2,1,0:T(8,128)(2,1)}), bf16[8,64,128]{2,1,0:T(8,128)(2,1)S(1)}, u32[]{:S(2)}, u32[]{:S(2)}) %all-to-all-start.1) | async-done | bytes 131104 | tf_op jit(solution)/shard_map/near_exchange/all_to_all | solution.py:266
  43.3 0.2 partial_pre.1
  43.5 22.1 %all-gather = bf16[512,256]{1,0:T(8,128)(2,1)S(1)} all-gather(bf16[128,256]{1,0:T(8,128)(2,1)S(1)} %partial_pre.1), channel_id=2, replica_groups=mesh['zh'=4,'zl'=4,'c'=2,'x'=4,'y'=4] {'zh'}, dimensions={0}, use_global_device_ids=true | all-gather | bytes 327680 | tf_op jit(solution)/shard_map/pre_sum_far/all_gather | solution.py:283
  65.7 8.4 %all_to_all.20.pre_ref = bf16[4,128,256]{2,1,0:T(8,128)(2,1)S(1)} all-to-all(bf16[4,128,256]{2,1,0:T(8,128)(2,1)S(1)} %pre_sum_far.1), channel_id=1, replica_groups=mesh['zh'=4,'zl'=4,'c'=2,'x'=4,'y'=4] {'zl'}, dimensions={0} | all-to-all | bytes 524288 | tf_op jit(solution)/shard_map/pre_gather/all_to_all | solution.py:291
  74.0 7.8 %collective-permute-start = (bf16[4,128,256]{2,1,0:T(8,128)(2,1)S(1)}, bf16[4,128,256]{2,1,0:T(8,128)(2,1)S(1)}, u32[]{:S(2)}, u32[]{:S(2)}) collective-permute-start(bf16[4,128,256]{2,1,0:T(8,128)(2,1)S(1)} %all_to_all.20.pre_ref), channel_id=1, source_target_pairs={{0,16},{16,0},{1,17},{17,1},{2,18},{18,2},{3,19},{19,3},{4,20},{20... | collective-permute-start | bytes 786440 | tf_op jit(solution)/shard_map/pre_gather/ppermute | solution.py:292
  81.9 0.0 copy-start
  81.9 0.0 copy-start.1
  81.9 0.0 copy-start.2
  81.9 1.4 %step_mine.1 = (f32[512,256]{1,0:T(8,128)S(1)}, f32[512,256]{1,0:T(8,128)S(1)}, bf16[64,1024]{1,0:T(8,128)(2,1)S(1)}) custom-call(s32[1]{0:T(128)} %bitcast.7.core_ref, bf16[4,128,256]{2,1,0:T(8,128)(2,1)S(1)} %all_to_all.20.pre_ref, bf16[512,1024]{1,0:T(8,128)(2,1)S(1)} %get-tuple-element.13.picks_ref.pick_ref, bf16[8,64,128]{2,1,0:T(8,128)(2,1)} %owned_sum.1.blocks_ref), custom_call_target="tpu_custom_call" | custom-call | flops 134217728 | bytes 2621444 | tf_op jit(solution)/shard_map/step_mine/pallas_call | solution.py:197
  83.3 0.0 collective-permute-done.pre_ref
  83.3 0.0 copy-done
  83.3 0.0 copy-done.1
  83.3 0.0 copy-done.2
  83.4 1.5 %step.1 = (bf16[256,256]{1,0:T(8,128)(2,1)S(1)}, bf16[16,80,256]{2,1,0:T(8,128)(2,1)S(1)}) custom-call(s32[1]{0:T(128)} %bitcast.feat_ref, bf16[4,128,256]{2,1,0:T(8,128)(2,1)S(1)} %collective-permute-done.pre_ref, f32[512,256]{1,0:T(8,128)S(1)} %get-tuple-element.14.gathered_ref, f32[512,256]{1,0:T(8,128)S(1)} %get-tuple-element.15.slope_ref, ...), custom_call_target="tpu_custom_call" | custom-call | bytes 4718596 | tf_op jit(solution)/shard_map/step/pallas_call | solution.py:197
  84.8 15.8 %all_to_all.21.parts_ref = bf16[16,80,256]{2,1,0:T(8,128)(2,1)S(1)} all-to-all(bf16[16,80,256]{2,1,0:T(8,128)(2,1)S(1)} %get-tuple-element.18), channel_id=1, replica_groups=mesh['zh'=4,'zl'=4,'c'=2,'x'=4,'y'=4] {'x','y'}, dimensions={0} | all-to-all | bytes 1310720 | tf_op jit(solution)/shard_map/grad_sum/all_to_all | solution.py:324
  100.6 0.7 grad_sum.1
  (2 shorter events, 0.0 us)
Async XLA Ops:
  4.2 7.7 %copy-start.6 = (bf16[32,256]{1,0:T(8,128)(2,1)S(1)}, bf16[32,256]{1,0:T(8,128)(2,1)}, u32[]{:S(2)}) copy-start(bf16[32,256]{1,0:T(8,128)(2,1)} %param.18) | copy-start | bytes 49156
  4.2 7.7 %copy-start.7 = (bf16[32,256]{1,0:T(8,128)(2,1)S(1)}, bf16[32,256]{1,0:T(8,128)(2,1)}, u32[]{:S(2)}) copy-start(bf16[32,256]{1,0:T(8,128)(2,1)} %param.17) | copy-start | bytes 49156
  4.2 24.9 %all-to-all-start = ((bf16[16,256,128]{2,1,0:T(8,128)(2,1)}), bf16[16,256,128]{2,1,0:T(8,128)(2,1)S(1)}, u32[]{:S(2)}, u32[]{:S(2)}) async-start(bf16[16,256,128]{2,1,0:T(8,128)(2,1)} %bitcast.15), calls=%async_computation | async-start | bytes 2097152 | tf_op jit(solution)/shard_map/aggregate_exchange/all_to_all | solution.py:252
  12.0 17.1 %copy-start.3 = (bf16[1024,32]{0,1:T(8,128)(2,1)S(1)}, bf16[1024,32]{0,1:T(8,128)(2,1)}, u32[]{:S(2)}) copy-start(bf16[1024,32]{0,1:T(8,128)(2,1)} %param.13) | copy-start | bytes 196612
  29.9 7.5 %copy-start.4 = (s32[256,10]{0,1:T(8,128)S(1)}, s32[256,10]{0,1:T(8,128)}, u32[]{:S(2)}) copy-start(s32[256,10]{0,1:T(8,128)} %param.21) | copy-start | bytes 30724
  29.9 13.3 %all-to-all-start.1 = ((bf16[8,64,128]{2,1,0:T(8,128)(2,1)}), bf16[8,64,128]{2,1,0:T(8,128)(2,1)S(1)}, u32[]{:S(2)}, u32[]{:S(2)}) async-start(bf16[8,64,128]{2,1,0:T(8,128)(2,1)} %owned_sum.1.blocks_ref), calls=%async_computation.1 | async-start | bytes 262144 | tf_op jit(solution)/shard_map/near_exchange/all_to_all | solution.py:266
  37.5 0.7 copy-start.5
  74.0 9.3 %collective-permute-start = (bf16[4,128,256]{2,1,0:T(8,128)(2,1)S(1)}, bf16[4,128,256]{2,1,0:T(8,128)(2,1)S(1)}, u32[]{:S(2)}, u32[]{:S(2)}) collective-permute-start(bf16[4,128,256]{2,1,0:T(8,128)(2,1)S(1)} %all_to_all.20.pre_ref), channel_id=1, source_target_pairs={{0,16},{16,0},{1,17},{17,1},{2,18},{18,2},{3,19},{19,3},{4,20},{20... | collective-permute-start | bytes 786440 | tf_op jit(solution)/shard_map/pre_gather/ppermute | solution.py:292
  81.9 1.5 %copy-start = (bf16[256,256]{1,0:T(8,128)(2,1)S(1)}, bf16[256,256]{1,0:T(8,128)(2,1)}, u32[]{:S(2)}) copy-start(bf16[256,256]{1,0:T(8,128)(2,1)} %self_ref.1) | copy-start | bytes 393220
  81.9 1.5 %copy-start.1 = (bf16[256,256]{1,0:T(8,128)(2,1)S(1)}, bf16[256,256]{1,0:T(8,128)(2,1)}, u32[]{:S(2)}) copy-start(bf16[256,256]{1,0:T(8,128)(2,1)} %neigh_ref.1) | copy-start | bytes 393220
  81.9 1.5 %copy-start.2 = (bf16[256,256]{1,0:T(8,128)(2,1)S(1)}, bf16[256,256]{1,0:T(8,128)(2,1)}, u32[]{:S(2)}) copy-start(bf16[256,256]{1,0:T(8,128)(2,1)} %cotangent_ref.1) | copy-start | bytes 393220
